TPU v7x, 32 devices: a whole 2x2x4 slice. The times are simulated.
32 devices in a mesh: group: 2 (over y), index: 8 (over z, x), query: 2 (over core).
Axes of the slice: x: 2, y: 2, z: 4, core: 2. Of those that a mesh axis runs over, the one named last changes fastest.
Arguments:
- queries: bfloat16 [128, 32, 128], P(('group', 'index', 'query')), parts along dimension 0, may hold values from -6 to 6
- cand_owner: int32 [128, 8], P(('group', 'index', 'query')), parts along dimension 0, may hold values from 0 to 7, as said below
- cand_local: int32 [128, 8], P(('group', 'index', 'query')), parts along dimension 0, may hold values from 0 to 127
- centroids: bfloat16 [2048, 128], P('index'), may hold values from -0.5 to 0.5
- passage_codes: int32 [1024, 64], P('index'), may hold values from 0 to 2047, as said below
- residuals: bfloat16 [1024, 64, 128], P('index'), may hold values from -0.25 to 0.25
- passage_lengths: int32 [1024], P('index'), may hold values from 16 to 64, as said below
Outputs:
- exact_scores: float32 [128, 8], P(('group', 'index', 'query')), parts along dimension 0
- centroid_scores: float32 [128, 8], P(('group', 'index', 'query')), parts along dimension 0
There are 2 independent parts, one for each index of `group`. A program takes and returns all parts, laid end to end along the dimension named above; an argument that names none is the same for every part. Nothing has to cross between parts.
Inputs may be any that keep to these rules, and one draw needn't show every extreme that they name: `cand_owner`: in each aligned block of 4 rows (the queries of one device) no index device is named more than 8 times, and in every block some index device is named exactly 8 times. `passage_codes`: in each aligned block of 128 rows (the passages of one index device), no range of 256 centroid numbers starting at a multiple of 256 is named by more than 1536 tokens, and in every block one such range is named by exactly 1536 tokens. `passage_lengths`: some passage of every index device has 64 tokens.
All inputs are finite; a program needn't handle non-finite values.
Results may differ from a plain program's by a relative error of at most 0.00037.
Values may be sent and summed in bfloat16 or wider, within the bound.
No kernel may reach another device: no remote copies, remote signals or barrier semaphores. Data moves between devices by JAX's collectives and lax.ppermute only.
A program may use at most 128 MiB of HBM per device.

v0:
```python
import jax
import jax.numpy as jnp
from jax import lax
from jax.sharding import PartitionSpec as P


def normalize_rows(values):
    wide = values.astype(jnp.float32)
    return (wide * lax.rsqrt(jnp.sum(wide * wide, axis=-1, keepdims=True) + 1e-06)).astype(
        jnp.bfloat16
    )


def max_sim(query_rows, doc_rows, lengths):
    sims = jnp.einsum("nid,njd->nij", query_rows, doc_rows, preferred_element_type=jnp.float32)
    live = jnp.arange(doc_rows.shape[1], dtype=jnp.int32)[None, None, :] < lengths[:, None, None]
    return jnp.sum(jnp.max(jnp.where(live, sims, -1000000000.0), axis=2), axis=1)


def bucket_slots(targets, proprietors):
    onehot = (targets[:, None] == jnp.arange(proprietors, dtype=jnp.int32)[None, :]).astype(
        jnp.int32
    )
    return jnp.sum((jnp.cumsum(onehot, axis=0) - 1) * onehot, axis=1)


def body(queries, cand_owner, cand_local, centroids, passage_codes, residuals, passage_lengths):
    proprietors = lax.axis_size("index")
    table = lax.all_gather(centroids, "index", axis=0, tiled=True)
    q_dev, per_query = cand_owner.shape
    count = q_dev * per_query
    slots = max(2, (2 * count + proprietors - 1) // proprietors)
    seq_len = residuals.shape[1]
    qtok = queries.shape[1]
    qnorm = normalize_rows(queries)
    flat_owner = cand_owner.reshape(count)
    flat_local = cand_local.reshape(count)
    position = bucket_slots(flat_owner, proprietors)
    requests = jnp.zeros((proprietors, slots), jnp.int32).at[flat_owner, position].set(flat_local)
    query_rows = jnp.repeat(qnorm, per_query, axis=0)
    slot_numbers = lax.all_to_all(requests, "index", split_axis=0, concat_axis=0, tiled=True)
    codes = passage_codes[slot_numbers]
    lengths = passage_lengths[slot_numbers]
    cent_rows = table[codes]
    decoded = normalize_rows(
        cent_rows.astype(jnp.float32) + residuals[slot_numbers].astype(jnp.float32)
    )
    codes, lengths, cent_rows, decoded = (codes, lengths, cent_rows, decoded)
    decoded, second, lengths = (
        lax.all_to_all(decoded, "index", split_axis=0, concat_axis=0, tiled=True),
        lax.all_to_all(codes, "index", split_axis=0, concat_axis=0, tiled=True),
        lax.all_to_all(lengths, "index", split_axis=0, concat_axis=0, tiled=True),
    )
    mine_decoded = decoded[flat_owner, position]
    mine_second = second[flat_owner, position]
    mine_lengths = lengths[flat_owner, position]
    exact = max_sim(query_rows, mine_decoded, mine_lengths)

    def per_query_terms(operands):
        tokens, query_codes, query_lengths = operands
        scores = jnp.einsum("id,cd->ic", tokens, table, preferred_element_type=jnp.float32)
        picked = jnp.take(scores, query_codes.reshape(-1), axis=1).reshape(qtok, per_query, seq_len)
        live = jnp.arange(seq_len, dtype=jnp.int32)[None, None, :] < query_lengths[None, :, None]
        return jnp.sum(jnp.max(jnp.where(live, picked, -1000000000.0), axis=2), axis=0)

    approx = lax.map(
        per_query_terms,
        (
            qnorm,
            mine_second.reshape(q_dev, per_query, seq_len),
            mine_lengths.reshape(q_dev, per_query),
        ),
    )
    approx = approx.reshape(count)
    return (exact.reshape(q_dev, per_query), approx.reshape(q_dev, per_query))


def solution(mesh):
    in_specs = (
        P(("group", "index", "query"), None, None),
        P(("group", "index", "query"), None),
        P(("group", "index", "query"), None),
        P("index", None),
        P("index", None),
        P("index", None, None),
        P("index"),
    )
    out_specs = (P(("group", "index", "query"), None), P(("group", "index", "query"), None))
    return jax.shard_map(body, mesh=mesh, in_specs=in_specs, out_specs=out_specs, check_vma=False)
```

profile of v0, /device:TPU:0, one launch (start us, length us, event | category | flops | bytes accessed | tf_op | source)
XLA Modules:
  0.0 118.5 jit_solution(8500741950728829199)
XLA Ops:
  0.7 0.9 eq.15
  1.6 0.8 reshape.214
  2.3 0.8 reshape.280
  3.2 0.2 select_reduce_fusion.1
  3.4 0.6 broadcast.144
  4.0 5.4 %scatter_fusion = s32[8,8]{1,0:T(8,128)} fusion(s32[8,8]{1,0:T(8,128)} %broadcast.144, s32[32]{0:T(128)S(1)} %get-tuple-element.49, s32[32]{0:T(128)S(1)} %reshape.280), kind=kCustom, calls=%fused_computation.8 | custom fusion | bytes 640 | tf_op jit(solution)/shard_map/scatter | solution.py:39
  9.4 7.3 %all-to-all-start = ((s32[8,1,8]{2,1,0:T(1,128)}), s32[8,1,8]{2,1,0:T(1,128)S(1)}, u32[]{:S(2)}, u32[]{:S(2)}) async-start(s32[8,1,8]{2,1,0:T(1,128)} %bitcast.10), calls=%async_computation | async-start | bytes 8192 | tf_op jit(solution)/shard_map/all_to_all | solution.py:41
  16.6 0.8 fusion.6
  17.5 32.1 %all_gather.3 = bf16[2048,128]{1,0:T(8,128)(2,1)S(1)} all-gather(bf16[256,128]{1,0:T(8,128)(2,1)} %param.12), channel_id=1, replica_groups=mesh['group'=2,'index'=8,'query'=2] {'index'}, dimensions={0}, use_global_device_ids=true | all-gather | bytes 589824 | tf_op jit(solution)/shard_map/all_gather | solution.py:29
  49.7 0.8 fusion.7
  50.5 0.8 copy.20
  51.5 0.8 gather_fusion.1
  52.3 0.7 all_to_all.25
  52.9 5.4 %all-to-all-start.1 = ((s32[8,1,8]{2,1,0:T(1,128)}), s32[8,1,8]{2,1,0:T(1,128)S(1)}, u32[]{:S(2)}, u32[]{:S(2)}) async-start(s32[8,1,8]{2,1,0:T(1,128)} %bitcast.12), calls=%async_computation.1 | async-start | bytes 8192 | tf_op jit(solution)/shard_map/all_to_all | solution.py:52
  58.3 0.6 gather_fusion.3
  59.0 1.7 %gather_fusion.5 = bf16[64,64,128]{2,1,0:T(8,128)(2,1)} fusion(bf16[128,64,128]{2,1,0:T(8,128)(2,1)S(1)} %copy-done, s32[1024]{0:T(1024)S(1)} %pad_clamp_fusion.1), kind=kCustom, calls=%fused_computation.5 | custom fusion | bytes 2097408 | tf_op jit(solution)/shard_map/gather | solution.py:46
  60.7 14.9 %gather_fusion.4 = bf16[4096,128]{1,0:T(8,128)(2,1)} fusion(bf16[2048,128]{1,0:T(8,128)(2,1)S(1)} %all_gather.3, s32[4096]{0:T(1024)S(1)} %broadcast_clamp_fusion), kind=kCustom, calls=%fused_computation.4 | custom fusion | bytes 2113536 | tf_op jit(solution)/shard_map/gather | solution.py:44
  75.6 2.3 %multiply_reduce_fusion = f32[8,8,64]{2,1,0:T(8,128)S(1)} fusion(bf16[8,8,64,128]{3,2,1,0:T(8,128)(2,1)} %bitcast.68, bf16[8,8,64,128]{3,2,1,0:T(8,128)(2,1)} %bitcast.67), kind=kLoop, calls=%fused_computation.24 | loop fusion | flops 2617344 | bytes 2113536 | tf_op jit(solution)/shard_map/reduce_sum | solution.py:9
  77.9 1.5 %multiply_convert_fusion = bf16[8,8,64,128]{3,2,1,0:T(8,128)(2,1)} fusion(f32[8,8,64]{2,1,0:T(8,128)S(1)} %add_rsqrt_fusion, bf16[64,64,128]{2,1,0:T(8,128)(2,1)S(1)} %copy-done.3, bf16[4096,128]{1,0:T(8,128)(2,1)S(1)} %copy-done.2), kind=kLoop, calls=%fused_computation.23 | loop fusion | flops 2621440 | bytes 3162112 | tf_op jit(solution)/shard_map/convert_element_type | solution.py:9
  79.4 0.7 reshape.292
  80.1 6.0 %all-to-all-start.3 = ((s32[8,1,512]{2,1,0:T(1,128)}), s32[8,1,512]{2,1,0:T(1,128)S(1)}, u32[]{:S(2)}, u32[]{:S(2)}) async-start(s32[8,1,512]{2,1,0:T(1,128)} %reshape.292), calls=%async_computation.3 | async-start | bytes 32768 | tf_op jit(solution)/shard_map/all_to_all | solution.py:51
  86.1 0.7 gather_fusion.2
  87.0 5.8 %all-to-all-done.3 = s32[8,1,512]{2,1,0:T(1,128)S(1)} async-done(((s32[8,1,512]{2,1,0:T(1,128)}), s32[8,1,512]{2,1,0:T(1,128)S(1)}, u32[]{:S(2)}, u32[]{:S(2)}) %all-to-all-start.3) | async-done | bytes 16416 | tf_op jit(solution)/shard_map/all_to_all | solution.py:51
  92.8 4.2 %all-to-all-start.2 = ((bf16[8,8,64,128]{3,2,1,0:T(8,128)(2,1)}), bf16[8,8,64,128]{3,2,1,0:T(8,128)(2,1)}, u32[]{:S(2)}, u32[]{:S(2)}) async-start(bf16[8,8,64,128]{3,2,1,0:T(8,128)(2,1)} %multiply_convert_fusion), calls=%async_computation.2 | async-start | bytes 2097152 | tf_op jit(solution)/shard_map/all_to_all | solution.py:50
  97.0 0.5 broadcast.256
  97.6 0.7 reduce
  98.3 0.7 gather_fusion.7
  99.0 16.3 %while.10 = (s32[]{:T(128)}, f32[4,8]{1,0:T(4,128)S(1)}, s32[4,8]{1,0:T(4,128)S(1)}, s32[4,8,64]{2,1,0:T(8,128)S(1)}, bf16[4,32,128]{2,1,0:T(8,128)(2,1)S(1)}, /...) while((s32[]{:T(128)}, f32[4,8]{1,0:T(4,128)S(1)}, s32[4,8]{1,0:T(4,128)S(1)}, ...), condition=%wide.region_10.11_spmd, body=%wide.region_7.10_spmd.sunk | while | flops 16832504 | bytes 1016121 | solution.py:66
  99.2 1.3 %fusion.22 = f32[32,2048]{0,1:T(8,128)} fusion(bf16[2048,128]{1,0:T(8,128)(2,1)S(1)} %get-tuple-element.118, bf16[4,32,128]{2,1,0:T(8,128)(2,1)S(1)} %get-tuple-element.117, s32[]{:T(128)S(6)} %copy.26), kind=kOutput, calls=%fused_computation.12.clone.1 | convolution fusion | flops 16777216 | bytes 794628 | tf_op jit(solution)/shard_map/while/body/eval_jaxpr/id,cd->ic/dot_general | solution.py:61
  100.4 2.3 %gather_fusion = f32[512,32]{1,0:T(8,128)S(1)} fusion(f32[32,2048]{0,1:T(8,128)} %fusion.22, s32[1024]{0:T(1024)S(1)} %pad_clamp_fusion.3), kind=kCustom, calls=%fused_computation.clone.1 | custom fusion | bytes 133120 | tf_op jit(solution)/shard_map/while/body/eval_jaxpr/jit(_take)/gather | solution.py:62
  102.7 0.2 select_reduce_fusion.3
  102.9 0.1 reduce_sum.56
  103.3 1.3 %fusion.22 = f32[32,2048]{0,1:T(8,128)} fusion(bf16[2048,128]{1,0:T(8,128)(2,1)S(1)} %get-tuple-element.118, bf16[4,32,128]{2,1,0:T(8,128)(2,1)S(1)} %get-tuple-element.117, s32[]{:T(128)S(6)} %copy.26), kind=kOutput, calls=%fused_computation.12.clone.1 | convolution fusion | flops 16777216 | bytes 794628 | tf_op jit(solution)/shard_map/while/body/eval_jaxpr/id,cd->ic/dot_general | solution.py:61
  104.5 2.3 %gather_fusion = f32[512,32]{1,0:T(8,128)S(1)} fusion(f32[32,2048]{0,1:T(8,128)} %fusion.22, s32[1024]{0:T(1024)S(1)} %pad_clamp_fusion.3), kind=kCustom, calls=%fused_computation.clone.1 | custom fusion | bytes 133120 | tf_op jit(solution)/shard_map/while/body/eval_jaxpr/jit(_take)/gather | solution.py:62
  106.8 0.2 select_reduce_fusion.3
  107.0 0.1 reduce_sum.56
  107.3 1.3 %fusion.22 = f32[32,2048]{0,1:T(8,128)} fusion(bf16[2048,128]{1,0:T(8,128)(2,1)S(1)} %get-tuple-element.118, bf16[4,32,128]{2,1,0:T(8,128)(2,1)S(1)} %get-tuple-element.117, s32[]{:T(128)S(6)} %copy.26), kind=kOutput, calls=%fused_computation.12.clone.1 | convolution fusion | flops 16777216 | bytes 794628 | tf_op jit(solution)/shard_map/while/body/eval_jaxpr/id,cd->ic/dot_general | solution.py:61
  108.6 2.3 %gather_fusion = f32[512,32]{1,0:T(8,128)S(1)} fusion(f32[32,2048]{0,1:T(8,128)} %fusion.22, s32[1024]{0:T(1024)S(1)} %pad_clamp_fusion.3), kind=kCustom, calls=%fused_computation.clone.1 | custom fusion | bytes 133120 | tf_op jit(solution)/shard_map/while/body/eval_jaxpr/jit(_take)/gather | solution.py:62
  110.9 0.2 select_reduce_fusion.3
  111.1 0.1 reduce_sum.56
  111.4 1.3 %fusion.22 = f32[32,2048]{0,1:T(8,128)} fusion(bf16[2048,128]{1,0:T(8,128)(2,1)S(1)} %get-tuple-element.118, bf16[4,32,128]{2,1,0:T(8,128)(2,1)S(1)} %get-tuple-element.117, s32[]{:T(128)S(6)} %copy.26), kind=kOutput, calls=%fused_computation.12.clone.1 | convolution fusion | flops 16777216 | bytes 794628 | tf_op jit(solution)/shard_map/while/body/eval_jaxpr/id,cd->ic/dot_general | solution.py:61
  112.7 2.3 %gather_fusion = f32[512,32]{1,0:T(8,128)S(1)} fusion(f32[32,2048]{0,1:T(8,128)} %fusion.22, s32[1024]{0:T(1024)S(1)} %pad_clamp_fusion.3), kind=kCustom, calls=%fused_computation.clone.1 | custom fusion | bytes 133120 | tf_op jit(solution)/shard_map/while/body/eval_jaxpr/jit(_take)/gather | solution.py:62
  114.9 0.2 select_reduce_fusion.3
  115.2 0.1 reduce_sum.56
  115.3 1.9 %gather_fusion.6 = bf16[32,64,128]{2,1,0:T(8,128)(2,1)S(1)} fusion(bf16[8,8,64,128]{3,2,1,0:T(8,128)(2,1)} %all-to-all-done.2, s32[32]{0:T(128)S(1)} %bitcast.71), kind=kCustom, calls=%fused_computation.6 | custom fusion | bytes 1048832 | tf_op jit(solution)/shard_map/gather | solution.py:54
  117.3 0.5 fusion.5
  117.8 0.1 reduce_sum.51
  117.9 0.7 reshape.217
  (53 shorter events, 1.5 us)
Async XLA Ops:
  0.6 58.4 %copy-start = (bf16[128,64,128]{2,1,0:T(8,128)(2,1)S(1)}, bf16[128,64,128]{2,1,0:T(8,128)(2,1)}, u32[]{:S(2)}) copy-start(bf16[128,64,128]{2,1,0:T(8,128)(2,1)} %param.14) | copy-start | bytes 6291460
  0.6 50.8 %copy-start.1 = (s32[128]{0:T(128)S(1)}, s32[128]{0:T(128)}, u32[]{:S(2)}) copy-start(s32[128]{0:T(128)} %param.15) | copy-start | bytes 1540
  9.4 42.0 %all-to-all-start = ((s32[8,1,8]{2,1,0:T(1,128)}), s32[8,1,8]{2,1,0:T(1,128)S(1)}, u32[]{:S(2)}, u32[]{:S(2)}) async-start(s32[8,1,8]{2,1,0:T(1,128)} %bitcast.10), calls=%async_computation | async-start | bytes 8192 | tf_op jit(solution)/shard_map/all_to_all | solution.py:41
  52.9 27.2 %all-to-all-start.1 = ((s32[8,1,8]{2,1,0:T(1,128)}), s32[8,1,8]{2,1,0:T(1,128)S(1)}, u32[]{:S(2)}, u32[]{:S(2)}) async-start(s32[8,1,8]{2,1,0:T(1,128)} %bitcast.12), calls=%async_computation.1 | async-start | bytes 8192 | tf_op jit(solution)/shard_map/all_to_all | solution.py:52
  75.6 2.3 %copy-start.2 = (bf16[4096,128]{1,0:T(8,128)(2,1)S(1)}, bf16[4096,128]{1,0:T(8,128)(2,1)}, u32[]{:S(2)}) copy-start(bf16[4096,128]{1,0:T(8,128)(2,1)} %gather_fusion.4) | copy-start | bytes 3145732
  75.6 2.3 %copy-start.3 = (bf16[64,64,128]{2,1,0:T(8,128)(2,1)S(1)}, bf16[64,64,128]{2,1,0:T(8,128)(2,1)}, u32[]{:S(2)}) copy-start(bf16[64,64,128]{2,1,0:T(8,128)(2,1)} %gather_fusion.5) | copy-start | bytes 3145732
  80.1 12.7 %all-to-all-start.3 = ((s32[8,1,512]{2,1,0:T(1,128)}), s32[8,1,512]{2,1,0:T(1,128)S(1)}, u32[]{:S(2)}, u32[]{:S(2)}) async-start(s32[8,1,512]{2,1,0:T(1,128)} %reshape.292), calls=%async_computation.3 | async-start | bytes 32768 | tf_op jit(solution)/shard_map/all_to_all | solution.py:51
  92.8 22.5 %all-to-all-start.2 = ((bf16[8,8,64,128]{3,2,1,0:T(8,128)(2,1)}), bf16[8,8,64,128]{3,2,1,0:T(8,128)(2,1)}, u32[]{:S(2)}, u32[]{:S(2)}) async-start(bf16[8,8,64,128]{3,2,1,0:T(8,128)(2,1)} %multiply_convert_fusion), calls=%async_computation.2 | async-start | bytes 2097152 | tf_op jit(solution)/shard_map/all_to_all | solution.py:50
  115.3 3.2 %copy-start.4 = (f32[4,8]{1,0:T(4,128)}, f32[4,8]{1,0:T(4,128)S(1)}, u32[]{:S(2)}) copy-start(f32[4,8]{1,0:T(4,128)S(1)} %get-tuple-element.33) | copy-start | bytes 388
where the time goes:
time: 119 us
  local copies, waits for them, and re-layouts  42.8 us (36%)
  blocking collectives  32.1 us (27%)
  starting transfers between devices  22.9 us (19%)
  other arithmetic  8.44 us (7%)
  waiting for transfers between devices  5.83 us (5%)
  matrix products  5.5 us (5%)
    all_gather x1, blocking collectives, body(): table = lax.all_gather(centroids, 'index', axis=0, tiled=True)  32.1 us
    gather x1, local copies, waits for them, and re-layouts, body(): cent_rows = table[codes]  14.9 us
    gather x4, local copies, waits for them, and re-layouts, per_query_terms(): jnp.take(scores, query_codes.reshape(-1), axis=1)  9.01 us
    all_to_all x1, starting transfers between devices, body(): lax.all_to_all(requests, 'index', split_axis=0, concat_axis=0, tiled=True)  7.25 us
    all_to_all x1, starting transfers between devices, body(): lax.all_to_all(codes, 'index', split_axis=0, concat_axis=0, tiled=True)  6 us
    all_to_all x1, waiting for transfers between devices, body(): lax.all_to_all(codes, 'index', split_axis=0, concat_axis=0, tiled=True)  5.83 us
    scatter x1, local copies, waits for them, and re-layouts, body(): jnp.zeros((proprietors, slots), jnp.int32).at[flat_owner, position]  5.37 us
    all_to_all x1, starting transfers between devices, body(): lax.all_to_all(lengths, 'index', split_axis=0, concat_axis=0, tiled=True)  5.37 us
  transfers between devices with their start and end apart: 4, of which 1 were waited for; matrix products, arithmetic and copies ran while one was open for 37% of the time, Pallas kernels for 0%

commit v1 on v0

v1 whole, which is shorter than its diff:
```python
import functools

import jax
import jax.numpy as jnp
from jax import lax
from jax.experimental import pallas as pl
from jax.experimental.pallas import tpu as pltpu
from jax.sharding import PartitionSpec as P

EPS = 1e-06
PAD = 16
VMEM_LIMIT = 56 * 1024 * 1024


def normalize(wide):
    return wide * lax.rsqrt(jnp.sum(wide * wide, axis=-1, keepdims=True) + EPS)


def pack_kernel(owner_ref, local_ref, queries_ref, cent_ref, out_ref, count_ref, req_ref):
    peers = out_ref.shape[0]
    q_dev, per_query = owner_ref.shape
    qrows = queries_ref.shape[0] * queries_ref.shape[1]
    dim = queries_ref.shape[2]
    half = cent_ref.shape[0] // lax.axis_size("query")
    core = lax.axis_index("query")

    def clear(i, carry):
        count_ref[i] = 0
        return carry

    lax.fori_loop(0, peers, clear, 0)
    row = lax.broadcasted_iota(jnp.int32, req_ref.shape, 0)
    lane = lax.broadcasted_iota(jnp.int32, req_ref.shape, 1)
    req = jnp.full(req_ref.shape, -1, jnp.int32)
    for q in range(q_dev):
        for k in range(per_query):
            owner = owner_ref[q, k]
            slot = count_ref[owner]
            count_ref[owner] = slot + 1
            here = row == owner
            req = jnp.where(here & (lane == slot), local_ref[q, k], req)
            req = jnp.where(here & (lane == slot + dim // 2), q * per_query + k, req)
    req_ref[...] = req.astype(jnp.float32)
    qnorm = normalize(queries_ref[...].reshape(qrows, dim).astype(jnp.float32)).astype(jnp.bfloat16)
    cent = cent_ref[pl.ds(pl.multiple_of(core * half, 16), half), :]

    def send(d, carry):
        out_ref[d, :qrows, :] = qnorm
        out_ref[d, qrows : qrows + half, :] = cent
        out_ref[d, qrows + half :, :] = jnp.broadcast_to(req_ref[pl.ds(d, 1), :], (PAD, dim)).astype(
            jnp.bfloat16
        )
        return carry

    lax.fori_loop(0, peers, send, 0, unroll=peers <= 16)


def score_kernel(
    slots,
    q_dev,
    per_query,
    qtok,
    req_ref,
    length_ref,
    recv_ref,
    other_ref,
    codes_ref,
    resid_ref,
    out_ref,
    table_ref,
    dec_ref,
    cent_ref,
):
    peers, half, dim = other_ref.shape
    qrows = q_dev * qtok
    seq = codes_ref.shape[0]
    shard = 2 * half
    core = lax.axis_index("query")

    def place(h, carry):
        cols = pl.ds(pl.multiple_of(h * dim, dim), dim)
        table_ref[:half, cols] = recv_ref[h, qrows : qrows + half, :]
        table_ref[half:, cols] = other_ref[h]
        return carry

    lax.fori_loop(0, peers, place, 0, unroll=peers <= 16)
    lane = lax.broadcasted_iota(jnp.int32, (seq, dim), 1)
    token = lax.broadcasted_iota(jnp.int32, (seq, dim), 0)
    row8 = lax.broadcasted_iota(jnp.int32, (2 * q_dev, dim), 0)
    lane8 = lax.broadcasted_iota(jnp.int32, (2 * q_dev, dim), 1)
    lane1 = lax.broadcasted_iota(jnp.int32, (1, dim), 1)

    def block(b, carry):
        hot, high = [], []
        for s in range(slots):
            p = jnp.maximum(req_ref[b, s], 0)
            code = jnp.take_along_axis(codes_ref[...], jnp.full((seq, dim), p, jnp.int32), axis=1)
            low = (code % shard) ^ (core * half)
            high.append(code // shard)
            hot.append(
                jnp.concatenate([low == lane + i * dim for i in range(shard // dim)], axis=1)
                .astype(jnp.float32)
                .astype(jnp.bfloat16)
            )
        hot = jnp.concatenate(hot, axis=0)
        high = jnp.concatenate(high, axis=0)

        def pick(h, cent):
            cols = pl.ds(pl.multiple_of(2 * h * dim, 2 * dim), 2 * dim)
            rows = jnp.dot(hot, table_ref[:, cols], preferred_element_type=jnp.float32)
            cent = jnp.where(high == 2 * h, rows[:, :dim], cent)
            return jnp.where(high == 2 * h + 1, rows[:, dim:], cent)

        cent = lax.fori_loop(
            0, peers // 2, pick, jnp.zeros((slots * seq, dim), jnp.float32), unroll=peers <= 16
        )
        cent_ref[...] = cent.astype(jnp.bfloat16)
        for s in range(slots):
            p = jnp.maximum(req_ref[b, s], 0)
            v = cent[s * seq : (s + 1) * seq] + resid_ref[p].astype(jnp.float32)
            dec_ref[s * seq : (s + 1) * seq, :] = normalize(v).astype(jnp.bfloat16)
        query = recv_ref[b, :qrows, :]
        nt = (((1,), (1,)), ((), ()))
        exact = lax.dot_general(dec_ref[...], query, nt, preferred_element_type=jnp.float32)
        approx = lax.dot_general(cent_ref[...], query, nt, preferred_element_type=jnp.float32)
        total = jnp.zeros((2 * q_dev, dim), jnp.float32)
        for s in range(slots):
            p = jnp.maximum(req_ref[b, s], 0)
            c = req_ref[b, s + dim // 2]
            q, k = c // per_query, c % per_query
            live = token < length_ref[p]
            mine = lane1 // qtok == q
            for off, sims in ((0, exact), (q_dev, approx)):
                best = jnp.max(
                    jnp.where(live, sims[s * seq : (s + 1) * seq], -1000000000.0), axis=0, keepdims=True
                )
                score = jnp.sum(jnp.where(mine, best, 0.0), axis=1, keepdims=True)
                total += jnp.where((row8 == q + off) & (lane8 == k) & (c >= 0), score, 0.0)
        out_ref[b] = total
        return carry

    lax.fori_loop(0, peers, block, 0)


def body(queries, cand_owner, cand_local, centroids, passage_codes, residuals, passage_lengths):
    peers = lax.axis_size("index")
    cores = lax.axis_size("query")
    q_dev, per_query = cand_owner.shape
    count = q_dev * per_query
    slots = max(2, (2 * count + peers - 1) // peers)
    seq, dim = residuals.shape[1:]
    qtok = queries.shape[1]
    qrows = q_dev * qtok
    half = centroids.shape[0] // cores
    rows = qrows + half + PAD
    vmem = pl.BlockSpec(memory_space=pltpu.VMEM)
    smem = pl.BlockSpec(memory_space=pltpu.SMEM)
    params = pltpu.CompilerParams(vmem_limit_bytes=VMEM_LIMIT)
    packed = pl.pallas_call(
        pack_kernel,
        out_shape=jax.ShapeDtypeStruct((peers, rows, dim), jnp.bfloat16),
        in_specs=[smem, smem, vmem, vmem],
        out_specs=vmem,
        scratch_shapes=[pltpu.SMEM((peers,), jnp.int32), pltpu.VMEM((peers, dim), jnp.float32)],
        compiler_params=params,
    )(cand_owner, cand_local, queries, centroids)
    recv = lax.all_to_all(packed, "index", split_axis=0, concat_axis=0, tiled=True)
    other = lax.ppermute(recv[:, qrows : qrows + half, :], "query", [(0, 1), (1, 0)])
    requests = recv[:, qrows + half, :].astype(jnp.int32)
    scores = pl.pallas_call(
        functools.partial(score_kernel, slots, q_dev, per_query, qtok),
        out_shape=jax.ShapeDtypeStruct((peers, 2 * q_dev, dim), jnp.float32),
        in_specs=[smem, smem, vmem, vmem, vmem, vmem],
        out_specs=vmem,
        scratch_shapes=[
            pltpu.VMEM((cores * half, peers * dim), jnp.bfloat16),
            pltpu.VMEM((slots * seq, dim), jnp.bfloat16),
            pltpu.VMEM((slots * seq, dim), jnp.bfloat16),
        ],
        compiler_params=params,
    )(requests, passage_lengths, recv, other, passage_codes.T, residuals)
    back = lax.all_to_all(scores, "index", split_axis=0, concat_axis=0, tiled=True)
    result = jnp.sum(back[:, :, :per_query], axis=0)
    return result[:q_dev], result[q_dev:]


def solution(mesh):
    in_specs = (
        P(("group", "index", "query"), None, None),
        P(("group", "index", "query"), None),
        P(("group", "index", "query"), None),
        P("index", None),
        P("index", None),
        P("index", None, None),
        P("index"),
    )
    out_specs = (P(("group", "index", "query"), None), P(("group", "index", "query"), None))
    return jax.shard_map(body, mesh=mesh, in_specs=in_specs, out_specs=out_specs, check_vma=False)
```

time: 119 us -> 49.7 us (0.42)
  local copies, waits for them, and re-layouts: 42.8 us -> 1.3 us
  starting transfers between devices: 22.9 us -> 0.07 us
  Pallas kernels: 0 us -> 12.6 us
  other arithmetic: 8.44 us -> 0.69 us
  matrix products: 5.5 us -> 0 us
  waiting for transfers between devices: 5.83 us -> 0.84 us
    all_to_all x0 -> x2, blocking collectives: none -> 33.2 us  [the longest x1 23.2 us: body(): lax.all_to_all(packed, 'index', split_axis=0, concat_axis=0, tiled=True)]
    all_gather x1 -> x0, blocking collectives: 32.1 us -> none  [body(): table = lax.all_gather(centroids, 'index', axis=0, tiled=True)]
    gather x11 -> x0, local copies, waits for them, and re-layouts: 30.2 us -> none  [the longest x1 14.9 us: body(): cent_rows = table[codes]]
    all_to_all x4 -> x0, starting transfers between devices: 22.9 us -> none  [the longest x1 7.25 us: body(): lax.all_to_all(requests, 'index', split_axis=0, concat_axis=0, tiled=True)]
    pallas_call x0 -> x2, Pallas kernels: none -> 12.6 us  [the longest x1 10.7 us: body(): pl.pallas_call(functools.partial(score_kernel, slots, q_dev, per_query, q...]
    all_to_all x4 -> x0, waiting for transfers between devices: 5.83 us -> none  [the longest x1 5.83 us: body(): lax.all_to_all(codes, 'index', split_axis=0, concat_axis=0, tiled=True)]
    dot_general x5 -> x0, matrix products: 5.5 us -> none  [the longest x4 5.04 us: per_query_terms(): jnp.einsum('id,cd->ic', tokens, table, preferred_element_type=jnp.float32)]
    scatter x1 -> x0, local copies, waits for them, and re-layouts: 5.37 us -> none  [body(): jnp.zeros((proprietors, slots), jnp.int32).at[flat_owner, position]]
  transfers between devices with their start and end apart: 4 -> 1, of which waited for: 1 -> 1; matrix products, arithmetic and copies ran while one was open for 37% -> 1% of each run, Pallas kernels for 0% -> 0%
where the time goes in v1:
time: 49.7 us; the launch traced here: 49.3 us
  blocking collectives  33.2 us (67%)
  Pallas kernels  12.6 us (25%)
  local copies, waits for them, and re-layouts  1.3 us (3%)
  waiting for transfers between devices  0.84 us (2%)
  other arithmetic  0.69 us (1%)
  between operations  0.65 us (1%)
    all_to_all x1, blocking collectives, body(): lax.all_to_all(packed, 'index', split_axis=0, concat_axis=0, tiled=True)  23.2 us
    pallas_call x1, Pallas kernels, body(): pl.pallas_call(functools.partial(score_kernel, slots, q_dev, per_query, q...  10.7 us
    all_to_all x1, blocking collectives, body(): lax.all_to_all(scores, 'index', split_axis=0, concat_axis=0, tiled=True)  9.92 us
    pallas_call x1, Pallas kernels, body(): pl.pallas_call(pack_kernel, out_shape=jax.ShapeDtypeStruct((peers, rows,...  1.87 us
  transfers between devices with their start and end apart: 1, of which 1 were waited for; matrix products, arithmetic and copies ran while one was open for 1% of the time, Pallas kernels for 0%

profile of v1, /device:TPU:0, one launch (start us, length us, event | category | flops | bytes accessed | tf_op | source)
XLA Modules:
  0.0 49.3 jit_solution(2894679213422082516)
XLA Ops:
  0.6 1.9 %shard_map.86 = bf16[8,272,128]{2,1,0:T(8,128)(2,1)} custom-call(s32[4,8]{1,0:T(4,128)} %owner_ref.1, s32[4,8]{1,0:T(4,128)} %local_ref.1, bf16[4,32,128]{2,1,0:T(8,128)(2,1)} %queries_ref.1, bf16[256,128]{1,0:T(8,128)(2,1)} %cent_ref.1), custom_call_target="tpu_custom_call" | custom-call | tf_op jit(solution)/shard_map/pallas_call | solution.py:159
  2.5 23.2 %all_to_all.10.recv_ref = bf16[8,272,128]{2,1,0:T(8,128)(2,1)S(1)} all-to-all(bf16[8,272,128]{2,1,0:T(8,128)(2,1)} %shard_map.86), channel_id=1, replica_groups=mesh['group'=2,'index'=8,'query'=2] {'index'}, dimensions={0} | all-to-all | bytes 1114112 | tf_op jit(solution)/shard_map/all_to_all | solution.py:167
  25.8 0.0 copy-start
  25.8 0.1 collective-permute-start
  25.9 0.7 %slice_convert_fusion = s32[8,1,128]{2,1,0:T(1,128)} fusion(bf16[8,272,128]{2,1,0:T(8,128)(2,1)S(1)} %all_to_all.10.recv_ref), kind=kLoop, calls=%fused_computation.1 | loop fusion | flops 1024 | bytes 6144 | tf_op jit(solution)/shard_map/convert_element_type | solution.py:169
  26.5 0.8 %collective-permute-done.other_ref = bf16[8,128,128]{2,1,0:T(8,128)(2,1)S(1)} collective-permute-done((bf16[8,128,128]{2,1,0:T(8,128)(2,1)S(1)}, bf16[8,128,128]{2,1,0:T(8,128)(2,1)S(1)}, u32[]{:S(2)}, u32[]{:S(2)}) %collective-permute-start) | collective-permute-done | bytes 262176 | tf_op jit(solution)/shard_map/ppermute | solution.py:168
  27.4 0.0 copy-start.1
  27.4 0.0 copy-done
  27.4 0.7 %copy-done.1 = bf16[8,128,128]{2,1,0:T(8,128)(2,1)} copy-done((bf16[8,128,128]{2,1,0:T(8,128)(2,1)}, bf16[8,128,128]{2,1,0:T(8,128)(2,1)S(1)}, u32[]{:S(2)}) %copy-start.1) | copy-done | bytes 262168
  28.1 10.7 %shard_map.87 = f32[8,8,128]{2,1,0:T(8,128)} custom-call(s32[8,128]{1,0:T(8,128)} %bitcast.3, s32[128]{0:T(128)} %length_ref.1, bf16[8,272,128]{2,1,0:T(8,128)(2,1)} %copy-done, bf16[8,128,128]{2,1,0:T(8,128)(2,1)} %copy-done.1, s32[64,128]{1,0:T(8,128)} %bitcast.2, bf16[128,64,128]{2,1,0:T(8,128)(2,1)} %resid_ref.1), custom_call_target="tpu_custom_call" | custom-call | tf_op jit(solution)/shard_map/pallas_call | solution.py:170
  38.8 9.9 %all_to_all.11 = f32[8,8,128]{2,1,0:T(8,128)S(1)} all-to-all(f32[8,8,128]{2,1,0:T(8,128)} %shard_map.87), channel_id=1, replica_groups=mesh['group'=2,'index'=8,'query'=2] {'index'}, dimensions={0} | all-to-all | bytes 65536 | tf_op jit(solution)/shard_map/all_to_all | solution.py:182
  48.7 0.6 %fusion = (f32[4,8]{1,0:T(4,128)}, f32[4,8]{1,0:T(4,128)}) fusion(f32[8,8]{1,0:T(8,128)S(1)} %slice_reduce_fusion), kind=kLoop, calls=%fused_computation.2 | loop fusion | bytes 512 | tf_op jit(solution)/shard_map/slice | solution.py:184
  (2 shorter events, 0.0 us)
Async XLA Ops:
  25.8 1.6 %copy-start = (bf16[8,272,128]{2,1,0:T(8,128)(2,1)}, bf16[8,272,128]{2,1,0:T(8,128)(2,1)S(1)}, u32[]{:S(2)}) copy-start(bf16[8,272,128]{2,1,0:T(8,128)(2,1)S(1)} %all_to_all.10.recv_ref) | copy-start | bytes 1671172
  25.8 1.6 %collective-permute-start = (bf16[8,128,128]{2,1,0:T(8,128)(2,1)S(1)}, bf16[8,128,128]{2,1,0:T(8,128)(2,1)S(1)}, u32[]{:S(2)}, u32[]{:S(2)}) collective-permute-start(bf16[8,128,128]{2,1,0:T(8,128)(2,1)S(1)} %slice.21), channel_id=1, source_target_pairs={{0,1},{1,0},{2,3},{3,2},{4,5},{5,4},{6,7},{7,6},{8,9},{9,8},{10,11... | collective-permute-start | bytes 786440 | tf_op jit(solution)/shard_map/ppermute | solution.py:168
  27.4 0.7 %copy-start.1 = (bf16[8,128,128]{2,1,0:T(8,128)(2,1)}, bf16[8,128,128]{2,1,0:T(8,128)(2,1)S(1)}, u32[]{:S(2)}) copy-start(bf16[8,128,128]{2,1,0:T(8,128)(2,1)S(1)} %collective-permute-done.other_ref) | copy-start | bytes 786436

commit v2 on v1

--- a/solution.py
+++ b/solution.py
@@ -9,7 +9,7 @@
 
 EPS = 1e-06
 PAD = 16
-VMEM_LIMIT = 56 * 1024 * 1024
+MIB = 1024 * 1024
 
 
 def normalize(wide):
@@ -155,7 +155,8 @@
     rows = qrows + half + PAD
     vmem = pl.BlockSpec(memory_space=pltpu.VMEM)
     smem = pl.BlockSpec(memory_space=pltpu.SMEM)
-    params = pltpu.CompilerParams(vmem_limit_bytes=VMEM_LIMIT)
+    scratch = 2 * peers * rows * dim // MIB
+    params = pltpu.CompilerParams(vmem_limit_bytes=(8 + 2 * scratch) * MIB)
     packed = pl.pallas_call(
         pack_kernel,
         out_shape=jax.ShapeDtypeStruct((peers, rows, dim), jnp.bfloat16),

time: 49.7 us -> 48.3 us (0.972)
  Pallas kernels: 12.6 us -> 9.65 us
  local copies, waits for them, and re-layouts: 1.3 us -> 3.72 us
  blocking collectives: 33.2 us -> 32.4 us
  waiting for transfers between devices: 0.84 us -> 1.51 us
  other arithmetic: 0.69 us -> 0.02 us
    unnamed x4 -> x14, local copies, waits for them, and re-layouts: 0.69 us -> 3.11 us
    pallas_call x1, Pallas kernels: 10.7 us -> 8.86 us  [body(): pl.pallas_call(functools.partial(score_kernel, slots, q_dev, per_query, q...]
    pallas_call x1, Pallas kernels: 1.87 us -> 0.8 us  [body(): pl.pallas_call(pack_kernel, out_shape=jax.ShapeDtypeStruct((peers, rows,...]
    convert_element_type x1, other arithmetic: 0.68 us -> 0.01 us  [body(): requests = recv[:, qrows + half, :].astype(jnp.int32)]
    ppermute x1, waiting for transfers between devices: 0.84 us -> 1.51 us  [body(): lax.ppermute(recv[:, qrows:qrows + half, :], 'query', [(0, 1), (1, 0)])]
    all_to_all x1, blocking collectives: 9.92 us -> 9.3 us  [body(): lax.all_to_all(scores, 'index', split_axis=0, concat_axis=0, tiled=True)]
  transfers between devices with their start and end apart: 1 -> 1, of which waited for: 1 -> 1; matrix products, arithmetic and copies ran while one was open for 1% -> 0% of each run, Pallas kernels for 0% -> 0%
where the time goes in v2:
time: 48.3 us; the launch traced here: 48 us
  blocking collectives  32.4 us (67%)
  Pallas kernels  9.65 us (20%)
  local copies, waits for them, and re-layouts  3.72 us (8%)
  waiting for transfers between devices  1.51 us (3%)
  between operations  0.68 us (1%)
    all_to_all x1, blocking collectives, body(): lax.all_to_all(packed, 'index', split_axis=0, concat_axis=0, tiled=True)  23.1 us
    all_to_all x1, blocking collectives, body(): lax.all_to_all(scores, 'index', split_axis=0, concat_axis=0, tiled=True)  9.3 us
    pallas_call x1, Pallas kernels, body(): pl.pallas_call(functools.partial(score_kernel, slots, q_dev, per_query, q...  8.86 us
    unnamed x14, local copies, waits for them, and re-layouts  3.11 us
    ppermute x1, waiting for transfers between devices, body(): lax.ppermute(recv[:, qrows:qrows + half, :], 'query', [(0, 1), (1, 0)])  1.51 us
  transfers between devices with their start and end apart: 1, of which 1 were waited for; matrix products, arithmetic and copies ran while one was open for 0% of the time, Pallas kernels for 0%

profile of v2, /device:TPU:0, one launch (start us, length us, event | category | flops | bytes accessed | tf_op | source)
XLA Modules:
  0.0 48.0 jit_solution(15048282570872185961)
XLA Ops:
  0.6 0.0 copy-start
  0.6 0.0 copy-start.1
  0.7 1.0 %copy-done.1 = bf16[256,128]{1,0:T(8,128)(2,1)S(1)} copy-done((bf16[256,128]{1,0:T(8,128)(2,1)S(1)}, bf16[256,128]{1,0:T(8,128)(2,1)}, u32[]{:S(2)}) %copy-start.1) | copy-done | bytes 65560
  1.6 0.0 copy-start.3
  1.6 0.8 %copy-done.3 = bf16[4,32,128]{2,1,0:T(8,128)(2,1)S(1)} copy-done((bf16[4,32,128]{2,1,0:T(8,128)(2,1)S(1)}, bf16[4,32,128]{2,1,0:T(8,128)(2,1)}, u32[]{:S(2)}) %copy-start.3) | copy-done | bytes 32792
  2.4 0.0 copy-start.4
  2.4 0.7 %copy-done.4 = s32[4,8]{1,0:T(4,128)S(1)} copy-done((s32[4,8]{1,0:T(4,128)S(1)}, s32[4,8]{1,0:T(4,128)}, u32[]{:S(2)}) %copy-start.4) | copy-done | bytes 152
  3.1 0.0 copy-start.5
  3.1 0.7 %copy-done.5 = s32[4,8]{1,0:T(4,128)S(1)} copy-done((s32[4,8]{1,0:T(4,128)S(1)}, s32[4,8]{1,0:T(4,128)}, u32[]{:S(2)}) %copy-start.5) | copy-done | bytes 152
  3.8 0.0 copy-start.2
  3.8 0.0 copy-start.6
  3.8 0.8 %shard_map.86 = bf16[8,272,128]{2,1,0:T(8,128)(2,1)S(1)} custom-call(s32[4,8]{1,0:T(4,128)S(1)} %copy-done.4, s32[4,8]{1,0:T(4,128)S(1)} %copy-done.5, bf16[4,32,128]{2,1,0:T(8,128)(2,1)S(1)} %copy-done.3, bf16[256,128]{1,0:T(8,128)(2,1)S(1)} %copy-done.1), custom_call_target="tpu_custom_call" | custom-call | tf_op jit(solution)/shard_map/pallas_call | solution.py:160
  4.6 23.1 %all_to_all.10.recv_ref = bf16[8,272,128]{2,1,0:T(8,128)(2,1)S(1)} all-to-all(bf16[8,272,128]{2,1,0:T(8,128)(2,1)S(1)} %shard_map.86), channel_id=1, replica_groups=mesh['group'=2,'index'=8,'query'=2] {'index'}, dimensions={0} | all-to-all | bytes 1114112 | tf_op jit(solution)/shard_map/all_to_all | solution.py:168
  27.6 0.1 collective-permute-start
  27.7 1.5 %collective-permute-done.other_ref = bf16[8,128,128]{2,1,0:T(8,128)(2,1)S(1)} collective-permute-done((bf16[8,128,128]{2,1,0:T(8,128)(2,1)S(1)}, bf16[8,128,128]{2,1,0:T(8,128)(2,1)S(1)}, u32[]{:S(2)}, u32[]{:S(2)}) %collective-permute-start) | collective-permute-done | bytes 262176 | tf_op jit(solution)/shard_map/ppermute | solution.py:169
  29.2 0.0 copy-done
  29.2 0.0 copy-done.2
  29.2 0.0 copy-done.6
  29.2 8.9 %shard_map.87 = f32[8,8,128]{2,1,0:T(8,128)S(1)} custom-call(s32[8,128]{1,0:T(8,128)S(1)} %bitcast.3, s32[128]{0:T(128)S(1)} %copy-done.6, bf16[8,272,128]{2,1,0:T(8,128)(2,1)S(1)} %all_to_all.10.recv_ref, bf16[8,128,128]{2,1,0:T(8,128)(2,1)S(1)} %collective-permute-done.other_ref, s32[64,128]{1,0:T(8,128)S(1)} %bitcast.2, bf16[128,64,128]{2,1,0:T(8,128)(2,1)S(1)} %copy-done), custom_call_target="tpu_custom_call" | custom-call | tf_op jit(solution)/shard_map/pallas_call | solution.py:171
  38.1 9.3 %all_to_all.11 = f32[8,8,128]{2,1,0:T(8,128)S(1)} all-to-all(f32[8,8,128]{2,1,0:T(8,128)S(1)} %shard_map.87), channel_id=1, replica_groups=mesh['group'=2,'index'=8,'query'=2] {'index'}, dimensions={0} | all-to-all | bytes 65536 | tf_op jit(solution)/shard_map/all_to_all | solution.py:183
  47.4 0.6 %fusion = (f32[4,8]{1,0:T(4,128)}, f32[4,8]{1,0:T(4,128)}) fusion(f32[8,8]{1,0:T(8,128)S(1)} %slice_reduce_fusion), kind=kLoop, calls=%fused_computation.2 | loop fusion | bytes 512 | tf_op jit(solution)/shard_map/slice | solution.py:185
  (3 shorter events, 0.0 us)
Async XLA Ops:
  0.6 28.6 %copy-start = (bf16[128,64,128]{2,1,0:T(8,128)(2,1)S(1)}, bf16[128,64,128]{2,1,0:T(8,128)(2,1)}, u32[]{:S(2)}) copy-start(bf16[128,64,128]{2,1,0:T(8,128)(2,1)} %resid_ref.1) | copy-start | bytes 6291460
  0.6 1.0 %copy-start.1 = (bf16[256,128]{1,0:T(8,128)(2,1)S(1)}, bf16[256,128]{1,0:T(8,128)(2,1)}, u32[]{:S(2)}) copy-start(bf16[256,128]{1,0:T(8,128)(2,1)} %cent_ref.1) | copy-start | bytes 196612
  1.6 0.8 %copy-start.3 = (bf16[4,32,128]{2,1,0:T(8,128)(2,1)S(1)}, bf16[4,32,128]{2,1,0:T(8,128)(2,1)}, u32[]{:S(2)}) copy-start(bf16[4,32,128]{2,1,0:T(8,128)(2,1)} %queries_ref.1) | copy-start | bytes 98308
  2.4 0.7 %copy-start.4 = (s32[4,8]{1,0:T(4,128)S(1)}, s32[4,8]{1,0:T(4,128)}, u32[]{:S(2)}) copy-start(s32[4,8]{1,0:T(4,128)} %owner_ref.1) | copy-start | bytes 388
  3.1 0.7 %copy-start.5 = (s32[4,8]{1,0:T(4,128)S(1)}, s32[4,8]{1,0:T(4,128)}, u32[]{:S(2)}) copy-start(s32[4,8]{1,0:T(4,128)} %local_ref.1) | copy-start | bytes 388
  3.8 25.5 %copy-start.2 = (s32[128,64]{0,1:T(8,128)S(1)}, s32[128,64]{0,1:T(8,128)}, u32[]{:S(2)}) copy-start(s32[128,64]{0,1:T(8,128)} %param.11) | copy-start | bytes 98308
  3.8 25.5 %copy-start.6 = (s32[128]{0:T(128)S(1)}, s32[128]{0:T(128)}, u32[]{:S(2)}) copy-start(s32[128]{0:T(128)} %length_ref.1) | copy-start | bytes 1540
  27.6 1.6 %collective-permute-start = (bf16[8,128,128]{2,1,0:T(8,128)(2,1)S(1)}, bf16[8,128,128]{2,1,0:T(8,128)(2,1)S(1)}, u32[]{:S(2)}, u32[]{:S(2)}) collective-permute-start(bf16[8,128,128]{2,1,0:T(8,128)(2,1)S(1)} %slice.21), channel_id=1, source_target_pairs={{0,1},{1,0},{2,3},{3,2},{4,5},{5,4},{6,7},{7,6},{8,9},{9,8},{10,11... | collective-permute-start | bytes 786440 | tf_op jit(solution)/shard_map/ppermute | solution.py:169

commit v3 on v2

--- a/solution.py
+++ b/solution.py
@@ -16,13 +16,23 @@
     return wide * lax.rsqrt(jnp.sum(wide * wide, axis=-1, keepdims=True) + EPS)
 
 
-def pack_kernel(owner_ref, local_ref, queries_ref, cent_ref, out_ref, count_ref, req_ref):
+def pack_kernel(
+    owner_hbm, local_hbm, queries_hbm, out_ref, count_ref, req_ref, owner_ref, local_ref, queries_ref, sems
+):
+    copies = [
+        pltpu.make_async_copy(src, dst, sems.at[i])
+        for i, (src, dst) in enumerate(
+            ((owner_hbm, owner_ref), (local_hbm, local_ref), (queries_hbm, queries_ref))
+        )
+    ]
+    for copy in copies:
+        copy.start()
+    for copy in copies:
+        copy.wait()
     peers = out_ref.shape[0]
     q_dev, per_query = owner_ref.shape
     qrows = queries_ref.shape[0] * queries_ref.shape[1]
     dim = queries_ref.shape[2]
-    half = cent_ref.shape[0] // lax.axis_size("query")
-    core = lax.axis_index("query")
 
     def clear(i, carry):
         count_ref[i] = 0
@@ -42,12 +52,10 @@
             req = jnp.where(here & (lane == slot + dim // 2), q * per_query + k, req)
     req_ref[...] = req.astype(jnp.float32)
     qnorm = normalize(queries_ref[...].reshape(qrows, dim).astype(jnp.float32)).astype(jnp.bfloat16)
-    cent = cent_ref[pl.ds(pl.multiple_of(core * half, 16), half), :]
 
     def send(d, carry):
         out_ref[d, :qrows, :] = qnorm
-        out_ref[d, qrows : qrows + half, :] = cent
-        out_ref[d, qrows + half :, :] = jnp.broadcast_to(req_ref[pl.ds(d, 1), :], (PAD, dim)).astype(
+        out_ref[d, qrows:, :] = jnp.broadcast_to(req_ref[pl.ds(d, 1), :], (PAD, dim)).astype(
             jnp.bfloat16
         )
         return carry
@@ -63,6 +71,7 @@
     req_ref,
     length_ref,
     recv_ref,
+    mine_ref,
     other_ref,
     codes_ref,
     resid_ref,
@@ -75,11 +84,12 @@
     qrows = q_dev * qtok
     seq = codes_ref.shape[0]
     shard = 2 * half
+    me = lax.axis_index("index")
     core = lax.axis_index("query")
 
     def place(h, carry):
-        cols = pl.ds(pl.multiple_of(h * dim, dim), dim)
-        table_ref[:half, cols] = recv_ref[h, qrows : qrows + half, :]
+        cols = pl.ds(pl.multiple_of((h ^ me) * dim, dim), dim)
+        table_ref[:half, cols] = mine_ref[h]
         table_ref[half:, cols] = other_ref[h]
         return carry
 
@@ -142,6 +152,20 @@
     lax.fori_loop(0, peers, block, 0)
 
 
+def gather_table(centroids):
+    peers, cores = lax.axis_size("index"), lax.axis_size("query")
+    half = centroids.shape[0] // cores
+    core = lax.axis_index("query")
+    swap = lambda x, t: lax.ppermute(x, "index", [(i, i ^ t) for i in range(peers)])
+    both = jnp.stack([centroids, swap(centroids, 1)])
+    have = lax.dynamic_slice_in_dim(both, core * half, half, axis=1)
+    while have.shape[0] < peers:
+        step = have.shape[0]
+        radix = min(4, peers // step)
+        have = jnp.concatenate([have] + [swap(have, m * step) for m in range(1, radix)], axis=0)
+    return have
+
+
 def body(queries, cand_owner, cand_local, centroids, passage_codes, residuals, passage_lengths):
     peers = lax.axis_size("index")
     cores = lax.axis_size("query")
@@ -152,34 +176,43 @@
     qtok = queries.shape[1]
     qrows = q_dev * qtok
     half = centroids.shape[0] // cores
-    rows = qrows + half + PAD
+    rows = qrows + PAD
     vmem = pl.BlockSpec(memory_space=pltpu.VMEM)
     smem = pl.BlockSpec(memory_space=pltpu.SMEM)
-    scratch = 2 * peers * rows * dim // MIB
-    params = pltpu.CompilerParams(vmem_limit_bytes=(8 + 2 * scratch) * MIB)
+    hbm = pl.BlockSpec(memory_space=pltpu.HBM)
+    pack_mib = 2 * peers * rows * dim * 2 // MIB
     packed = pl.pallas_call(
         pack_kernel,
         out_shape=jax.ShapeDtypeStruct((peers, rows, dim), jnp.bfloat16),
-        in_specs=[smem, smem, vmem, vmem],
+        in_specs=[hbm, hbm, hbm],
         out_specs=vmem,
-        scratch_shapes=[pltpu.SMEM((peers,), jnp.int32), pltpu.VMEM((peers, dim), jnp.float32)],
-        compiler_params=params,
-    )(cand_owner, cand_local, queries, centroids)
+        scratch_shapes=[
+            pltpu.SMEM((peers,), jnp.int32),
+            pltpu.VMEM((peers, dim), jnp.float32),
+            pltpu.SMEM(cand_owner.shape, jnp.int32),
+            pltpu.SMEM(cand_local.shape, jnp.int32),
+            pltpu.VMEM(queries.shape, queries.dtype),
+            pltpu.SemaphoreType.DMA((3,)),
+        ],
+        compiler_params=pltpu.CompilerParams(vmem_limit_bytes=(4 + pack_mib) * MIB),
+    )(cand_owner, cand_local, queries)
     recv = lax.all_to_all(packed, "index", split_axis=0, concat_axis=0, tiled=True)
-    other = lax.ppermute(recv[:, qrows : qrows + half, :], "query", [(0, 1), (1, 0)])
-    requests = recv[:, qrows + half, :].astype(jnp.int32)
+    mine = gather_table(centroids)
+    other = lax.ppermute(mine, "query", [(0, 1), (1, 0)])
+    requests = recv[:, qrows, :].astype(jnp.int32)
+    table_mib = 2 * peers * half * dim * 2 // MIB
     scores = pl.pallas_call(
         functools.partial(score_kernel, slots, q_dev, per_query, qtok),
         out_shape=jax.ShapeDtypeStruct((peers, 2 * q_dev, dim), jnp.float32),
-        in_specs=[smem, smem, vmem, vmem, vmem, vmem],
+        in_specs=[smem, smem, vmem, vmem, vmem, vmem, vmem],
         out_specs=vmem,
         scratch_shapes=[
             pltpu.VMEM((cores * half, peers * dim), jnp.bfloat16),
             pltpu.VMEM((slots * seq, dim), jnp.bfloat16),
             pltpu.VMEM((slots * seq, dim), jnp.bfloat16),
         ],
-        compiler_params=params,
-    )(requests, passage_lengths, recv, other, passage_codes.T, residuals)
+        compiler_params=pltpu.CompilerParams(vmem_limit_bytes=(8 + 2 * table_mib) * MIB),
+    )(requests, passage_lengths, recv, mine, other, passage_codes.T, residuals)
     back = lax.all_to_all(scores, "index", split_axis=0, concat_axis=0, tiled=True)
     result = jnp.sum(back[:, :, :per_query], axis=0)
     return result[:q_dev], result[q_dev:]

time: 48.3 us -> 52.8 us (1.093)
  blocking collectives: 32.4 us -> 10.4 us
  starting transfers between devices: 0.07 us -> 14.1 us
  waiting for transfers between devices: 1.51 us -> 10.2 us
  local copies, waits for them, and re-layouts: 3.72 us -> 5.7 us
  other arithmetic: 0.02 us -> 0.82 us
  Pallas kernels: 9.65 us -> 10.4 us
    all_to_all x1 -> x0, blocking collectives: 23.1 us -> none  [body(): lax.all_to_all(packed, 'index', split_axis=0, concat_axis=0, tiled=True)]
    ppermute x1 -> x5, waiting for transfers between devices: 1.51 us -> 10.2 us  [the longest x4 8.69 us: gather_table(): lax.ppermute(x, 'index', [(i, i ^ t) for i in range(peers)])]
    all_to_all x0 -> x1, starting transfers between devices: none -> 7.26 us  [body(): lax.all_to_all(packed, 'index', split_axis=0, concat_axis=0, tiled=True)]
    ppermute x1 -> x5, starting transfers between devices: 0.07 us -> 6.85 us  [the longest x4 6.78 us: gather_table(): lax.ppermute(x, 'index', [(i, i ^ t) for i in range(peers)])]
    unnamed x14 -> x12, local copies, waits for them, and re-layouts: 3.11 us -> 5.12 us
    all_to_all x1, blocking collectives: 9.3 us -> 10.4 us  [body(): lax.all_to_all(scores, 'index', split_axis=0, concat_axis=0, tiled=True)]
    another operation x0 -> x1, other arithmetic: none -> 0.76 us  [gather_table(): both = jnp.stack([centroids, swap(centroids, 1)])]
    pallas_call x1, Pallas kernels: 0.8 us -> 1.52 us  [body(): pl.pallas_call(pack_kernel, out_shape=jax.ShapeDtypeStruct((peers, rows,...]
  transfers between devices with their start and end apart: 1 -> 6, of which waited for: 1 -> 5; matrix products, arithmetic and copies ran while one was open for 0% -> 2% of each run, Pallas kernels for 0% -> 0%
where the time goes in v3:
time: 52.8 us; the launch traced here: 52.2 us
  starting transfers between devices  14.1 us (27%)
  Pallas kernels  10.4 us (20%)
  blocking collectives  10.4 us (20%)
  waiting for transfers between devices  10.2 us (19%)
  local copies, waits for them, and re-layouts  5.7 us (11%)
  other arithmetic  0.82 us (2%)
  between operations  0.69 us (1%)
    all_to_all x1, blocking collectives, body(): lax.all_to_all(scores, 'index', split_axis=0, concat_axis=0, tiled=True)  10.4 us
    pallas_call x1, Pallas kernels, body(): pl.pallas_call(functools.partial(score_kernel, slots, q_dev, per_query, q...  8.83 us
    ppermute x4, waiting for transfers between devices, gather_table(): lax.ppermute(x, 'index', [(i, i ^ t) for i in range(peers)])  8.69 us
    all_to_all x1, starting transfers between devices, body(): lax.all_to_all(packed, 'index', split_axis=0, concat_axis=0, tiled=True)  7.26 us
    ppermute x4, starting transfers between devices, gather_table(): lax.ppermute(x, 'index', [(i, i ^ t) for i in range(peers)])  6.78 us
    unnamed x12, local copies, waits for them, and re-layouts  5.12 us
    pallas_call x1, Pallas kernels, body(): pl.pallas_call(pack_kernel, out_shape=jax.ShapeDtypeStruct((peers, rows,...  1.52 us
    ppermute x1, waiting for transfers between devices, body(): other = lax.ppermute(mine, 'query', [(0, 1), (1, 0)])  1.5 us
  transfers between devices with their start and end apart: 6, of which 5 were waited for; matrix products, arithmetic and copies ran while one was open for 2% of the time, Pallas kernels for 0%

profile of v3, /device:TPU:0, one launch (start us, length us, event | category | flops | bytes accessed | tf_op | source)
XLA Modules:
  0.0 52.2 jit_solution(942251053412593152)
XLA Ops:
  0.6 0.0 copy-start.2
  0.6 0.7 %copy-done.2 = bf16[4,32,128]{2,1,0:T(8,128)(2,1)S(1)} copy-done((bf16[4,32,128]{2,1,0:T(8,128)(2,1)S(1)}, bf16[4,32,128]{2,1,0:T(8,128)(2,1)}, u32[]{:S(2)}) %copy-start.2) | copy-done | bytes 32792
  1.4 0.0 copy-start.3
  1.4 0.7 %copy-done.3 = s32[4,8]{1,0:T(4,128)S(1)} copy-done((s32[4,8]{1,0:T(4,128)S(1)}, s32[4,8]{1,0:T(4,128)}, u32[]{:S(2)}) %copy-start.3) | copy-done | bytes 152
  2.1 0.0 copy-start.4
  2.1 0.7 %copy-done.4 = s32[4,8]{1,0:T(4,128)S(1)} copy-done((s32[4,8]{1,0:T(4,128)S(1)}, s32[4,8]{1,0:T(4,128)}, u32[]{:S(2)}) %copy-start.4) | copy-done | bytes 152
  2.8 1.5 %shard_map.86 = bf16[8,144,128]{2,1,0:T(8,128)(2,1)} custom-call(s32[4,8]{1,0:T(4,128)S(1)} %copy-done.3, s32[4,8]{1,0:T(4,128)S(1)} %copy-done.4, bf16[4,32,128]{2,1,0:T(8,128)(2,1)S(1)} %copy-done.2), custom_call_target="tpu_custom_call" | custom-call | tf_op jit(solution)/shard_map/pallas_call | solution.py:184
  4.3 7.3 %all-to-all-start = ((bf16[8,144,128]{2,1,0:T(8,128)(2,1)}), bf16[8,144,128]{2,1,0:T(8,128)(2,1)S(1)}, u32[]{:S(2)}, u32[]{:S(2)}) async-start(bf16[8,144,128]{2,1,0:T(8,128)(2,1)} %shard_map.86), calls=%async_computation | async-start | bytes 589824 | tf_op jit(solution)/shard_map/all_to_all | solution.py:199
  11.5 2.0 %collective-permute-start = (bf16[256,128]{1,0:T(8,128)(2,1)}, bf16[256,128]{1,0:T(8,128)(2,1)S(1)}, u32[]{:S(2)}, u32[]{:S(2)}) collective-permute-start(bf16[256,128]{1,0:T(8,128)(2,1)} %param.10), channel_id=1, source_target_pairs={{0,2},{2,0},{4,6},{6,4},{8,10},{10,8},{12,14},{14,12},{1,3},{3,1},... | collective-permute-start | bytes 196616 | tf_op jit(solution)/shard_map/ppermute | solution.py:159
  13.6 4.0 %collective-permute-done = bf16[256,128]{1,0:T(8,128)(2,1)S(1)} collective-permute-done((bf16[256,128]{1,0:T(8,128)(2,1)}, bf16[256,128]{1,0:T(8,128)(2,1)S(1)}, u32[]{:S(2)}, u32[]{:S(2)}) %collective-permute-start) | collective-permute-done | bytes 65568 | tf_op jit(solution)/shard_map/ppermute | solution.py:159
  17.6 0.8 %fusion = bf16[2,128,128]{2,1,0:T(8,128)(2,1)S(1)} fusion(s32[]{:T(128)S(6)} %select_n.3, bf16[1,256,128]{2,1,0:T(8,128)(2,1)} %bitcast.6, bf16[1,256,128]{2,1,0:T(8,128)(2,1)S(1)} %bitcast.7), kind=kLoop, calls=%fused_computation.3 | loop fusion | flops 131072 | bytes 196612 | tf_op jit(solution)/shard_map/stack | solution.py:160
  18.4 4.1 %collective-permute-start.3 = (bf16[2,128,128]{2,1,0:T(8,128)(2,1)S(1)}, bf16[2,128,128]{2,1,0:T(8,128)(2,1)S(1)}, u32[]{:S(2)}, u32[]{:S(2)}) collective-permute-start(bf16[2,128,128]{2,1,0:T(8,128)(2,1)S(1)} %fusion), channel_id=1, source_target_pairs={{0,12},{2,14},{4,8},{6,10},{8,4},{10,6},{12,0},{14,2},{1,13},{3,15... | collective-permute-start | bytes 196616 | tf_op jit(solution)/shard_map/ppermute | solution.py:159
  22.5 0.0 collective-permute-start.2
  22.5 0.6 %collective-permute-start.1 = (bf16[2,128,128]{2,1,0:T(8,128)(2,1)S(1)}, bf16[2,128,128]{2,1,0:T(8,128)(2,1)S(1)}, u32[]{:S(2)}, u32[]{:S(2)}) collective-permute-start(bf16[2,128,128]{2,1,0:T(8,128)(2,1)S(1)} %fusion), channel_id=1, source_target_pairs={{0,4},{2,6},{4,0},{6,2},{8,12},{10,14},{12,8},{14,10},{1,5},{3,7},... | collective-permute-start | bytes 196616 | tf_op jit(solution)/shard_map/ppermute | solution.py:159
  23.1 1.7 %collective-permute-done.3 = bf16[2,128,128]{2,1,0:T(8,128)(2,1)S(1)} collective-permute-done((bf16[2,128,128]{2,1,0:T(8,128)(2,1)S(1)}, bf16[2,128,128]{2,1,0:T(8,128)(2,1)S(1)}, u32[]{:S(2)}, u32[]{:S(2)}) %collective-permute-start.3) | collective-permute-done | bytes 65568 | tf_op jit(solution)/shard_map/ppermute | solution.py:159
  24.8 2.9 %collective-permute-done.2 = bf16[2,128,128]{2,1,0:T(8,128)(2,1)S(1)} collective-permute-done((bf16[2,128,128]{2,1,0:T(8,128)(2,1)S(1)}, bf16[2,128,128]{2,1,0:T(8,128)(2,1)S(1)}, u32[]{:S(2)}, u32[]{:S(2)}) %collective-permute-start.2) | collective-permute-done | bytes 65568 | tf_op jit(solution)/shard_map/ppermute | solution.py:159
  27.7 0.1 collective-permute-done.1
  27.8 0.1 collective-permute-start.4
  27.9 0.0 all-to-all-done.recv_ref
  27.9 1.5 %collective-permute-done.4.other_ref = bf16[8,128,128]{2,1,0:T(8,128)(2,1)S(1)} collective-permute-done((bf16[8,128,128]{2,1,0:T(8,128)(2,1)S(1)}, bf16[8,128,128]{2,1,0:T(8,128)(2,1)S(1)}, u32[]{:S(2)}, u32[]{:S(2)}) %collective-permute-start.4) | collective-permute-done | bytes 262176 | tf_op jit(solution)/shard_map/ppermute | solution.py:201
  29.4 0.0 copy-start
  29.4 1.6 %copy-done = bf16[128,64,128]{2,1,0:T(8,128)(2,1)S(1)} copy-done((bf16[128,64,128]{2,1,0:T(8,128)(2,1)S(1)}, bf16[128,64,128]{2,1,0:T(8,128)(2,1)}, u32[]{:S(2)}) %copy-start) | copy-done | bytes 2097176
  31.0 0.0 copy-start.1
  31.0 0.8 %copy-done.1 = s32[128,64]{0,1:T(8,128)S(1)} copy-done((s32[128,64]{0,1:T(8,128)S(1)}, s32[128,64]{0,1:T(8,128)}, u32[]{:S(2)}) %copy-start.1) | copy-done | bytes 32792
  31.8 0.0 copy-start.5
  31.8 0.7 %copy-done.5 = s32[128]{0:T(128)S(1)} copy-done((s32[128]{0:T(128)S(1)}, s32[128]{0:T(128)}, u32[]{:S(2)}) %copy-start.5) | copy-done | bytes 536
  32.4 8.8 %shard_map.87 = f32[8,8,128]{2,1,0:T(8,128)S(1)} custom-call(s32[8,128]{1,0:T(8,128)S(1)} %bitcast.5, s32[128]{0:T(128)S(1)} %copy-done.5, bf16[8,144,128]{2,1,0:T(8,128)(2,1)S(1)} %all-to-all-done.recv_ref, bf16[8,128,128]{2,1,0:T(8,128)(2,1)S(1)} %pad_maximum_fusion.mine_ref, bf16[8,128,128]{2,1,0:T(8,128)(2,1)S(1)} %collective-permute-done.4.other_ref, ...), custom_call_target="tpu_custom_call" | custom-call | tf_op jit(solution)/shard_map/pallas_call | solution.py:204
  41.3 10.4 %all_to_all.10 = f32[8,8,128]{2,1,0:T(8,128)S(1)} all-to-all(f32[8,8,128]{2,1,0:T(8,128)S(1)} %shard_map.87), channel_id=1, replica_groups=mesh['group'=2,'index'=8,'query'=2] {'index'}, dimensions={0} | all-to-all | bytes 65536 | tf_op jit(solution)/shard_map/all_to_all | solution.py:216
  51.6 0.6 %fusion.1 = (f32[4,8]{1,0:T(4,128)}, f32[4,8]{1,0:T(4,128)}) fusion(f32[8,8]{1,0:T(8,128)S(1)} %slice_reduce_fusion), kind=kLoop, calls=%fused_computation.6 | loop fusion | bytes 512 | tf_op jit(solution)/shard_map/slice | solution.py:218
  (3 shorter events, 0.1 us)
Async XLA Ops:
  0.6 0.8 %copy-start.2 = (bf16[4,32,128]{2,1,0:T(8,128)(2,1)S(1)}, bf16[4,32,128]{2,1,0:T(8,128)(2,1)}, u32[]{:S(2)}) copy-start(bf16[4,32,128]{2,1,0:T(8,128)(2,1)} %queries_hbm.1) | copy-start | bytes 98308
  1.4 0.7 %copy-start.3 = (s32[4,8]{1,0:T(4,128)S(1)}, s32[4,8]{1,0:T(4,128)}, u32[]{:S(2)}) copy-start(s32[4,8]{1,0:T(4,128)} %owner_hbm.1) | copy-start | bytes 388
  2.1 0.7 %copy-start.4 = (s32[4,8]{1,0:T(4,128)S(1)}, s32[4,8]{1,0:T(4,128)}, u32[]{:S(2)}) copy-start(s32[4,8]{1,0:T(4,128)} %local_hbm.1) | copy-start | bytes 388
  4.3 23.6 %all-to-all-start = ((bf16[8,144,128]{2,1,0:T(8,128)(2,1)}), bf16[8,144,128]{2,1,0:T(8,128)(2,1)S(1)}, u32[]{:S(2)}, u32[]{:S(2)}) async-start(bf16[8,144,128]{2,1,0:T(8,128)(2,1)} %shard_map.86), calls=%async_computation | async-start | bytes 589824 | tf_op jit(solution)/shard_map/all_to_all | solution.py:199
  11.5 6.0 %collective-permute-start = (bf16[256,128]{1,0:T(8,128)(2,1)}, bf16[256,128]{1,0:T(8,128)(2,1)S(1)}, u32[]{:S(2)}, u32[]{:S(2)}) collective-permute-start(bf16[256,128]{1,0:T(8,128)(2,1)} %param.10), channel_id=1, source_target_pairs={{0,2},{2,0},{4,6},{6,4},{8,10},{10,8},{12,14},{14,12},{1,3},{3,1},... | collective-permute-start | bytes 196616 | tf_op jit(solution)/shard_map/ppermute | solution.py:159
  18.4 6.5 %collective-permute-start.3 = (bf16[2,128,128]{2,1,0:T(8,128)(2,1)S(1)}, bf16[2,128,128]{2,1,0:T(8,128)(2,1)S(1)}, u32[]{:S(2)}, u32[]{:S(2)}) collective-permute-start(bf16[2,128,128]{2,1,0:T(8,128)(2,1)S(1)} %fusion), channel_id=1, source_target_pairs={{0,12},{2,14},{4,8},{6,10},{8,4},{10,6},{12,0},{14,2},{1,13},{3,15... | collective-permute-start | bytes 196616 | tf_op jit(solution)/shard_map/ppermute | solution.py:159
  22.5 5.2 %collective-permute-start.2 = (bf16[2,128,128]{2,1,0:T(8,128)(2,1)S(1)}, bf16[2,128,128]{2,1,0:T(8,128)(2,1)S(1)}, u32[]{:S(2)}, u32[]{:S(2)}) collective-permute-start(bf16[2,128,128]{2,1,0:T(8,128)(2,1)S(1)} %fusion), channel_id=1, source_target_pairs={{0,8},{2,10},{4,12},{6,14},{8,0},{10,2},{12,4},{14,6},{1,9},{3,11}... | collective-permute-start | bytes 196616 | tf_op jit(solution)/shard_map/ppermute | solution.py:159
  22.5 5.3 %collective-permute-start.1 = (bf16[2,128,128]{2,1,0:T(8,128)(2,1)S(1)}, bf16[2,128,128]{2,1,0:T(8,128)(2,1)S(1)}, u32[]{:S(2)}, u32[]{:S(2)}) collective-permute-start(bf16[2,128,128]{2,1,0:T(8,128)(2,1)S(1)} %fusion), channel_id=1, source_target_pairs={{0,4},{2,6},{4,0},{6,2},{8,12},{10,14},{12,8},{14,10},{1,5},{3,7},... | collective-permute-start | bytes 196616 | tf_op jit(solution)/shard_map/ppermute | solution.py:159
  27.8 1.6 %collective-permute-start.4 = (bf16[8,128,128]{2,1,0:T(8,128)(2,1)S(1)}, bf16[8,128,128]{2,1,0:T(8,128)(2,1)S(1)}, u32[]{:S(2)}, u32[]{:S(2)}) collective-permute-start(bf16[8,128,128]{2,1,0:T(8,128)(2,1)S(1)} %pad_maximum_fusion.mine_ref), channel_id=1, source_target_pairs={{0,1},{1,0},{2,3},{3,2},{4,5},{5,4},{6,7},{7,6},{8,9},{9,8},{10,11... | collective-permute-start | bytes 786440 | tf_op jit(solution)/shard_map/ppermute | solution.py:201
  29.4 1.6 %copy-start = (bf16[128,64,128]{2,1,0:T(8,128)(2,1)S(1)}, bf16[128,64,128]{2,1,0:T(8,128)(2,1)}, u32[]{:S(2)}) copy-start(bf16[128,64,128]{2,1,0:T(8,128)(2,1)} %resid_ref.1) | copy-start | bytes 6291460
  31.0 0.8 %copy-start.1 = (s32[128,64]{0,1:T(8,128)S(1)}, s32[128,64]{0,1:T(8,128)}, u32[]{:S(2)}) copy-start(s32[128,64]{0,1:T(8,128)} %param.11) | copy-start | bytes 98308
  31.8 0.7 %copy-start.5 = (s32[128]{0:T(128)S(1)}, s32[128]{0:T(128)}, u32[]{:S(2)}) copy-start(s32[128]{0:T(128)} %length_ref.1) | copy-start | bytes 1540

commit v4 on v2

--- a/solution.py
+++ b/solution.py
@@ -16,19 +16,57 @@
     return wide * lax.rsqrt(jnp.sum(wide * wide, axis=-1, keepdims=True) + EPS)
 
 
-def pack_kernel(owner_ref, local_ref, queries_ref, cent_ref, out_ref, count_ref, req_ref):
-    peers = out_ref.shape[0]
+def pack_kernel(
+    owner_hbm,
+    local_hbm,
+    queries_hbm,
+    cent_hbm,
+    codes_hbm,
+    resid_hbm,
+    length_hbm,
+    out_ref,
+    codes_out,
+    resid_out,
+    length_out,
+    count_ref,
+    req_ref,
+    owner_ref,
+    local_ref,
+    queries_ref,
+    cent_ref,
+    sems,
+):
+    copies = out_ref.shape[0]
+    peers = count_ref.shape[0]
     q_dev, per_query = owner_ref.shape
     qrows = queries_ref.shape[0] * queries_ref.shape[1]
-    dim = queries_ref.shape[2]
-    half = cent_ref.shape[0] // lax.axis_size("query")
+    half, dim = cent_ref.shape
     core = lax.axis_index("query")
+    cent_half = cent_hbm.at[pl.ds(pl.multiple_of(core * half, 16), half)]
+    moves = [
+        pltpu.make_async_copy(src, dst, sems.at[i])
+        for i, (src, dst) in enumerate(
+            (
+                (owner_hbm, owner_ref),
+                (local_hbm, local_ref),
+                (queries_hbm, queries_ref),
+                (cent_half, cent_ref),
+                (codes_hbm, codes_out),
+                (length_hbm, length_out),
+                (resid_hbm, resid_out),
+            )
+        )
+    ]
+    for move in moves:
+        move.start()
 
     def clear(i, carry):
         count_ref[i] = 0
         return carry
 
     lax.fori_loop(0, peers, clear, 0)
+    for move in moves[:4]:
+        move.wait()
     row = lax.broadcasted_iota(jnp.int32, req_ref.shape, 0)
     lane = lax.broadcasted_iota(jnp.int32, req_ref.shape, 1)
     req = jnp.full(req_ref.shape, -1, jnp.int32)
@@ -42,48 +80,44 @@
             req = jnp.where(here & (lane == slot + dim // 2), q * per_query + k, req)
     req_ref[...] = req.astype(jnp.float32)
     qnorm = normalize(queries_ref[...].reshape(qrows, dim).astype(jnp.float32)).astype(jnp.bfloat16)
-    cent = cent_ref[pl.ds(pl.multiple_of(core * half, 16), half), :]
 
     def send(d, carry):
         out_ref[d, :qrows, :] = qnorm
-        out_ref[d, qrows : qrows + half, :] = cent
-        out_ref[d, qrows + half :, :] = jnp.broadcast_to(req_ref[pl.ds(d, 1), :], (PAD, dim)).astype(
-            jnp.bfloat16
-        )
-        return carry
-
-    lax.fori_loop(0, peers, send, 0, unroll=peers <= 16)
-
-
-def score_kernel(
-    slots,
-    q_dev,
-    per_query,
-    qtok,
-    req_ref,
-    length_ref,
-    recv_ref,
-    other_ref,
-    codes_ref,
-    resid_ref,
-    out_ref,
-    table_ref,
-    dec_ref,
-    cent_ref,
-):
+        out_ref[d, qrows : qrows + half, :] = cent_ref[...]
+        asked = req_ref[pl.ds(d, PAD), :]
+        out_ref[d, qrows + half :, :] = asked.astype(jnp.bfloat16)
+        return carry
+
+    lax.fori_loop(0, copies, send, 0)
+    for move in moves[4:]:
+        move.wait()
+
+
+def score_kernel(slots, q_dev, per_query, qtok, order, req_ref, length_ref, *refs):
+    *parts, other_ref, codes_ref, resid_ref, out_ref, query_ref, table_ref, dec_ref, cent_ref = refs
     peers, half, dim = other_ref.shape
     qrows = q_dev * qtok
     seq = codes_ref.shape[0]
     shard = 2 * half
+    me = lax.axis_index("index")
     core = lax.axis_index("query")
 
-    def place(h, carry):
-        cols = pl.ds(pl.multiple_of(h * dim, dim), dim)
-        table_ref[:half, cols] = recv_ref[h, qrows : qrows + half, :]
-        table_ref[half:, cols] = other_ref[h]
-        return carry
-
-    lax.fori_loop(0, peers, place, 0, unroll=peers <= 16)
+    def place(t, part, swapped):
+        peer = me ^ order[t] if order else t
+        cols = pl.ds(pl.multiple_of(peer * dim, dim), dim)
+        table_ref[:half, cols] = part[qrows : qrows + half, :]
+        table_ref[half:, cols] = swapped[...]
+        query_ref[t] = part[:qrows, :]
+
+    def place_loop(t, carry):
+        place(t, parts[0].at[t], other_ref.at[t])
+        return carry
+
+    if order:
+        for t in range(peers):
+            place(t, parts[t], other_ref.at[t])
+    else:
+        lax.fori_loop(0, peers, place_loop, 0)
     lane = lax.broadcasted_iota(jnp.int32, (seq, dim), 1)
     token = lax.broadcasted_iota(jnp.int32, (seq, dim), 0)
     row8 = lax.broadcasted_iota(jnp.int32, (2 * q_dev, dim), 0)
@@ -119,7 +153,7 @@
             p = jnp.maximum(req_ref[b, s], 0)
             v = cent[s * seq : (s + 1) * seq] + resid_ref[p].astype(jnp.float32)
             dec_ref[s * seq : (s + 1) * seq, :] = normalize(v).astype(jnp.bfloat16)
-        query = recv_ref[b, :qrows, :]
+        query = query_ref[b]
         nt = (((1,), (1,)), ((), ()))
         exact = lax.dot_general(dec_ref[...], query, nt, preferred_element_type=jnp.float32)
         approx = lax.dot_general(cent_ref[...], query, nt, preferred_element_type=jnp.float32)
@@ -136,7 +170,7 @@
                 )
                 score = jnp.sum(jnp.where(mine, best, 0.0), axis=1, keepdims=True)
                 total += jnp.where((row8 == q + off) & (lane8 == k) & (c >= 0), score, 0.0)
-        out_ref[b] = total
+        out_ref[me ^ (peers - 1 - b) if order else b] = total
         return carry
 
     lax.fori_loop(0, peers, block, 0)
@@ -153,33 +187,59 @@
     qrows = q_dev * qtok
     half = centroids.shape[0] // cores
     rows = qrows + half + PAD
+    order = tuple(range(peers - 1, -1, -1)) if peers <= PAD and peers & (peers - 1) == 0 else ()
     vmem = pl.BlockSpec(memory_space=pltpu.VMEM)
     smem = pl.BlockSpec(memory_space=pltpu.SMEM)
-    scratch = 2 * peers * rows * dim // MIB
-    params = pltpu.CompilerParams(vmem_limit_bytes=(8 + 2 * scratch) * MIB)
-    packed = pl.pallas_call(
+    hbm = pl.BlockSpec(memory_space=pltpu.HBM)
+    copies = 1 if order else peers
+    pack_mib = 2 * copies * rows * dim * 2 // MIB
+    held = [passage_codes.T, residuals, passage_lengths]
+    inputs = [cand_owner, cand_local, queries, centroids] + held
+    packed, *held = pl.pallas_call(
         pack_kernel,
-        out_shape=jax.ShapeDtypeStruct((peers, rows, dim), jnp.bfloat16),
-        in_specs=[smem, smem, vmem, vmem],
-        out_specs=vmem,
-        scratch_shapes=[pltpu.SMEM((peers,), jnp.int32), pltpu.VMEM((peers, dim), jnp.float32)],
-        compiler_params=params,
-    )(cand_owner, cand_local, queries, centroids)
-    recv = lax.all_to_all(packed, "index", split_axis=0, concat_axis=0, tiled=True)
-    other = lax.ppermute(recv[:, qrows : qrows + half, :], "query", [(0, 1), (1, 0)])
-    requests = recv[:, qrows + half, :].astype(jnp.int32)
+        out_shape=[jax.ShapeDtypeStruct((copies, rows, dim), jnp.bfloat16)]
+        + [jax.ShapeDtypeStruct(x.shape, x.dtype) for x in held],
+        in_specs=[hbm] * 7,
+        out_specs=[vmem] * 4,
+        scratch_shapes=[
+            pltpu.SMEM((peers,), jnp.int32),
+            pltpu.VMEM((peers + PAD, dim), jnp.float32),
+            pltpu.SMEM(cand_owner.shape, jnp.int32),
+            pltpu.SMEM(cand_local.shape, jnp.int32),
+            pltpu.VMEM(queries.shape, queries.dtype),
+            pltpu.VMEM((half, dim), centroids.dtype),
+            pltpu.SemaphoreType.DMA((7,)),
+        ],
+        compiler_params=pltpu.CompilerParams(vmem_limit_bytes=(8 + pack_mib) * MIB),
+    )(*(pltpu.with_memory_space_constraint(x, pltpu.HBM) for x in inputs))
+    codes, resid, lengths = held
+    if order:
+        parts = [
+            lax.ppermute(packed[0], "index", [(i, i ^ t) for i in range(peers)]) if t else packed[0]
+            for t in order
+        ]
+        mine = jnp.stack([part[qrows : qrows + half] for part in parts])
+        asked = jnp.stack([part[qrows + half :] for part in parts])
+        asked = lax.dynamic_index_in_dim(asked, lax.axis_index("index"), 1, keepdims=False)
+    else:
+        parts = [lax.all_to_all(packed, "index", split_axis=0, concat_axis=0, tiled=True)]
+        mine = parts[0][:, qrows : qrows + half]
+        asked = parts[0][:, qrows + half]
+    other = lax.ppermute(mine, "query", [(0, 1), (1, 0)])
+    table_mib = 2 * peers * half * dim * 2 // MIB
     scores = pl.pallas_call(
-        functools.partial(score_kernel, slots, q_dev, per_query, qtok),
+        functools.partial(score_kernel, slots, q_dev, per_query, qtok, order),
         out_shape=jax.ShapeDtypeStruct((peers, 2 * q_dev, dim), jnp.float32),
-        in_specs=[smem, smem, vmem, vmem, vmem, vmem],
+        in_specs=[smem, smem] + [vmem] * (len(parts) + 3),
         out_specs=vmem,
         scratch_shapes=[
+            pltpu.VMEM((peers, qrows, dim), jnp.bfloat16),
             pltpu.VMEM((cores * half, peers * dim), jnp.bfloat16),
             pltpu.VMEM((slots * seq, dim), jnp.bfloat16),
             pltpu.VMEM((slots * seq, dim), jnp.bfloat16),
         ],
-        compiler_params=params,
-    )(requests, passage_lengths, recv, other, passage_codes.T, residuals)
+        compiler_params=pltpu.CompilerParams(vmem_limit_bytes=(8 + 2 * table_mib) * MIB),
+    )(asked.astype(jnp.int32), lengths, *parts, other, codes, resid)
     back = lax.all_to_all(scores, "index", split_axis=0, concat_axis=0, tiled=True)
     result = jnp.sum(back[:, :, :per_query], axis=0)
     return result[:q_dev], result[q_dev:]

time: 48.3 us -> 43.8 us (0.907)
  blocking collectives: 32.4 us -> 12.1 us
  starting transfers between devices: 0.07 us -> 13.4 us
  waiting for transfers between devices: 1.51 us -> 6.07 us
  local copies, waits for them, and re-layouts: 3.72 us -> 0.72 us
  Pallas kernels: 9.65 us -> 10.6 us
    all_to_all x1 -> x0, blocking collectives: 23.1 us -> none  [body(): lax.all_to_all(packed, 'index', split_axis=0, concat_axis=0, tiled=True)]
    ppermute x1 -> x8, starting transfers between devices: 0.07 us -> 13.4 us  [the longest x7 13.3 us: body(): lax.ppermute(packed[0], 'index', [(i, i ^ t) for i in range(peers)])]
    ppermute x1 -> x8, waiting for transfers between devices: 1.51 us -> 6.07 us  [the longest x7 4.66 us: body(): lax.ppermute(packed[0], 'index', [(i, i ^ t) for i in range(peers)])]
    unnamed x14, local copies, waits for them, and re-layouts: 3.11 us -> 0.12 us
    all_to_all x1, blocking collectives: 9.3 us -> 12.1 us  [body(): lax.all_to_all(scores, 'index', split_axis=0, concat_axis=0, tiled=True)]
    pallas_call x1, Pallas kernels: 0.8 us -> 1.73 us  [body(): pl.pallas_call(pack_kernel, out_shape=[jax.ShapeDtypeStruct((copies, rows...]
  transfers between devices with their start and end apart: 1 -> 8, of which waited for: 1 -> 3; matrix products, arithmetic and copies ran while one was open for 0% -> 0% of each run, Pallas kernels for 0% -> 0%
where the time goes in v4:
time: 43.8 us; the launch traced here: 43.6 us
  starting transfers between devices  13.4 us (31%)
  blocking collectives  12.1 us (28%)
  Pallas kernels  10.6 us (24%)
  waiting for transfers between devices  6.07 us (14%)
  local copies, waits for them, and re-layouts  0.72 us (2%)
  between operations  0.71 us (2%)
    ppermute x7, starting transfers between devices, body(): lax.ppermute(packed[0], 'index', [(i, i ^ t) for i in range(peers)])  13.3 us
    all_to_all x1, blocking collectives, body(): lax.all_to_all(scores, 'index', split_axis=0, concat_axis=0, tiled=True)  12.1 us
    pallas_call x1, Pallas kernels, body(): pl.pallas_call(functools.partial(score_kernel, slots, q_dev, per_query, q...  8.85 us
    ppermute x7, waiting for transfers between devices, body(): lax.ppermute(packed[0], 'index', [(i, i ^ t) for i in range(peers)])  4.66 us
    pallas_call x1, Pallas kernels, body(): pl.pallas_call(pack_kernel, out_shape=[jax.ShapeDtypeStruct((copies, rows...  1.73 us
    ppermute x1, waiting for transfers between devices, body(): other = lax.ppermute(mine, 'query', [(0, 1), (1, 0)])  1.4 us
  transfers between devices with their start and end apart: 8, of which 3 were waited for; matrix products, arithmetic and copies ran while one was open for 0% of the time, Pallas kernels for 0%

profile of v4, /device:TPU:0, one launch (start us, length us, event | category | flops | bytes accessed | tf_op | source)
XLA Modules:
  0.0 43.6 jit_solution(706321759285334441)
XLA Ops:
  0.6 1.7 %shard_map.86 = (bf16[1,272,128]{2,1,0:T(8,128)(2,1)S(1)}, s32[64,128]{1,0:T(8,128)S(1)}, bf16[128,64,128]{2,1,0:T(8,128)(2,1)S(1)}, s32[128]{0:T(128)S(1)}) custom-call(s32[4,8]{1,0:T(4,128)} %owner_hbm.1, s32[4,8]{1,0:T(4,128)} %local_hbm.1, bf16[4,32,128]{2,1,0:T(8,128)(2,1)} %queries_hbm.1, bf16[256,128]{1,0:T(8,128)(2,1)} %cent_hbm.1, ...), custom_call_target="tpu_custom_call" | custom-call | tf_op jit(solution)/shard_map/pallas_call | solution.py:198
  2.4 6.0 %collective-permute-start = (bf16[272,128]{1,0:T(8,128)(2,1)S(1)}, bf16[272,128]{1,0:T(8,128)(2,1)S(1)}, u32[]{:S(2)}, u32[]{:S(2)}) collective-permute-start(bf16[272,128]{1,0:T(8,128)(2,1)S(1)} %bitcast.59), channel_id=1, source_target_pairs={{0,14},{2,12},{4,10},{6,8},{8,6},{10,4},{12,2},{14,0},{1,15},{3,13... | collective-permute-start | bytes 208904 | tf_op jit(solution)/shard_map/ppermute | solution.py:218
  8.4 0.2 collective-permute-start.1
  8.6 0.8 %collective-permute-start.2 = (bf16[272,128]{1,0:T(8,128)(2,1)S(1)}, bf16[272,128]{1,0:T(8,128)(2,1)S(1)}, u32[]{:S(2)}, u32[]{:S(2)}) collective-permute-start(bf16[272,128]{1,0:T(8,128)(2,1)S(1)} %bitcast.61), channel_id=1, source_target_pairs={{0,10},{2,8},{4,14},{6,12},{8,2},{10,0},{12,6},{14,4},{1,11},{3,9}... | collective-permute-start | bytes 208904 | tf_op jit(solution)/shard_map/ppermute | solution.py:218
  9.4 2.0 %collective-permute-start.3 = (bf16[272,128]{1,0:T(8,128)(2,1)S(1)}, bf16[272,128]{1,0:T(8,128)(2,1)S(1)}, u32[]{:S(2)}, u32[]{:S(2)}) collective-permute-start(bf16[272,128]{1,0:T(8,128)(2,1)S(1)} %bitcast.62), channel_id=1, source_target_pairs={{0,8},{2,10},{4,12},{6,14},{8,0},{10,2},{12,4},{14,6},{1,9},{3,11}... | collective-permute-start | bytes 208904 | tf_op jit(solution)/shard_map/ppermute | solution.py:218
  11.4 2.3 %collective-permute-start.4 = (bf16[272,128]{1,0:T(8,128)(2,1)S(1)}, bf16[272,128]{1,0:T(8,128)(2,1)S(1)}, u32[]{:S(2)}, u32[]{:S(2)}) collective-permute-start(bf16[272,128]{1,0:T(8,128)(2,1)S(1)} %bitcast.63), channel_id=1, source_target_pairs={{0,6},{2,4},{4,2},{6,0},{8,14},{10,12},{12,10},{14,8},{1,7},{3,5},... | collective-permute-start | bytes 208904 | tf_op jit(solution)/shard_map/ppermute | solution.py:218
  13.7 0.0 collective-permute-done.refs_0_
  13.7 1.4 %collective-permute-start.5 = (bf16[272,128]{1,0:T(8,128)(2,1)S(1)}, bf16[272,128]{1,0:T(8,128)(2,1)S(1)}, u32[]{:S(2)}, u32[]{:S(2)}) collective-permute-start(bf16[272,128]{1,0:T(8,128)(2,1)S(1)} %bitcast.64), channel_id=1, source_target_pairs={{0,4},{2,6},{4,0},{6,2},{8,12},{10,14},{12,8},{14,10},{1,5},{3,7},... | collective-permute-start | bytes 208904 | tf_op jit(solution)/shard_map/ppermute | solution.py:218
  15.2 0.0 collective-permute-done.1.refs_1_
  15.2 0.5 %collective-permute-start.6 = (bf16[272,128]{1,0:T(8,128)(2,1)S(1)}, bf16[272,128]{1,0:T(8,128)(2,1)S(1)}, u32[]{:S(2)}, u32[]{:S(2)}) collective-permute-start(bf16[272,128]{1,0:T(8,128)(2,1)S(1)} %bitcast.65), channel_id=1, source_target_pairs={{0,2},{2,0},{4,6},{6,4},{8,10},{10,8},{12,14},{14,12},{1,3},{3,1},... | collective-permute-start | bytes 208904 | tf_op jit(solution)/shard_map/ppermute | solution.py:218
  15.7 3.6 %collective-permute-done.2.refs_2_ = bf16[272,128]{1,0:T(8,128)(2,1)S(1)} collective-permute-done((bf16[272,128]{1,0:T(8,128)(2,1)S(1)}, bf16[272,128]{1,0:T(8,128)(2,1)S(1)}, u32[]{:S(2)}, u32[]{:S(2)}) %collective-permute-start.2) | collective-permute-done | bytes 69664 | tf_op jit(solution)/shard_map/ppermute | solution.py:218
  19.3 1.0 %collective-permute-done.3.refs_3_ = bf16[272,128]{1,0:T(8,128)(2,1)S(1)} collective-permute-done((bf16[272,128]{1,0:T(8,128)(2,1)S(1)}, bf16[272,128]{1,0:T(8,128)(2,1)S(1)}, u32[]{:S(2)}, u32[]{:S(2)}) %collective-permute-start.3) | collective-permute-done | bytes 69664 | tf_op jit(solution)/shard_map/ppermute | solution.py:218
  20.3 0.0 collective-permute-done.4.refs_4_
  20.4 0.0 collective-permute-done.5.refs_5_
  20.4 0.0 collective-permute-done.6.refs_6_
  20.4 0.1 collective-permute-start.7
  20.6 1.4 %collective-permute-done.7.refs_8_ = bf16[8,128,128]{2,1,0:T(8,128)(2,1)S(1)} collective-permute-done((bf16[8,128,128]{2,1,0:T(8,128)(2,1)S(1)}, bf16[8,128,128]{2,1,0:T(8,128)(2,1)S(1)}, u32[]{:S(2)}, u32[]{:S(2)}) %collective-permute-start.7) | collective-permute-done | bytes 262176 | tf_op jit(solution)/shard_map/ppermute | solution.py:228
  22.0 8.8 %shard_map.87 = f32[8,8,128]{2,1,0:T(8,128)S(1)} custom-call(s32[8,128]{1,0:T(8,128)S(1)} %bitcast.67, s32[128]{0:T(128)S(1)} %get-tuple-element.7.length_ref, bf16[272,128]{1,0:T(8,128)(2,1)S(1)} %collective-permute-done.refs_0_, bf16[272,128]{1,0:T(8,128)(2,1)S(1)} %collective-permute-done.1.refs_1_, bf16[272,128]{1,0:T(8,128)(2,1)S(1)} %collective-permute-done.2.refs_2_, ...), custom_call_target="tpu_custom_call" | custom-call | tf_op jit(solution)/shard_map/pallas_call | solution.py:230
  30.9 12.1 %all_to_all.5 = f32[8,8,128]{2,1,0:T(8,128)S(1)} all-to-all(f32[8,8,128]{2,1,0:T(8,128)S(1)} %shard_map.87), channel_id=1, replica_groups=mesh['group'=2,'index'=8,'query'=2] {'index'}, dimensions={0} | all-to-all | bytes 65536 | tf_op jit(solution)/shard_map/all_to_all | solution.py:243
  43.0 0.6 %fusion = (f32[4,8]{1,0:T(4,128)}, f32[4,8]{1,0:T(4,128)}) fusion(f32[8,8]{1,0:T(8,128)S(1)} %slice_reduce_fusion), kind=kLoop, calls=%fused_computation.32 | loop fusion | bytes 512 | tf_op jit(solution)/shard_map/slice | solution.py:245
  (18 shorter events, 0.2 us)
Async XLA Ops:
  2.4 11.3 %collective-permute-start = (bf16[272,128]{1,0:T(8,128)(2,1)S(1)}, bf16[272,128]{1,0:T(8,128)(2,1)S(1)}, u32[]{:S(2)}, u32[]{:S(2)}) collective-permute-start(bf16[272,128]{1,0:T(8,128)(2,1)S(1)} %bitcast.59), channel_id=1, source_target_pairs={{0,14},{2,12},{4,10},{6,8},{8,6},{10,4},{12,2},{14,0},{1,15},{3,13... | collective-permute-start | bytes 208904 | tf_op jit(solution)/shard_map/ppermute | solution.py:218
  8.4 6.7 %collective-permute-start.1 = (bf16[272,128]{1,0:T(8,128)(2,1)S(1)}, bf16[272,128]{1,0:T(8,128)(2,1)S(1)}, u32[]{:S(2)}, u32[]{:S(2)}) collective-permute-start(bf16[272,128]{1,0:T(8,128)(2,1)S(1)} %bitcast.60), channel_id=1, source_target_pairs={{0,12},{2,14},{4,8},{6,10},{8,4},{10,6},{12,0},{14,2},{1,13},{3,15... | collective-permute-start | bytes 208904 | tf_op jit(solution)/shard_map/ppermute | solution.py:218
  8.6 10.7 %collective-permute-start.2 = (bf16[272,128]{1,0:T(8,128)(2,1)S(1)}, bf16[272,128]{1,0:T(8,128)(2,1)S(1)}, u32[]{:S(2)}, u32[]{:S(2)}) collective-permute-start(bf16[272,128]{1,0:T(8,128)(2,1)S(1)} %bitcast.61), channel_id=1, source_target_pairs={{0,10},{2,8},{4,14},{6,12},{8,2},{10,0},{12,6},{14,4},{1,11},{3,9}... | collective-permute-start | bytes 208904 | tf_op jit(solution)/shard_map/ppermute | solution.py:218
  9.4 10.9 %collective-permute-start.3 = (bf16[272,128]{1,0:T(8,128)(2,1)S(1)}, bf16[272,128]{1,0:T(8,128)(2,1)S(1)}, u32[]{:S(2)}, u32[]{:S(2)}) collective-permute-start(bf16[272,128]{1,0:T(8,128)(2,1)S(1)} %bitcast.62), channel_id=1, source_target_pairs={{0,8},{2,10},{4,12},{6,14},{8,0},{10,2},{12,4},{14,6},{1,9},{3,11}... | collective-permute-start | bytes 208904 | tf_op jit(solution)/shard_map/ppermute | solution.py:218
  11.4 8.9 %collective-permute-start.4 = (bf16[272,128]{1,0:T(8,128)(2,1)S(1)}, bf16[272,128]{1,0:T(8,128)(2,1)S(1)}, u32[]{:S(2)}, u32[]{:S(2)}) collective-permute-start(bf16[272,128]{1,0:T(8,128)(2,1)S(1)} %bitcast.63), channel_id=1, source_target_pairs={{0,6},{2,4},{4,2},{6,0},{8,14},{10,12},{12,10},{14,8},{1,7},{3,5},... | collective-permute-start | bytes 208904 | tf_op jit(solution)/shard_map/ppermute | solution.py:218
  13.7 6.7 %collective-permute-start.5 = (bf16[272,128]{1,0:T(8,128)(2,1)S(1)}, bf16[272,128]{1,0:T(8,128)(2,1)S(1)}, u32[]{:S(2)}, u32[]{:S(2)}) collective-permute-start(bf16[272,128]{1,0:T(8,128)(2,1)S(1)} %bitcast.64), channel_id=1, source_target_pairs={{0,4},{2,6},{4,0},{6,2},{8,12},{10,14},{12,8},{14,10},{1,5},{3,7},... | collective-permute-start | bytes 208904 | tf_op jit(solution)/shard_map/ppermute | solution.py:218
  15.2 5.3 %collective-permute-start.6 = (bf16[272,128]{1,0:T(8,128)(2,1)S(1)}, bf16[272,128]{1,0:T(8,128)(2,1)S(1)}, u32[]{:S(2)}, u32[]{:S(2)}) collective-permute-start(bf16[272,128]{1,0:T(8,128)(2,1)S(1)} %bitcast.65), channel_id=1, source_target_pairs={{0,2},{2,0},{4,6},{6,4},{8,10},{10,8},{12,14},{14,12},{1,3},{3,1},... | collective-permute-start | bytes 208904 | tf_op jit(solution)/shard_map/ppermute | solution.py:218
  20.4 1.6 %collective-permute-start.7 = (bf16[8,128,128]{2,1,0:T(8,128)(2,1)S(1)}, bf16[8,128,128]{2,1,0:T(8,128)(2,1)S(1)}, u32[]{:S(2)}, u32[]{:S(2)}) collective-permute-start(bf16[8,128,128]{2,1,0:T(8,128)(2,1)S(1)} %constant_dynamic-update-slice_fusion.8), channel_id=1, source_target_pairs={{0,1},{1,0},{2,3},{3,2},{4,5},{5,4},{6,7},{7,6},{8,9},{9,8},{10,11... | collective-permute-start | bytes 786440 | tf_op jit(solution)/shard_map/ppermute | solution.py:228

commit v5 on v4

--- a/solution.py
+++ b/solution.py
@@ -9,6 +9,8 @@
 
 EPS = 1e-06
 PAD = 16
+UNIT = 32
+GROUP = 16
 MIB = 1024 * 1024
 
 
@@ -93,21 +95,58 @@
         move.wait()
 
 
-def score_kernel(slots, q_dev, per_query, qtok, order, req_ref, length_ref, *refs):
-    *parts, other_ref, codes_ref, resid_ref, out_ref, query_ref, table_ref, dec_ref, cent_ref = refs
+def score_kernel(slots, q_dev, per_query, qtok, order, req_ref, length_ref, codes_any, *refs):
+    (*parts, other_ref, resid_ref, out_ref) = refs[:-10]
+    query_ref, table_ref, rows_ref, more_ref, best_ref, near_ref, cand_ref, units_ref, codes_ref, sem = refs[-10:]
     peers, half, dim = other_ref.shape
     qrows = q_dev * qtok
-    seq = codes_ref.shape[0]
+    passages, seq = resid_ref.shape[:2]
+    pieces = seq // UNIT
     shard = 2 * half
+    total = peers * slots
     me = lax.axis_index("index")
     core = lax.axis_index("query")
 
+    bring = pltpu.make_async_copy(codes_any, codes_ref, sem)
+    bring.start()
+    best_ref[...] = jnp.full(best_ref.shape, -1000000000.0, jnp.float32)
+    near_ref[...] = jnp.full(near_ref.shape, -1000000000.0, jnp.float32)
+
+    piece_bits = (pieces - 1).bit_length()
+    pass_bits = (passages - 1).bit_length()
+    slot_bits = total.bit_length()
+    cand_bits = (per_query - 1).bit_length()
+    slot_at = piece_bits + pass_bits
+    head_at = slot_at + slot_bits
+
+    def field(word, at, bits):
+        return lax.shift_right_logical(word, at) & ((1 << bits) - 1)
+
+    def listing(b, n):
+        for s in range(slots):
+            p = req_ref[b, s]
+            c = req_ref[b, s + dim // 2]
+            slot = b * slots + s
+            cand_ref[pl.ds(slot, 1), :] = jnp.full((1, dim), c, jnp.int32)
+            length = jnp.where(p >= 0, length_ref[jnp.maximum(p, 0)], 0)
+            head = b * q_dev + lax.shift_right_logical(c, cand_bits)
+            word = (head << head_at) + (slot << slot_at) + (p << piece_bits)
+            for u in range(pieces):
+                units_ref[n] = word + u
+                n = n + jnp.where(length > u * UNIT, 1, 0)
+        return n
+
+    count = lax.fori_loop(0, peers, listing, 0)
+    for u in range(3 * GROUP):
+        units_ref[count + u] = total << slot_at
+
     def place(t, part, swapped):
         peer = me ^ order[t] if order else t
-        cols = pl.ds(pl.multiple_of(peer * dim, dim), dim)
-        table_ref[:half, cols] = part[qrows : qrows + half, :]
-        table_ref[half:, cols] = swapped[...]
-        query_ref[t] = part[:qrows, :]
+        first = pl.multiple_of(peer * shard + core * half, 8)
+        second = pl.multiple_of(peer * shard + half - core * half, 8)
+        table_ref[pl.ds(first, half), :] = part[qrows : qrows + half, :].astype(jnp.float32)
+        table_ref[pl.ds(second, half), :] = swapped[...].astype(jnp.float32)
+        query_ref[pl.ds(pl.multiple_of(t * qrows, 16), qrows), :] = part[:qrows, :]
 
     def place_loop(t, carry):
         place(t, parts[0].at[t], other_ref.at[t])
@@ -118,62 +157,71 @@
             place(t, parts[t], other_ref.at[t])
     else:
         lax.fori_loop(0, peers, place_loop, 0)
-    lane = lax.broadcasted_iota(jnp.int32, (seq, dim), 1)
-    token = lax.broadcasted_iota(jnp.int32, (seq, dim), 0)
-    row8 = lax.broadcasted_iota(jnp.int32, (2 * q_dev, dim), 0)
-    lane8 = lax.broadcasted_iota(jnp.int32, (2 * q_dev, dim), 1)
-    lane1 = lax.broadcasted_iota(jnp.int32, (1, dim), 1)
-
-    def block(b, carry):
-        hot, high = [], []
-        for s in range(slots):
-            p = jnp.maximum(req_ref[b, s], 0)
-            code = jnp.take_along_axis(codes_ref[...], jnp.full((seq, dim), p, jnp.int32), axis=1)
-            low = (code % shard) ^ (core * half)
-            high.append(code // shard)
-            hot.append(
-                jnp.concatenate([low == lane + i * dim for i in range(shard // dim)], axis=1)
-                .astype(jnp.float32)
-                .astype(jnp.bfloat16)
-            )
-        hot = jnp.concatenate(hot, axis=0)
-        high = jnp.concatenate(high, axis=0)
-
-        def pick(h, cent):
-            cols = pl.ds(pl.multiple_of(2 * h * dim, 2 * dim), 2 * dim)
-            rows = jnp.dot(hot, table_ref[:, cols], preferred_element_type=jnp.float32)
-            cent = jnp.where(high == 2 * h, rows[:, :dim], cent)
-            return jnp.where(high == 2 * h + 1, rows[:, dim:], cent)
-
-        cent = lax.fori_loop(
-            0, peers // 2, pick, jnp.zeros((slots * seq, dim), jnp.float32), unroll=peers <= 16
-        )
-        cent_ref[...] = cent.astype(jnp.bfloat16)
-        for s in range(slots):
-            p = jnp.maximum(req_ref[b, s], 0)
-            v = cent[s * seq : (s + 1) * seq] + resid_ref[p].astype(jnp.float32)
-            dec_ref[s * seq : (s + 1) * seq, :] = normalize(v).astype(jnp.bfloat16)
-        query = query_ref[b]
-        nt = (((1,), (1,)), ((), ()))
-        exact = lax.dot_general(dec_ref[...], query, nt, preferred_element_type=jnp.float32)
-        approx = lax.dot_general(cent_ref[...], query, nt, preferred_element_type=jnp.float32)
-        total = jnp.zeros((2 * q_dev, dim), jnp.float32)
-        for s in range(slots):
-            p = jnp.maximum(req_ref[b, s], 0)
-            c = req_ref[b, s + dim // 2]
-            q, k = c // per_query, c % per_query
-            live = token < length_ref[p]
-            mine = lane1 // qtok == q
-            for off, sims in ((0, exact), (q_dev, approx)):
-                best = jnp.max(
-                    jnp.where(live, sims[s * seq : (s + 1) * seq], -1000000000.0), axis=0, keepdims=True
-                )
-                score = jnp.sum(jnp.where(mine, best, 0.0), axis=1, keepdims=True)
-                total += jnp.where((row8 == q + off) & (lane8 == k) & (c >= 0), score, 0.0)
-        out_ref[me ^ (peers - 1 - b) if order else b] = total
+
+    token = lax.broadcasted_iota(jnp.int32, (UNIT, qtok), 0)
+    nt = (((1,), (1,)), ((), ()))
+
+    def fetch(g, j, rows):
+        word = units_ref[g * GROUP + j]
+        base = field(word, 0, piece_bits) * (UNIT * passages) + field(word, piece_bits, pass_bits)
+        for t in range(UNIT):
+            rows[j * UNIT + t : j * UNIT + t + 1, :] = table_ref[pl.ds(codes_ref[base + t * passages], 1), :]
+
+    def compare(g, j, rows):
+        word = units_ref[g * GROUP + j]
+        piece = field(word, 0, piece_bits)
+        p = field(word, piece_bits, pass_bits)
+        row = piece * (total + 8) + field(word, slot_at, slot_bits)
+        head = lax.shift_right_logical(word, head_at)
+        resid = resid_ref[p, pl.ds(pl.multiple_of(piece * UNIT, UNIT), UNIT), :]
+        query = query_ref[pl.ds(pl.multiple_of(head * qtok, qtok), qtok), :]
+        left = length_ref[p] - piece * UNIT
+        cent = rows[j * UNIT : (j + 1) * UNIT, :]
+        v = cent + resid.astype(jnp.float32)
+        both = jnp.concatenate([normalize(v).astype(jnp.bfloat16), cent.astype(jnp.bfloat16)], axis=0)
+        sims = lax.dot_general(both, query, nt, preferred_element_type=jnp.float32)
+        tops = [
+            jnp.max(jnp.where(token < left, sims[o : o + UNIT], -1000000000.0), axis=0, keepdims=True)
+            for o in (0, UNIT)
+        ]
+        return row, tops
+
+    def step(g, now, later):
+        found = []
+        for j in range(GROUP):
+            found.append(compare(g, j, now))
+            fetch(g + 1, j, later)
+        for row, (exact, approx) in found:
+            best_ref[pl.ds(row, 1), :] = exact
+            near_ref[pl.ds(row, 1), :] = approx
+
+    def pair(i, carry):
+        step(2 * i, rows_ref, more_ref)
+        step(2 * i + 1, more_ref, rows_ref)
         return carry
 
-    lax.fori_loop(0, peers, block, 0)
+    bring.wait()
+    for j in range(GROUP):
+        fetch(0, j, rows_ref)
+    lax.fori_loop(0, (count + 2 * GROUP - 1) // (2 * GROUP), pair, 0)
+
+    def score(ref):
+        best = ref[:total, :]
+        for u in range(1, pieces):
+            best = jnp.maximum(best, ref[u * (total + 8) : u * (total + 8) + total, :])
+        return jnp.sum(best, axis=1, keepdims=True)
+
+    cand = cand_ref[...]
+    lane = lax.broadcasted_iota(jnp.int32, (total, dim), 1)
+    placed = jnp.where(lane == cand, score(best_ref), 0.0)
+    placed += jnp.where(lane == cand + q_dev * per_query, score(near_ref), 0.0)
+    placed = jnp.where(cand >= 0, placed, 0.0)
+    placed = jnp.sum(placed.reshape(peers, slots, dim), axis=1)
+    turned = [placed] + [pltpu.roll(placed, dim - r * per_query, 1) for r in range(1, 2 * q_dev)]
+    for b in range(peers):
+        to = me ^ order[b] if order else b
+        for r in range(2 * q_dev):
+            out_ref[to, r : r + 1, :] = turned[r][b : b + 1, :]
 
 
 def body(queries, cand_owner, cand_local, centroids, passage_codes, residuals, passage_lengths):
@@ -193,7 +241,7 @@
     hbm = pl.BlockSpec(memory_space=pltpu.HBM)
     copies = 1 if order else peers
     pack_mib = 2 * copies * rows * dim * 2 // MIB
-    held = [passage_codes.T, residuals, passage_lengths]
+    held = [passage_codes.T.reshape(-1), residuals, passage_lengths]
     inputs = [cand_owner, cand_local, queries, centroids] + held
     packed, *held = pl.pallas_call(
         pack_kernel,
@@ -227,19 +275,26 @@
         asked = parts[0][:, qrows + half]
     other = lax.ppermute(mine, "query", [(0, 1), (1, 0)])
     table_mib = 2 * peers * half * dim * 2 // MIB
+    bests = (seq // UNIT) * (peers * slots + 8)
     scores = pl.pallas_call(
         functools.partial(score_kernel, slots, q_dev, per_query, qtok, order),
         out_shape=jax.ShapeDtypeStruct((peers, 2 * q_dev, dim), jnp.float32),
-        in_specs=[smem, smem] + [vmem] * (len(parts) + 3),
+        in_specs=[smem, smem, pl.BlockSpec(memory_space=pl.ANY)] + [vmem] * (len(parts) + 2),
         out_specs=vmem,
         scratch_shapes=[
-            pltpu.VMEM((peers, qrows, dim), jnp.bfloat16),
-            pltpu.VMEM((cores * half, peers * dim), jnp.bfloat16),
-            pltpu.VMEM((slots * seq, dim), jnp.bfloat16),
-            pltpu.VMEM((slots * seq, dim), jnp.bfloat16),
+            pltpu.VMEM((peers * qrows, dim), jnp.bfloat16),
+            pltpu.VMEM((peers * cores * half, dim), jnp.float32),
+            pltpu.VMEM((GROUP * UNIT, dim), jnp.float32),
+            pltpu.VMEM((GROUP * UNIT, dim), jnp.float32),
+            pltpu.VMEM((bests, qtok), jnp.float32),
+            pltpu.VMEM((bests, qtok), jnp.float32),
+            pltpu.VMEM((peers * slots, dim), jnp.int32),
+            pltpu.SMEM((peers * slots * (seq // UNIT) + 3 * GROUP,), jnp.int32),
+            pltpu.SMEM(codes.shape, jnp.int32),
+            pltpu.SemaphoreType.DMA,
         ],
-        compiler_params=pltpu.CompilerParams(vmem_limit_bytes=(8 + 2 * table_mib) * MIB),
-    )(asked.astype(jnp.int32), lengths, *parts, other, codes, resid)
+        compiler_params=pltpu.CompilerParams(vmem_limit_bytes=(8 + 4 * table_mib) * MIB),
+    )(asked.astype(jnp.int32), lengths, codes, *parts, other, resid)
     back = lax.all_to_all(scores, "index", split_axis=0, concat_axis=0, tiled=True)
     result = jnp.sum(back[:, :, :per_query], axis=0)
     return result[:q_dev], result[q_dev:]

time: 43.8 us -> 40.6 us (0.927)
  Pallas kernels: 10.6 us -> 5.44 us
  blocking collectives: 12.1 us -> 14.1 us
    pallas_call x1, Pallas kernels: 8.85 us -> 3.71 us  [body(): pl.pallas_call(functools.partial(score_kernel, slots, q_dev, per_query, q...]
    all_to_all x1, blocking collectives: 12.1 us -> 14.1 us  [body(): lax.all_to_all(scores, 'index', split_axis=0, concat_axis=0, tiled=True)]
where the time goes in v5:
time: 40.6 us; the launch traced here: 40.4 us
  blocking collectives  14.1 us (35%)
  starting transfers between devices  13.4 us (33%)
  waiting for transfers between devices  6.07 us (15%)
  Pallas kernels  5.44 us (13%)
  local copies, waits for them, and re-layouts  0.72 us (2%)
  between operations  0.72 us (2%)
    all_to_all x1, blocking collectives, body(): lax.all_to_all(scores, 'index', split_axis=0, concat_axis=0, tiled=True)  14.1 us
    ppermute x7, starting transfers between devices, body(): lax.ppermute(packed[0], 'index', [(i, i ^ t) for i in range(peers)])  13.3 us
    ppermute x7, waiting for transfers between devices, body(): lax.ppermute(packed[0], 'index', [(i, i ^ t) for i in range(peers)])  4.66 us
    pallas_call x1, Pallas kernels, body(): pl.pallas_call(functools.partial(score_kernel, slots, q_dev, per_query, q...  3.71 us
    pallas_call x1, Pallas kernels, body(): pl.pallas_call(pack_kernel, out_shape=[jax.ShapeDtypeStruct((copies, rows...  1.73 us
    ppermute x1, waiting for transfers between devices, body(): other = lax.ppermute(mine, 'query', [(0, 1), (1, 0)])  1.4 us
  transfers between devices with their start and end apart: 8, of which 3 were waited for; matrix products, arithmetic and copies ran while one was open for 0% of the time, Pallas kernels for 0%

profile of v5, /device:TPU:0, one launch (start us, length us, event | category | flops | bytes accessed | tf_op | source)
XLA Modules:
  0.0 40.4 jit_solution(5159392468130677499)
XLA Ops:
  0.6 1.7 %shard_map.86 = (bf16[1,272,128]{2,1,0:T(8,128)(2,1)S(1)}, s32[8192]{0:T(1024)S(1)}, bf16[128,64,128]{2,1,0:T(8,128)(2,1)S(1)}, s32[128]{0:T(128)S(1)}) custom-call(s32[4,8]{1,0:T(4,128)} %owner_hbm.1, s32[4,8]{1,0:T(4,128)} %local_hbm.1, bf16[4,32,128]{2,1,0:T(8,128)(2,1)} %queries_hbm.1, bf16[256,128]{1,0:T(8,128)(2,1)} %cent_hbm.1, s32[8192]{0:T(1024)} %bitcast.70, ...), custom_call_target="tpu_custom_call" | custom-call | tf_op jit(solution)/shard_map/pallas_call | solution.py:246
  2.4 6.0 %collective-permute-start = (bf16[272,128]{1,0:T(8,128)(2,1)S(1)}, bf16[272,128]{1,0:T(8,128)(2,1)S(1)}, u32[]{:S(2)}, u32[]{:S(2)}) collective-permute-start(bf16[272,128]{1,0:T(8,128)(2,1)S(1)} %bitcast.61), channel_id=1, source_target_pairs={{0,14},{2,12},{4,10},{6,8},{8,6},{10,4},{12,2},{14,0},{1,15},{3,13... | collective-permute-start | bytes 208904 | tf_op jit(solution)/shard_map/ppermute | solution.py:266
  8.4 0.2 collective-permute-start.1
  8.6 0.8 %collective-permute-start.2 = (bf16[272,128]{1,0:T(8,128)(2,1)S(1)}, bf16[272,128]{1,0:T(8,128)(2,1)S(1)}, u32[]{:S(2)}, u32[]{:S(2)}) collective-permute-start(bf16[272,128]{1,0:T(8,128)(2,1)S(1)} %bitcast.63), channel_id=1, source_target_pairs={{0,10},{2,8},{4,14},{6,12},{8,2},{10,0},{12,6},{14,4},{1,11},{3,9}... | collective-permute-start | bytes 208904 | tf_op jit(solution)/shard_map/ppermute | solution.py:266
  9.4 2.0 %collective-permute-start.3 = (bf16[272,128]{1,0:T(8,128)(2,1)S(1)}, bf16[272,128]{1,0:T(8,128)(2,1)S(1)}, u32[]{:S(2)}, u32[]{:S(2)}) collective-permute-start(bf16[272,128]{1,0:T(8,128)(2,1)S(1)} %bitcast.64), channel_id=1, source_target_pairs={{0,8},{2,10},{4,12},{6,14},{8,0},{10,2},{12,4},{14,6},{1,9},{3,11}... | collective-permute-start | bytes 208904 | tf_op jit(solution)/shard_map/ppermute | solution.py:266
  11.4 2.3 %collective-permute-start.4 = (bf16[272,128]{1,0:T(8,128)(2,1)S(1)}, bf16[272,128]{1,0:T(8,128)(2,1)S(1)}, u32[]{:S(2)}, u32[]{:S(2)}) collective-permute-start(bf16[272,128]{1,0:T(8,128)(2,1)S(1)} %bitcast.65), channel_id=1, source_target_pairs={{0,6},{2,4},{4,2},{6,0},{8,14},{10,12},{12,10},{14,8},{1,7},{3,5},... | collective-permute-start | bytes 208904 | tf_op jit(solution)/shard_map/ppermute | solution.py:266
  13.7 0.0 collective-permute-done.refs_0_
  13.7 1.4 %collective-permute-start.5 = (bf16[272,128]{1,0:T(8,128)(2,1)S(1)}, bf16[272,128]{1,0:T(8,128)(2,1)S(1)}, u32[]{:S(2)}, u32[]{:S(2)}) collective-permute-start(bf16[272,128]{1,0:T(8,128)(2,1)S(1)} %bitcast.66), channel_id=1, source_target_pairs={{0,4},{2,6},{4,0},{6,2},{8,12},{10,14},{12,8},{14,10},{1,5},{3,7},... | collective-permute-start | bytes 208904 | tf_op jit(solution)/shard_map/ppermute | solution.py:266
  15.2 0.0 collective-permute-done.1.refs_1_
  15.2 0.5 %collective-permute-start.6 = (bf16[272,128]{1,0:T(8,128)(2,1)S(1)}, bf16[272,128]{1,0:T(8,128)(2,1)S(1)}, u32[]{:S(2)}, u32[]{:S(2)}) collective-permute-start(bf16[272,128]{1,0:T(8,128)(2,1)S(1)} %bitcast.67), channel_id=1, source_target_pairs={{0,2},{2,0},{4,6},{6,4},{8,10},{10,8},{12,14},{14,12},{1,3},{3,1},... | collective-permute-start | bytes 208904 | tf_op jit(solution)/shard_map/ppermute | solution.py:266
  15.7 3.6 %collective-permute-done.2.refs_2_ = bf16[272,128]{1,0:T(8,128)(2,1)S(1)} collective-permute-done((bf16[272,128]{1,0:T(8,128)(2,1)S(1)}, bf16[272,128]{1,0:T(8,128)(2,1)S(1)}, u32[]{:S(2)}, u32[]{:S(2)}) %collective-permute-start.2) | collective-permute-done | bytes 69664 | tf_op jit(solution)/shard_map/ppermute | solution.py:266
  19.3 1.0 %collective-permute-done.3.refs_3_ = bf16[272,128]{1,0:T(8,128)(2,1)S(1)} collective-permute-done((bf16[272,128]{1,0:T(8,128)(2,1)S(1)}, bf16[272,128]{1,0:T(8,128)(2,1)S(1)}, u32[]{:S(2)}, u32[]{:S(2)}) %collective-permute-start.3) | collective-permute-done | bytes 69664 | tf_op jit(solution)/shard_map/ppermute | solution.py:266
  20.3 0.0 collective-permute-done.4.refs_4_
  20.4 0.0 collective-permute-done.5.refs_5_
  20.4 0.0 collective-permute-done.6.refs_6_
  20.4 0.1 collective-permute-start.7
  20.6 1.4 %collective-permute-done.7.refs_8_ = bf16[8,128,128]{2,1,0:T(8,128)(2,1)S(1)} collective-permute-done((bf16[8,128,128]{2,1,0:T(8,128)(2,1)S(1)}, bf16[8,128,128]{2,1,0:T(8,128)(2,1)S(1)}, u32[]{:S(2)}, u32[]{:S(2)}) %collective-permute-start.7) | collective-permute-done | bytes 262176 | tf_op jit(solution)/shard_map/ppermute | solution.py:276
  22.0 3.7 %shard_map.87 = f32[8,8,128]{2,1,0:T(8,128)S(1)} custom-call(s32[8,128]{1,0:T(8,128)S(1)} %bitcast.69, s32[128]{0:T(128)S(1)} %get-tuple-element.7.length_ref, s32[8192]{0:T(1024)S(1)} %get-tuple-element.8.codes_any, bf16[272,128]{1,0:T(8,128)(2,1)S(1)} %collective-permute-done.refs_0_, bf16[272,128]{1,0:T(8,128)(2,1)S(1)} %collective-permute-done.1.refs_1_, ...), custom_call_target="tpu_custom_call" | custom-call | tf_op jit(solution)/shard_map/pallas_call | solution.py:279
  25.8 14.1 %all_to_all.5 = f32[8,8,128]{2,1,0:T(8,128)S(1)} all-to-all(f32[8,8,128]{2,1,0:T(8,128)S(1)} %shard_map.87), channel_id=1, replica_groups=mesh['group'=2,'index'=8,'query'=2] {'index'}, dimensions={0} | all-to-all | bytes 65536 | tf_op jit(solution)/shard_map/all_to_all | solution.py:298
  39.8 0.6 %fusion = (f32[4,8]{1,0:T(4,128)}, f32[4,8]{1,0:T(4,128)}) fusion(f32[8,8]{1,0:T(8,128)S(1)} %slice_reduce_fusion), kind=kLoop, calls=%fused_computation.32 | loop fusion | bytes 512 | tf_op jit(solution)/shard_map/slice | solution.py:300
  (18 shorter events, 0.2 us)
Async XLA Ops:
  2.4 11.3 %collective-permute-start = (bf16[272,128]{1,0:T(8,128)(2,1)S(1)}, bf16[272,128]{1,0:T(8,128)(2,1)S(1)}, u32[]{:S(2)}, u32[]{:S(2)}) collective-permute-start(bf16[272,128]{1,0:T(8,128)(2,1)S(1)} %bitcast.61), channel_id=1, source_target_pairs={{0,14},{2,12},{4,10},{6,8},{8,6},{10,4},{12,2},{14,0},{1,15},{3,13... | collective-permute-start | bytes 208904 | tf_op jit(solution)/shard_map/ppermute | solution.py:266
  8.4 6.7 %collective-permute-start.1 = (bf16[272,128]{1,0:T(8,128)(2,1)S(1)}, bf16[272,128]{1,0:T(8,128)(2,1)S(1)}, u32[]{:S(2)}, u32[]{:S(2)}) collective-permute-start(bf16[272,128]{1,0:T(8,128)(2,1)S(1)} %bitcast.62), channel_id=1, source_target_pairs={{0,12},{2,14},{4,8},{6,10},{8,4},{10,6},{12,0},{14,2},{1,13},{3,15... | collective-permute-start | bytes 208904 | tf_op jit(solution)/shard_map/ppermute | solution.py:266
  8.6 10.7 %collective-permute-start.2 = (bf16[272,128]{1,0:T(8,128)(2,1)S(1)}, bf16[272,128]{1,0:T(8,128)(2,1)S(1)}, u32[]{:S(2)}, u32[]{:S(2)}) collective-permute-start(bf16[272,128]{1,0:T(8,128)(2,1)S(1)} %bitcast.63), channel_id=1, source_target_pairs={{0,10},{2,8},{4,14},{6,12},{8,2},{10,0},{12,6},{14,4},{1,11},{3,9}... | collective-permute-start | bytes 208904 | tf_op jit(solution)/shard_map/ppermute | solution.py:266
  9.4 10.9 %collective-permute-start.3 = (bf16[272,128]{1,0:T(8,128)(2,1)S(1)}, bf16[272,128]{1,0:T(8,128)(2,1)S(1)}, u32[]{:S(2)}, u32[]{:S(2)}) collective-permute-start(bf16[272,128]{1,0:T(8,128)(2,1)S(1)} %bitcast.64), channel_id=1, source_target_pairs={{0,8},{2,10},{4,12},{6,14},{8,0},{10,2},{12,4},{14,6},{1,9},{3,11}... | collective-permute-start | bytes 208904 | tf_op jit(solution)/shard_map/ppermute | solution.py:266
  11.4 8.9 %collective-permute-start.4 = (bf16[272,128]{1,0:T(8,128)(2,1)S(1)}, bf16[272,128]{1,0:T(8,128)(2,1)S(1)}, u32[]{:S(2)}, u32[]{:S(2)}) collective-permute-start(bf16[272,128]{1,0:T(8,128)(2,1)S(1)} %bitcast.65), channel_id=1, source_target_pairs={{0,6},{2,4},{4,2},{6,0},{8,14},{10,12},{12,10},{14,8},{1,7},{3,5},... | collective-permute-start | bytes 208904 | tf_op jit(solution)/shard_map/ppermute | solution.py:266
  13.7 6.7 %collective-permute-start.5 = (bf16[272,128]{1,0:T(8,128)(2,1)S(1)}, bf16[272,128]{1,0:T(8,128)(2,1)S(1)}, u32[]{:S(2)}, u32[]{:S(2)}) collective-permute-start(bf16[272,128]{1,0:T(8,128)(2,1)S(1)} %bitcast.66), channel_id=1, source_target_pairs={{0,4},{2,6},{4,0},{6,2},{8,12},{10,14},{12,8},{14,10},{1,5},{3,7},... | collective-permute-start | bytes 208904 | tf_op jit(solution)/shard_map/ppermute | solution.py:266
  15.2 5.3 %collective-permute-start.6 = (bf16[272,128]{1,0:T(8,128)(2,1)S(1)}, bf16[272,128]{1,0:T(8,128)(2,1)S(1)}, u32[]{:S(2)}, u32[]{:S(2)}) collective-permute-start(bf16[272,128]{1,0:T(8,128)(2,1)S(1)} %bitcast.67), channel_id=1, source_target_pairs={{0,2},{2,0},{4,6},{6,4},{8,10},{10,8},{12,14},{14,12},{1,3},{3,1},... | collective-permute-start | bytes 208904 | tf_op jit(solution)/shard_map/ppermute | solution.py:266
  20.4 1.6 %collective-permute-start.7 = (bf16[8,128,128]{2,1,0:T(8,128)(2,1)S(1)}, bf16[8,128,128]{2,1,0:T(8,128)(2,1)S(1)}, u32[]{:S(2)}, u32[]{:S(2)}) collective-permute-start(bf16[8,128,128]{2,1,0:T(8,128)(2,1)S(1)} %constant_dynamic-update-slice_fusion.8), channel_id=1, source_target_pairs={{0,1},{1,0},{2,3},{3,2},{4,5},{5,4},{6,7},{7,6},{8,9},{9,8},{10,11... | collective-permute-start | bytes 786440 | tf_op jit(solution)/shard_map/ppermute | solution.py:276

commit v6 on v5

--- a/solution.py
+++ b/solution.py
@@ -10,7 +10,8 @@
 EPS = 1e-06
 PAD = 16
 UNIT = 32
-GROUP = 16
+GROUP = 32
+FETCH = 8
 MIB = 1024 * 1024
 
 
@@ -96,8 +97,8 @@
 
 
 def score_kernel(slots, q_dev, per_query, qtok, order, req_ref, length_ref, codes_any, *refs):
-    (*parts, other_ref, resid_ref, out_ref) = refs[:-10]
-    query_ref, table_ref, rows_ref, more_ref, best_ref, near_ref, cand_ref, units_ref, codes_ref, sem = refs[-10:]
+    (*parts, other_ref, resid_ref, out_ref) = refs[:-9]
+    query_ref, table_ref, rows_ref, best_ref, near_ref, cand_ref, units_ref, codes_ref, sem = refs[-9:]
     peers, half, dim = other_ref.shape
     qrows = q_dev * qtok
     passages, seq = resid_ref.shape[:2]
@@ -123,12 +124,12 @@
         return lax.shift_right_logical(word, at) & ((1 << bits) - 1)
 
     def listing(b, n):
-        for s in range(slots):
-            p = req_ref[b, s]
-            c = req_ref[b, s + dim // 2]
+        asked = [req_ref[b, s] for s in range(slots)]
+        cands = [req_ref[b, s + dim // 2] for s in range(slots)]
+        lengths = [jnp.where(p >= 0, length_ref[jnp.maximum(p, 0)], 0) for p in asked]
+        for s, (p, c, length) in enumerate(zip(asked, cands, lengths)):
             slot = b * slots + s
             cand_ref[pl.ds(slot, 1), :] = jnp.full((1, dim), c, jnp.int32)
-            length = jnp.where(p >= 0, length_ref[jnp.maximum(p, 0)], 0)
             head = b * q_dev + lax.shift_right_logical(c, cand_bits)
             word = (head << head_at) + (slot << slot_at) + (p << piece_bits)
             for u in range(pieces):
@@ -137,7 +138,7 @@
         return n
 
     count = lax.fori_loop(0, peers, listing, 0)
-    for u in range(3 * GROUP):
+    for u in range(GROUP):
         units_ref[count + u] = total << slot_at
 
     def place(t, part, swapped):
@@ -161,49 +162,45 @@
     token = lax.broadcasted_iota(jnp.int32, (UNIT, qtok), 0)
     nt = (((1,), (1,)), ((), ()))
 
-    def fetch(g, j, rows):
-        word = units_ref[g * GROUP + j]
-        base = field(word, 0, piece_bits) * (UNIT * passages) + field(word, piece_bits, pass_bits)
-        for t in range(UNIT):
-            rows[j * UNIT + t : j * UNIT + t + 1, :] = table_ref[pl.ds(codes_ref[base + t * passages], 1), :]
-
-    def compare(g, j, rows):
-        word = units_ref[g * GROUP + j]
-        piece = field(word, 0, piece_bits)
-        p = field(word, piece_bits, pass_bits)
-        row = piece * (total + 8) + field(word, slot_at, slot_bits)
-        head = lax.shift_right_logical(word, head_at)
-        resid = resid_ref[p, pl.ds(pl.multiple_of(piece * UNIT, UNIT), UNIT), :]
-        query = query_ref[pl.ds(pl.multiple_of(head * qtok, qtok), qtok), :]
-        left = length_ref[p] - piece * UNIT
-        cent = rows[j * UNIT : (j + 1) * UNIT, :]
-        v = cent + resid.astype(jnp.float32)
-        both = jnp.concatenate([normalize(v).astype(jnp.bfloat16), cent.astype(jnp.bfloat16)], axis=0)
-        sims = lax.dot_general(both, query, nt, preferred_element_type=jnp.float32)
-        tops = [
-            jnp.max(jnp.where(token < left, sims[o : o + UNIT], -1000000000.0), axis=0, keepdims=True)
-            for o in (0, UNIT)
-        ]
-        return row, tops
-
-    def step(g, now, later):
+    def fetch(g, carry):
+        for j in range(FETCH):
+            unit = g * FETCH + j
+            word = units_ref[unit]
+            base = field(word, 0, piece_bits) * (UNIT * passages) + field(word, piece_bits, pass_bits)
+            rows = rows_ref.at[pl.ds(pl.multiple_of(unit * UNIT, UNIT), UNIT)]
+            for t in range(UNIT):
+                rows[t : t + 1, :] = table_ref[pl.ds(codes_ref[base + t * passages], 1), :]
+        return carry
+
+    def compare(g, carry):
         found = []
         for j in range(GROUP):
-            found.append(compare(g, j, now))
-            fetch(g + 1, j, later)
+            unit = g * GROUP + j
+            word = units_ref[unit]
+            piece = field(word, 0, piece_bits)
+            p = field(word, piece_bits, pass_bits)
+            row = piece * (total + 8) + field(word, slot_at, slot_bits)
+            head = lax.shift_right_logical(word, head_at)
+            resid = resid_ref[p, pl.ds(pl.multiple_of(piece * UNIT, UNIT), UNIT), :]
+            query = query_ref[pl.ds(pl.multiple_of(head * qtok, qtok), qtok), :]
+            left = length_ref[p] - piece * UNIT
+            cent = rows_ref[pl.ds(pl.multiple_of(unit * UNIT, UNIT), UNIT), :]
+            v = cent + resid.astype(jnp.float32)
+            both = jnp.concatenate([normalize(v).astype(jnp.bfloat16), cent.astype(jnp.bfloat16)], axis=0)
+            sims = lax.dot_general(both, query, nt, preferred_element_type=jnp.float32)
+            tops = [
+                jnp.max(jnp.where(token < left, sims[o : o + UNIT], -1000000000.0), axis=0, keepdims=True)
+                for o in (0, UNIT)
+            ]
+            found.append((row, tops))
         for row, (exact, approx) in found:
             best_ref[pl.ds(row, 1), :] = exact
             near_ref[pl.ds(row, 1), :] = approx
-
-    def pair(i, carry):
-        step(2 * i, rows_ref, more_ref)
-        step(2 * i + 1, more_ref, rows_ref)
         return carry
 
     bring.wait()
-    for j in range(GROUP):
-        fetch(0, j, rows_ref)
-    lax.fori_loop(0, (count + 2 * GROUP - 1) // (2 * GROUP), pair, 0)
+    lax.fori_loop(0, (count + FETCH - 1) // FETCH, fetch, 0)
+    lax.fori_loop(0, (count + GROUP - 1) // GROUP, compare, 0)
 
     def score(ref):
         best = ref[:total, :]
@@ -284,16 +281,15 @@
         scratch_shapes=[
             pltpu.VMEM((peers * qrows, dim), jnp.bfloat16),
             pltpu.VMEM((peers * cores * half, dim), jnp.float32),
-            pltpu.VMEM((GROUP * UNIT, dim), jnp.float32),
-            pltpu.VMEM((GROUP * UNIT, dim), jnp.float32),
+            pltpu.VMEM((peers * slots * seq + GROUP * UNIT, dim), jnp.float32),
             pltpu.VMEM((bests, qtok), jnp.float32),
             pltpu.VMEM((bests, qtok), jnp.float32),
             pltpu.VMEM((peers * slots, dim), jnp.int32),
-            pltpu.SMEM((peers * slots * (seq // UNIT) + 3 * GROUP,), jnp.int32),
+            pltpu.SMEM((peers * slots * (seq // UNIT) + GROUP,), jnp.int32),
             pltpu.SMEM(codes.shape, jnp.int32),
             pltpu.SemaphoreType.DMA,
         ],
-        compiler_params=pltpu.CompilerParams(vmem_limit_bytes=(8 + 4 * table_mib) * MIB),
+        compiler_params=pltpu.CompilerParams(vmem_limit_bytes=(12 + 4 * table_mib + peers * slots * seq * dim * 4 // MIB) * MIB),
     )(asked.astype(jnp.int32), lengths, codes, *parts, other, resid)
     back = lax.all_to_all(scores, "index", split_axis=0, concat_axis=0, tiled=True)
     result = jnp.sum(back[:, :, :per_query], axis=0)

time: 40.6 us -> 39.3 us (0.968)
  blocking collectives: 14.1 us -> 11 us
  Pallas kernels: 5.44 us -> 6.88 us
    all_to_all x1, blocking collectives: 14.1 us -> 11 us  [body(): lax.all_to_all(scores, 'index', split_axis=0, concat_axis=0, tiled=True)]
    pallas_call x1, Pallas kernels: 3.71 us -> 5.15 us  [body(): pl.pallas_call(functools.partial(score_kernel, slots, q_dev, per_query, q...]
where the time goes in v6:
time: 39.3 us; the launch traced here: 38.8 us
  starting transfers between devices  13.4 us (34%)
  blocking collectives  11 us (28%)
  Pallas kernels  6.88 us (18%)
  waiting for transfers between devices  6.07 us (15%)
  local copies, waits for them, and re-layouts  0.72 us (2%)
  between operations  0.72 us (2%)
    ppermute x7, starting transfers between devices, body(): lax.ppermute(packed[0], 'index', [(i, i ^ t) for i in range(peers)])  13.3 us
    all_to_all x1, blocking collectives, body(): lax.all_to_all(scores, 'index', split_axis=0, concat_axis=0, tiled=True)  11 us
    pallas_call x1, Pallas kernels, body(): pl.pallas_call(functools.partial(score_kernel, slots, q_dev, per_query, q...  5.15 us
    ppermute x7, waiting for transfers between devices, body(): lax.ppermute(packed[0], 'index', [(i, i ^ t) for i in range(peers)])  4.66 us
    pallas_call x1, Pallas kernels, body(): pl.pallas_call(pack_kernel, out_shape=[jax.ShapeDtypeStruct((copies, rows...  1.73 us
    ppermute x1, waiting for transfers between devices, body(): other = lax.ppermute(mine, 'query', [(0, 1), (1, 0)])  1.4 us
  transfers between devices with their start and end apart: 8, of which 3 were waited for; matrix products, arithmetic and copies ran while one was open for 0% of the time, Pallas kernels for 0%

profile of v6, /device:TPU:0, one launch (start us, length us, event | category | flops | bytes accessed | tf_op | source)
XLA Modules:
  0.0 38.8 jit_solution(12523825272889427332)
XLA Ops:
  0.6 1.7 %shard_map.86 = (bf16[1,272,128]{2,1,0:T(8,128)(2,1)S(1)}, s32[8192]{0:T(1024)S(1)}, bf16[128,64,128]{2,1,0:T(8,128)(2,1)S(1)}, s32[128]{0:T(128)S(1)}) custom-call(s32[4,8]{1,0:T(4,128)} %owner_hbm.1, s32[4,8]{1,0:T(4,128)} %local_hbm.1, bf16[4,32,128]{2,1,0:T(8,128)(2,1)} %queries_hbm.1, bf16[256,128]{1,0:T(8,128)(2,1)} %cent_hbm.1, s32[8192]{0:T(1024)} %bitcast.70, ...), custom_call_target="tpu_custom_call" | custom-call | tf_op jit(solution)/shard_map/pallas_call | solution.py:243
  2.4 6.0 %collective-permute-start = (bf16[272,128]{1,0:T(8,128)(2,1)S(1)}, bf16[272,128]{1,0:T(8,128)(2,1)S(1)}, u32[]{:S(2)}, u32[]{:S(2)}) collective-permute-start(bf16[272,128]{1,0:T(8,128)(2,1)S(1)} %bitcast.61), channel_id=1, source_target_pairs={{0,14},{2,12},{4,10},{6,8},{8,6},{10,4},{12,2},{14,0},{1,15},{3,13... | collective-permute-start | bytes 208904 | tf_op jit(solution)/shard_map/ppermute | solution.py:263
  8.4 0.2 collective-permute-start.1
  8.6 0.8 %collective-permute-start.2 = (bf16[272,128]{1,0:T(8,128)(2,1)S(1)}, bf16[272,128]{1,0:T(8,128)(2,1)S(1)}, u32[]{:S(2)}, u32[]{:S(2)}) collective-permute-start(bf16[272,128]{1,0:T(8,128)(2,1)S(1)} %bitcast.63), channel_id=1, source_target_pairs={{0,10},{2,8},{4,14},{6,12},{8,2},{10,0},{12,6},{14,4},{1,11},{3,9}... | collective-permute-start | bytes 208904 | tf_op jit(solution)/shard_map/ppermute | solution.py:263
  9.4 2.0 %collective-permute-start.3 = (bf16[272,128]{1,0:T(8,128)(2,1)S(1)}, bf16[272,128]{1,0:T(8,128)(2,1)S(1)}, u32[]{:S(2)}, u32[]{:S(2)}) collective-permute-start(bf16[272,128]{1,0:T(8,128)(2,1)S(1)} %bitcast.64), channel_id=1, source_target_pairs={{0,8},{2,10},{4,12},{6,14},{8,0},{10,2},{12,4},{14,6},{1,9},{3,11}... | collective-permute-start | bytes 208904 | tf_op jit(solution)/shard_map/ppermute | solution.py:263
  11.4 2.3 %collective-permute-start.4 = (bf16[272,128]{1,0:T(8,128)(2,1)S(1)}, bf16[272,128]{1,0:T(8,128)(2,1)S(1)}, u32[]{:S(2)}, u32[]{:S(2)}) collective-permute-start(bf16[272,128]{1,0:T(8,128)(2,1)S(1)} %bitcast.65), channel_id=1, source_target_pairs={{0,6},{2,4},{4,2},{6,0},{8,14},{10,12},{12,10},{14,8},{1,7},{3,5},... | collective-permute-start | bytes 208904 | tf_op jit(solution)/shard_map/ppermute | solution.py:263
  13.7 0.0 collective-permute-done.refs_0_
  13.7 1.4 %collective-permute-start.5 = (bf16[272,128]{1,0:T(8,128)(2,1)S(1)}, bf16[272,128]{1,0:T(8,128)(2,1)S(1)}, u32[]{:S(2)}, u32[]{:S(2)}) collective-permute-start(bf16[272,128]{1,0:T(8,128)(2,1)S(1)} %bitcast.66), channel_id=1, source_target_pairs={{0,4},{2,6},{4,0},{6,2},{8,12},{10,14},{12,8},{14,10},{1,5},{3,7},... | collective-permute-start | bytes 208904 | tf_op jit(solution)/shard_map/ppermute | solution.py:263
  15.2 0.0 collective-permute-done.1.refs_1_
  15.2 0.5 %collective-permute-start.6 = (bf16[272,128]{1,0:T(8,128)(2,1)S(1)}, bf16[272,128]{1,0:T(8,128)(2,1)S(1)}, u32[]{:S(2)}, u32[]{:S(2)}) collective-permute-start(bf16[272,128]{1,0:T(8,128)(2,1)S(1)} %bitcast.67), channel_id=1, source_target_pairs={{0,2},{2,0},{4,6},{6,4},{8,10},{10,8},{12,14},{14,12},{1,3},{3,1},... | collective-permute-start | bytes 208904 | tf_op jit(solution)/shard_map/ppermute | solution.py:263
  15.7 3.6 %collective-permute-done.2.refs_2_ = bf16[272,128]{1,0:T(8,128)(2,1)S(1)} collective-permute-done((bf16[272,128]{1,0:T(8,128)(2,1)S(1)}, bf16[272,128]{1,0:T(8,128)(2,1)S(1)}, u32[]{:S(2)}, u32[]{:S(2)}) %collective-permute-start.2) | collective-permute-done | bytes 69664 | tf_op jit(solution)/shard_map/ppermute | solution.py:263
  19.3 1.0 %collective-permute-done.3.refs_3_ = bf16[272,128]{1,0:T(8,128)(2,1)S(1)} collective-permute-done((bf16[272,128]{1,0:T(8,128)(2,1)S(1)}, bf16[272,128]{1,0:T(8,128)(2,1)S(1)}, u32[]{:S(2)}, u32[]{:S(2)}) %collective-permute-start.3) | collective-permute-done | bytes 69664 | tf_op jit(solution)/shard_map/ppermute | solution.py:263
  20.3 0.0 collective-permute-done.4.refs_4_
  20.4 0.0 collective-permute-done.5.refs_5_
  20.4 0.0 collective-permute-done.6.refs_6_
  20.4 0.1 collective-permute-start.7
  20.6 1.4 %collective-permute-done.7.refs_8_ = bf16[8,128,128]{2,1,0:T(8,128)(2,1)S(1)} collective-permute-done((bf16[8,128,128]{2,1,0:T(8,128)(2,1)S(1)}, bf16[8,128,128]{2,1,0:T(8,128)(2,1)S(1)}, u32[]{:S(2)}, u32[]{:S(2)}) %collective-permute-start.7) | collective-permute-done | bytes 262176 | tf_op jit(solution)/shard_map/ppermute | solution.py:273
  22.0 5.2 %shard_map.87 = f32[8,8,128]{2,1,0:T(8,128)S(1)} custom-call(s32[8,128]{1,0:T(8,128)S(1)} %bitcast.69, s32[128]{0:T(128)S(1)} %get-tuple-element.7.length_ref, s32[8192]{0:T(1024)S(1)} %get-tuple-element.8.codes_any, bf16[272,128]{1,0:T(8,128)(2,1)S(1)} %collective-permute-done.refs_0_, bf16[272,128]{1,0:T(8,128)(2,1)S(1)} %collective-permute-done.1.refs_1_, ...), custom_call_target="tpu_custom_call" | custom-call | tf_op jit(solution)/shard_map/pallas_call | solution.py:276
  27.2 11.0 %all_to_all.5 = f32[8,8,128]{2,1,0:T(8,128)S(1)} all-to-all(f32[8,8,128]{2,1,0:T(8,128)S(1)} %shard_map.87), channel_id=1, replica_groups=mesh['group'=2,'index'=8,'query'=2] {'index'}, dimensions={0} | all-to-all | bytes 65536 | tf_op jit(solution)/shard_map/all_to_all | solution.py:294
  38.2 0.6 %fusion = (f32[4,8]{1,0:T(4,128)}, f32[4,8]{1,0:T(4,128)}) fusion(f32[8,8]{1,0:T(8,128)S(1)} %slice_reduce_fusion), kind=kLoop, calls=%fused_computation.32 | loop fusion | bytes 512 | tf_op jit(solution)/shard_map/slice | solution.py:296
  (18 shorter events, 0.2 us)
Async XLA Ops:
  2.4 11.3 %collective-permute-start = (bf16[272,128]{1,0:T(8,128)(2,1)S(1)}, bf16[272,128]{1,0:T(8,128)(2,1)S(1)}, u32[]{:S(2)}, u32[]{:S(2)}) collective-permute-start(bf16[272,128]{1,0:T(8,128)(2,1)S(1)} %bitcast.61), channel_id=1, source_target_pairs={{0,14},{2,12},{4,10},{6,8},{8,6},{10,4},{12,2},{14,0},{1,15},{3,13... | collective-permute-start | bytes 208904 | tf_op jit(solution)/shard_map/ppermute | solution.py:263
  8.4 6.7 %collective-permute-start.1 = (bf16[272,128]{1,0:T(8,128)(2,1)S(1)}, bf16[272,128]{1,0:T(8,128)(2,1)S(1)}, u32[]{:S(2)}, u32[]{:S(2)}) collective-permute-start(bf16[272,128]{1,0:T(8,128)(2,1)S(1)} %bitcast.62), channel_id=1, source_target_pairs={{0,12},{2,14},{4,8},{6,10},{8,4},{10,6},{12,0},{14,2},{1,13},{3,15... | collective-permute-start | bytes 208904 | tf_op jit(solution)/shard_map/ppermute | solution.py:263
  8.6 10.7 %collective-permute-start.2 = (bf16[272,128]{1,0:T(8,128)(2,1)S(1)}, bf16[272,128]{1,0:T(8,128)(2,1)S(1)}, u32[]{:S(2)}, u32[]{:S(2)}) collective-permute-start(bf16[272,128]{1,0:T(8,128)(2,1)S(1)} %bitcast.63), channel_id=1, source_target_pairs={{0,10},{2,8},{4,14},{6,12},{8,2},{10,0},{12,6},{14,4},{1,11},{3,9}... | collective-permute-start | bytes 208904 | tf_op jit(solution)/shard_map/ppermute | solution.py:263
  9.4 10.9 %collective-permute-start.3 = (bf16[272,128]{1,0:T(8,128)(2,1)S(1)}, bf16[272,128]{1,0:T(8,128)(2,1)S(1)}, u32[]{:S(2)}, u32[]{:S(2)}) collective-permute-start(bf16[272,128]{1,0:T(8,128)(2,1)S(1)} %bitcast.64), channel_id=1, source_target_pairs={{0,8},{2,10},{4,12},{6,14},{8,0},{10,2},{12,4},{14,6},{1,9},{3,11}... | collective-permute-start | bytes 208904 | tf_op jit(solution)/shard_map/ppermute | solution.py:263
  11.4 8.9 %collective-permute-start.4 = (bf16[272,128]{1,0:T(8,128)(2,1)S(1)}, bf16[272,128]{1,0:T(8,128)(2,1)S(1)}, u32[]{:S(2)}, u32[]{:S(2)}) collective-permute-start(bf16[272,128]{1,0:T(8,128)(2,1)S(1)} %bitcast.65), channel_id=1, source_target_pairs={{0,6},{2,4},{4,2},{6,0},{8,14},{10,12},{12,10},{14,8},{1,7},{3,5},... | collective-permute-start | bytes 208904 | tf_op jit(solution)/shard_map/ppermute | solution.py:263
  13.7 6.7 %collective-permute-start.5 = (bf16[272,128]{1,0:T(8,128)(2,1)S(1)}, bf16[272,128]{1,0:T(8,128)(2,1)S(1)}, u32[]{:S(2)}, u32[]{:S(2)}) collective-permute-start(bf16[272,128]{1,0:T(8,128)(2,1)S(1)} %bitcast.66), channel_id=1, source_target_pairs={{0,4},{2,6},{4,0},{6,2},{8,12},{10,14},{12,8},{14,10},{1,5},{3,7},... | collective-permute-start | bytes 208904 | tf_op jit(solution)/shard_map/ppermute | solution.py:263
  15.2 5.3 %collective-permute-start.6 = (bf16[272,128]{1,0:T(8,128)(2,1)S(1)}, bf16[272,128]{1,0:T(8,128)(2,1)S(1)}, u32[]{:S(2)}, u32[]{:S(2)}) collective-permute-start(bf16[272,128]{1,0:T(8,128)(2,1)S(1)} %bitcast.67), channel_id=1, source_target_pairs={{0,2},{2,0},{4,6},{6,4},{8,10},{10,8},{12,14},{14,12},{1,3},{3,1},... | collective-permute-start | bytes 208904 | tf_op jit(solution)/shard_map/ppermute | solution.py:263
  20.4 1.6 %collective-permute-start.7 = (bf16[8,128,128]{2,1,0:T(8,128)(2,1)S(1)}, bf16[8,128,128]{2,1,0:T(8,128)(2,1)S(1)}, u32[]{:S(2)}, u32[]{:S(2)}) collective-permute-start(bf16[8,128,128]{2,1,0:T(8,128)(2,1)S(1)} %constant_dynamic-update-slice_fusion.8), channel_id=1, source_target_pairs={{0,1},{1,0},{2,3},{3,2},{4,5},{5,4},{6,7},{7,6},{8,9},{9,8},{10,11... | collective-permute-start | bytes 786440 | tf_op jit(solution)/shard_map/ppermute | solution.py:273

commit v7 on v6

--- a/solution.py
+++ b/solution.py
@@ -25,11 +25,9 @@
     queries_hbm,
     cent_hbm,
     codes_hbm,
-    resid_hbm,
     length_hbm,
     out_ref,
     codes_out,
-    resid_out,
     length_out,
     count_ref,
     req_ref,
@@ -56,7 +54,6 @@
                 (cent_half, cent_ref),
                 (codes_hbm, codes_out),
                 (length_hbm, length_out),
-                (resid_hbm, resid_out),
             )
         )
     ]
@@ -97,19 +94,21 @@
 
 
 def score_kernel(slots, q_dev, per_query, qtok, order, req_ref, length_ref, codes_any, *refs):
-    (*parts, other_ref, resid_ref, out_ref) = refs[:-9]
-    query_ref, table_ref, rows_ref, best_ref, near_ref, cand_ref, units_ref, codes_ref, sem = refs[-9:]
+    (*parts, other_ref, resid_hbm, out_ref) = refs[:-10]
+    query_ref, table_ref, rows_ref, best_ref, near_ref, cand_ref, units_ref, codes_ref, resid_ref, sems = refs[-10:]
     peers, half, dim = other_ref.shape
     qrows = q_dev * qtok
-    passages, seq = resid_ref.shape[:2]
+    passages, seq = resid_hbm.shape[:2]
     pieces = seq // UNIT
     shard = 2 * half
     total = peers * slots
     me = lax.axis_index("index")
     core = lax.axis_index("query")
 
-    bring = pltpu.make_async_copy(codes_any, codes_ref, sem)
-    bring.start()
+    bring_codes = pltpu.make_async_copy(codes_any, codes_ref, sems.at[0])
+    bring_codes.start()
+    bring_resid = pltpu.make_async_copy(resid_hbm, resid_ref, sems.at[1])
+    bring_resid.start()
     best_ref[...] = jnp.full(best_ref.shape, -1000000000.0, jnp.float32)
     near_ref[...] = jnp.full(near_ref.shape, -1000000000.0, jnp.float32)
 
@@ -198,8 +197,9 @@
             near_ref[pl.ds(row, 1), :] = approx
         return carry
 
-    bring.wait()
+    bring_codes.wait()
     lax.fori_loop(0, (count + FETCH - 1) // FETCH, fetch, 0)
+    bring_resid.wait()
     lax.fori_loop(0, (count + GROUP - 1) // GROUP, compare, 0)
 
     def score(ref):
@@ -238,14 +238,14 @@
     hbm = pl.BlockSpec(memory_space=pltpu.HBM)
     copies = 1 if order else peers
     pack_mib = 2 * copies * rows * dim * 2 // MIB
-    held = [passage_codes.T.reshape(-1), residuals, passage_lengths]
+    held = [passage_codes.T.reshape(-1), passage_lengths]
     inputs = [cand_owner, cand_local, queries, centroids] + held
     packed, *held = pl.pallas_call(
         pack_kernel,
         out_shape=[jax.ShapeDtypeStruct((copies, rows, dim), jnp.bfloat16)]
         + [jax.ShapeDtypeStruct(x.shape, x.dtype) for x in held],
-        in_specs=[hbm] * 7,
-        out_specs=[vmem] * 4,
+        in_specs=[hbm] * 6,
+        out_specs=[vmem] * 3,
         scratch_shapes=[
             pltpu.SMEM((peers,), jnp.int32),
             pltpu.VMEM((peers + PAD, dim), jnp.float32),
@@ -253,11 +253,12 @@
             pltpu.SMEM(cand_local.shape, jnp.int32),
             pltpu.VMEM(queries.shape, queries.dtype),
             pltpu.VMEM((half, dim), centroids.dtype),
-            pltpu.SemaphoreType.DMA((7,)),
+            pltpu.SemaphoreType.DMA((6,)),
         ],
         compiler_params=pltpu.CompilerParams(vmem_limit_bytes=(8 + pack_mib) * MIB),
     )(*(pltpu.with_memory_space_constraint(x, pltpu.HBM) for x in inputs))
-    codes, resid, lengths = held
+    codes, lengths = held
+    resid = pltpu.with_memory_space_constraint(residuals, pltpu.HBM)
     if order:
         parts = [
             lax.ppermute(packed[0], "index", [(i, i ^ t) for i in range(peers)]) if t else packed[0]
@@ -276,7 +277,7 @@
     scores = pl.pallas_call(
         functools.partial(score_kernel, slots, q_dev, per_query, qtok, order),
         out_shape=jax.ShapeDtypeStruct((peers, 2 * q_dev, dim), jnp.float32),
-        in_specs=[smem, smem, pl.BlockSpec(memory_space=pl.ANY)] + [vmem] * (len(parts) + 2),
+        in_specs=[smem, smem, pl.BlockSpec(memory_space=pl.ANY)] + [vmem] * (len(parts) + 1) + [hbm],
         out_specs=vmem,
         scratch_shapes=[
             pltpu.VMEM((peers * qrows, dim), jnp.bfloat16),
@@ -287,7 +288,8 @@
             pltpu.VMEM((peers * slots, dim), jnp.int32),
             pltpu.SMEM((peers * slots * (seq // UNIT) + GROUP,), jnp.int32),
             pltpu.SMEM(codes.shape, jnp.int32),
-            pltpu.SemaphoreType.DMA,
+            pltpu.VMEM(residuals.shape, residuals.dtype),
+            pltpu.SemaphoreType.DMA((2,)),
         ],
         compiler_params=pltpu.CompilerParams(vmem_limit_bytes=(12 + 4 * table_mib + peers * slots * seq * dim * 4 // MIB) * MIB),
     )(asked.astype(jnp.int32), lengths, codes, *parts, other, resid)

time: 39.3 us -> 39.1 us (level); the launches traced: 38.8 us -> 39.2 us
  blocking collectives: 11 us -> 14.3 us
  Pallas kernels: 6.88 us -> 3.96 us
    all_to_all x1, blocking collectives: 11 us -> 14.3 us  [body(): lax.all_to_all(scores, 'index', split_axis=0, concat_axis=0, tiled=True)]
    pallas_call x1, Pallas kernels: 5.15 us -> 2.99 us  [body(): pl.pallas_call(functools.partial(score_kernel, slots, q_dev, per_query, q...]
    pallas_call x1, Pallas kernels: 1.73 us -> 0.97 us  [body(): pl.pallas_call(pack_kernel, out_shape=[jax.ShapeDtypeStruct((copies, rows...]
where the time goes in v7:
time: 39.1 us; the launch traced here: 39.2 us
  blocking collectives  14.3 us (37%)
  starting transfers between devices  13.4 us (34%)
  waiting for transfers between devices  6.07 us (16%)
  Pallas kernels  3.96 us (10%)
  local copies, waits for them, and re-layouts  0.72 us (2%)
  between operations  0.72 us (2%)
    all_to_all x1, blocking collectives, body(): lax.all_to_all(scores, 'index', split_axis=0, concat_axis=0, tiled=True)  14.3 us
    ppermute x7, starting transfers between devices, body(): lax.ppermute(packed[0], 'index', [(i, i ^ t) for i in range(peers)])  13.3 us
    ppermute x7, waiting for transfers between devices, body(): lax.ppermute(packed[0], 'index', [(i, i ^ t) for i in range(peers)])  4.66 us
    pallas_call x1, Pallas kernels, body(): pl.pallas_call(functools.partial(score_kernel, slots, q_dev, per_query, q...  2.99 us
    ppermute x1, waiting for transfers between devices, body(): other = lax.ppermute(mine, 'query', [(0, 1), (1, 0)])  1.4 us
    pallas_call x1, Pallas kernels, body(): pl.pallas_call(pack_kernel, out_shape=[jax.ShapeDtypeStruct((copies, rows...  0.97 us
  transfers between devices with their start and end apart: 8, of which 3 were waited for; matrix products, arithmetic and copies ran while one was open for 0% of the time, Pallas kernels for 0%

profile of v7, /device:TPU:0, one launch (start us, length us, event | category | flops | bytes accessed | tf_op | source)
XLA Modules:
  0.0 39.2 jit_solution(4071666955274177579)
XLA Ops:
  0.6 1.0 %shard_map.86 = (bf16[1,272,128]{2,1,0:T(8,128)(2,1)S(1)}, s32[8192]{0:T(1024)S(1)}, s32[128]{0:T(128)S(1)}) custom-call(s32[4,8]{1,0:T(4,128)} %owner_hbm.1, s32[4,8]{1,0:T(4,128)} %local_hbm.1, bf16[4,32,128]{2,1,0:T(8,128)(2,1)} %queries_hbm.1, bf16[256,128]{1,0:T(8,128)(2,1)} %cent_hbm.1, s32[8192]{0:T(1024)} %bitcast.70, s32[128]{0:T(128)} %length_hbm.1), custom_call_target="tpu_custom_call" | custom-call | tf_op jit(solution)/shard_map/pallas_call | solution.py:243
  1.6 6.0 %collective-permute-start = (bf16[272,128]{1,0:T(8,128)(2,1)S(1)}, bf16[272,128]{1,0:T(8,128)(2,1)S(1)}, u32[]{:S(2)}, u32[]{:S(2)}) collective-permute-start(bf16[272,128]{1,0:T(8,128)(2,1)S(1)} %bitcast.61), channel_id=1, source_target_pairs={{0,14},{2,12},{4,10},{6,8},{8,6},{10,4},{12,2},{14,0},{1,15},{3,13... | collective-permute-start | bytes 208904 | tf_op jit(solution)/shard_map/ppermute | solution.py:264
  7.7 0.2 collective-permute-start.1
  7.9 0.8 %collective-permute-start.2 = (bf16[272,128]{1,0:T(8,128)(2,1)S(1)}, bf16[272,128]{1,0:T(8,128)(2,1)S(1)}, u32[]{:S(2)}, u32[]{:S(2)}) collective-permute-start(bf16[272,128]{1,0:T(8,128)(2,1)S(1)} %bitcast.63), channel_id=1, source_target_pairs={{0,10},{2,8},{4,14},{6,12},{8,2},{10,0},{12,6},{14,4},{1,11},{3,9}... | collective-permute-start | bytes 208904 | tf_op jit(solution)/shard_map/ppermute | solution.py:264
  8.6 2.0 %collective-permute-start.3 = (bf16[272,128]{1,0:T(8,128)(2,1)S(1)}, bf16[272,128]{1,0:T(8,128)(2,1)S(1)}, u32[]{:S(2)}, u32[]{:S(2)}) collective-permute-start(bf16[272,128]{1,0:T(8,128)(2,1)S(1)} %bitcast.64), channel_id=1, source_target_pairs={{0,8},{2,10},{4,12},{6,14},{8,0},{10,2},{12,4},{14,6},{1,9},{3,11}... | collective-permute-start | bytes 208904 | tf_op jit(solution)/shard_map/ppermute | solution.py:264
  10.7 2.3 %collective-permute-start.4 = (bf16[272,128]{1,0:T(8,128)(2,1)S(1)}, bf16[272,128]{1,0:T(8,128)(2,1)S(1)}, u32[]{:S(2)}, u32[]{:S(2)}) collective-permute-start(bf16[272,128]{1,0:T(8,128)(2,1)S(1)} %bitcast.65), channel_id=1, source_target_pairs={{0,6},{2,4},{4,2},{6,0},{8,14},{10,12},{12,10},{14,8},{1,7},{3,5},... | collective-permute-start | bytes 208904 | tf_op jit(solution)/shard_map/ppermute | solution.py:264
  12.9 0.0 collective-permute-done.refs_0_
  12.9 1.4 %collective-permute-start.5 = (bf16[272,128]{1,0:T(8,128)(2,1)S(1)}, bf16[272,128]{1,0:T(8,128)(2,1)S(1)}, u32[]{:S(2)}, u32[]{:S(2)}) collective-permute-start(bf16[272,128]{1,0:T(8,128)(2,1)S(1)} %bitcast.66), channel_id=1, source_target_pairs={{0,4},{2,6},{4,0},{6,2},{8,12},{10,14},{12,8},{14,10},{1,5},{3,7},... | collective-permute-start | bytes 208904 | tf_op jit(solution)/shard_map/ppermute | solution.py:264
  14.4 0.0 collective-permute-done.1.refs_1_
  14.4 0.5 %collective-permute-start.6 = (bf16[272,128]{1,0:T(8,128)(2,1)S(1)}, bf16[272,128]{1,0:T(8,128)(2,1)S(1)}, u32[]{:S(2)}, u32[]{:S(2)}) collective-permute-start(bf16[272,128]{1,0:T(8,128)(2,1)S(1)} %bitcast.67), channel_id=1, source_target_pairs={{0,2},{2,0},{4,6},{6,4},{8,10},{10,8},{12,14},{14,12},{1,3},{3,1},... | collective-permute-start | bytes 208904 | tf_op jit(solution)/shard_map/ppermute | solution.py:264
  14.9 3.6 %collective-permute-done.2.refs_2_ = bf16[272,128]{1,0:T(8,128)(2,1)S(1)} collective-permute-done((bf16[272,128]{1,0:T(8,128)(2,1)S(1)}, bf16[272,128]{1,0:T(8,128)(2,1)S(1)}, u32[]{:S(2)}, u32[]{:S(2)}) %collective-permute-start.2) | collective-permute-done | bytes 69664 | tf_op jit(solution)/shard_map/ppermute | solution.py:264
  18.6 1.0 %collective-permute-done.3.refs_3_ = bf16[272,128]{1,0:T(8,128)(2,1)S(1)} collective-permute-done((bf16[272,128]{1,0:T(8,128)(2,1)S(1)}, bf16[272,128]{1,0:T(8,128)(2,1)S(1)}, u32[]{:S(2)}, u32[]{:S(2)}) %collective-permute-start.3) | collective-permute-done | bytes 69664 | tf_op jit(solution)/shard_map/ppermute | solution.py:264
  19.6 0.0 collective-permute-done.4.refs_4_
  19.6 0.0 collective-permute-done.5.refs_5_
  19.6 0.0 collective-permute-done.6.refs_6_
  19.7 0.1 collective-permute-start.7
  19.9 1.4 %collective-permute-done.7.refs_8_ = bf16[8,128,128]{2,1,0:T(8,128)(2,1)S(1)} collective-permute-done((bf16[8,128,128]{2,1,0:T(8,128)(2,1)S(1)}, bf16[8,128,128]{2,1,0:T(8,128)(2,1)S(1)}, u32[]{:S(2)}, u32[]{:S(2)}) %collective-permute-start.7) | collective-permute-done | bytes 262176 | tf_op jit(solution)/shard_map/ppermute | solution.py:274
  21.3 3.0 %shard_map.87 = f32[8,8,128]{2,1,0:T(8,128)S(1)} custom-call(s32[8,128]{1,0:T(8,128)S(1)} %bitcast.69, s32[128]{0:T(128)S(1)} %get-tuple-element.6.length_ref, s32[8192]{0:T(1024)S(1)} %get-tuple-element.7.codes_any, bf16[272,128]{1,0:T(8,128)(2,1)S(1)} %collective-permute-done.refs_0_, bf16[272,128]{1,0:T(8,128)(2,1)S(1)} %collective-permute-done.1.refs_1_, ...), custom_call_target="tpu_custom_call" | custom-call | tf_op jit(solution)/shard_map/pallas_call | solution.py:277
  24.3 14.3 %all_to_all.5 = f32[8,8,128]{2,1,0:T(8,128)S(1)} all-to-all(f32[8,8,128]{2,1,0:T(8,128)S(1)} %shard_map.87), channel_id=1, replica_groups=mesh['group'=2,'index'=8,'query'=2] {'index'}, dimensions={0} | all-to-all | bytes 65536 | tf_op jit(solution)/shard_map/all_to_all | solution.py:296
  38.6 0.6 %fusion = (f32[4,8]{1,0:T(4,128)}, f32[4,8]{1,0:T(4,128)}) fusion(f32[8,8]{1,0:T(8,128)S(1)} %slice_reduce_fusion), kind=kLoop, calls=%fused_computation.32 | loop fusion | bytes 512 | tf_op jit(solution)/shard_map/slice | solution.py:298
  (18 shorter events, 0.2 us)
Async XLA Ops:
  1.6 11.3 %collective-permute-start = (bf16[272,128]{1,0:T(8,128)(2,1)S(1)}, bf16[272,128]{1,0:T(8,128)(2,1)S(1)}, u32[]{:S(2)}, u32[]{:S(2)}) collective-permute-start(bf16[272,128]{1,0:T(8,128)(2,1)S(1)} %bitcast.61), channel_id=1, source_target_pairs={{0,14},{2,12},{4,10},{6,8},{8,6},{10,4},{12,2},{14,0},{1,15},{3,13... | collective-permute-start | bytes 208904 | tf_op jit(solution)/shard_map/ppermute | solution.py:264
  7.7 6.7 %collective-permute-start.1 = (bf16[272,128]{1,0:T(8,128)(2,1)S(1)}, bf16[272,128]{1,0:T(8,128)(2,1)S(1)}, u32[]{:S(2)}, u32[]{:S(2)}) collective-permute-start(bf16[272,128]{1,0:T(8,128)(2,1)S(1)} %bitcast.62), channel_id=1, source_target_pairs={{0,12},{2,14},{4,8},{6,10},{8,4},{10,6},{12,0},{14,2},{1,13},{3,15... | collective-permute-start | bytes 208904 | tf_op jit(solution)/shard_map/ppermute | solution.py:264
  7.9 10.7 %collective-permute-start.2 = (bf16[272,128]{1,0:T(8,128)(2,1)S(1)}, bf16[272,128]{1,0:T(8,128)(2,1)S(1)}, u32[]{:S(2)}, u32[]{:S(2)}) collective-permute-start(bf16[272,128]{1,0:T(8,128)(2,1)S(1)} %bitcast.63), channel_id=1, source_target_pairs={{0,10},{2,8},{4,14},{6,12},{8,2},{10,0},{12,6},{14,4},{1,11},{3,9}... | collective-permute-start | bytes 208904 | tf_op jit(solution)/shard_map/ppermute | solution.py:264
  8.6 10.9 %collective-permute-start.3 = (bf16[272,128]{1,0:T(8,128)(2,1)S(1)}, bf16[272,128]{1,0:T(8,128)(2,1)S(1)}, u32[]{:S(2)}, u32[]{:S(2)}) collective-permute-start(bf16[272,128]{1,0:T(8,128)(2,1)S(1)} %bitcast.64), channel_id=1, source_target_pairs={{0,8},{2,10},{4,12},{6,14},{8,0},{10,2},{12,4},{14,6},{1,9},{3,11}... | collective-permute-start | bytes 208904 | tf_op jit(solution)/shard_map/ppermute | solution.py:264
  10.7 8.9 %collective-permute-start.4 = (bf16[272,128]{1,0:T(8,128)(2,1)S(1)}, bf16[272,128]{1,0:T(8,128)(2,1)S(1)}, u32[]{:S(2)}, u32[]{:S(2)}) collective-permute-start(bf16[272,128]{1,0:T(8,128)(2,1)S(1)} %bitcast.65), channel_id=1, source_target_pairs={{0,6},{2,4},{4,2},{6,0},{8,14},{10,12},{12,10},{14,8},{1,7},{3,5},... | collective-permute-start | bytes 208904 | tf_op jit(solution)/shard_map/ppermute | solution.py:264
  12.9 6.7 %collective-permute-start.5 = (bf16[272,128]{1,0:T(8,128)(2,1)S(1)}, bf16[272,128]{1,0:T(8,128)(2,1)S(1)}, u32[]{:S(2)}, u32[]{:S(2)}) collective-permute-start(bf16[272,128]{1,0:T(8,128)(2,1)S(1)} %bitcast.66), channel_id=1, source_target_pairs={{0,4},{2,6},{4,0},{6,2},{8,12},{10,14},{12,8},{14,10},{1,5},{3,7},... | collective-permute-start | bytes 208904 | tf_op jit(solution)/shard_map/ppermute | solution.py:264
  14.4 5.3 %collective-permute-start.6 = (bf16[272,128]{1,0:T(8,128)(2,1)S(1)}, bf16[272,128]{1,0:T(8,128)(2,1)S(1)}, u32[]{:S(2)}, u32[]{:S(2)}) collective-permute-start(bf16[272,128]{1,0:T(8,128)(2,1)S(1)} %bitcast.67), channel_id=1, source_target_pairs={{0,2},{2,0},{4,6},{6,4},{8,10},{10,8},{12,14},{14,12},{1,3},{3,1},... | collective-permute-start | bytes 208904 | tf_op jit(solution)/shard_map/ppermute | solution.py:264
  19.7 1.6 %collective-permute-start.7 = (bf16[8,128,128]{2,1,0:T(8,128)(2,1)S(1)}, bf16[8,128,128]{2,1,0:T(8,128)(2,1)S(1)}, u32[]{:S(2)}, u32[]{:S(2)}) collective-permute-start(bf16[8,128,128]{2,1,0:T(8,128)(2,1)S(1)} %constant_dynamic-update-slice_fusion.8), channel_id=1, source_target_pairs={{0,1},{1,0},{2,3},{3,2},{4,5},{5,4},{6,7},{7,6},{8,9},{9,8},{10,11... | collective-permute-start | bytes 786440 | tf_op jit(solution)/shard_map/ppermute | solution.py:274

commit v8 on v7

--- a/solution.py
+++ b/solution.py
@@ -11,6 +11,8 @@
 PAD = 16
 UNIT = 32
 GROUP = 32
+ORDER = (4, 6, 1, 3, 2, 5, 7, 0)
+RELAYED = (5, 7)
 FETCH = 8
 MIB = 1024 * 1024
 
@@ -232,7 +234,7 @@
     qrows = q_dev * qtok
     half = centroids.shape[0] // cores
     rows = qrows + half + PAD
-    order = tuple(range(peers - 1, -1, -1)) if peers <= PAD and peers & (peers - 1) == 0 else ()
+    order = ORDER if peers == len(ORDER) else ()
     vmem = pl.BlockSpec(memory_space=pltpu.VMEM)
     smem = pl.BlockSpec(memory_space=pltpu.SMEM)
     hbm = pl.BlockSpec(memory_space=pltpu.HBM)
@@ -260,10 +262,14 @@
     codes, lengths = held
     resid = pltpu.with_memory_space_constraint(residuals, pltpu.HBM)
     if order:
-        parts = [
-            lax.ppermute(packed[0], "index", [(i, i ^ t) for i in range(peers)]) if t else packed[0]
-            for t in order
-        ]
+        swap = lambda x, t: lax.ppermute(x, "index", [(i, i ^ t) for i in range(peers)])
+        known = {0: packed[0]}
+        for t in order:
+            if t not in known and t not in RELAYED:
+                known[t] = swap(known[0], t)
+        for t in RELAYED:
+            known[t] = swap(known[t ^ 1], 1)
+        parts = [known[t] for t in order]
         mine = jnp.stack([part[qrows : qrows + half] for part in parts])
         asked = jnp.stack([part[qrows + half :] for part in parts])
         asked = lax.dynamic_index_in_dim(asked, lax.axis_index("index"), 1, keepdims=False)

time: 39.1 us -> 36.5 us (0.934); the launches traced: 39.2 us -> 35.9 us
  waiting for transfers between devices: 6.07 us -> 4.31 us
  starting transfers between devices: 13.4 us -> 12.2 us
  blocking collectives: 14.3 us -> 13.8 us
    ppermute x7, waiting for transfers between devices: 4.66 us -> 2.85 us  [body(): lax.ppermute(x, 'index', [(i, i ^ t) for i in range(peers)])]
    ppermute x7, starting transfers between devices: 13.3 us -> 12.1 us  [body(): lax.ppermute(x, 'index', [(i, i ^ t) for i in range(peers)])]
    all_to_all x1, blocking collectives: 14.3 us -> 13.8 us  [body(): lax.all_to_all(scores, 'index', split_axis=0, concat_axis=0, tiled=True)]
  transfers between devices with their start and end apart: 8 -> 8, of which waited for: 3 -> 5; matrix products, arithmetic and copies ran while one was open for 0% -> 0% of each run, Pallas kernels for 0% -> 0%
where the time goes in v8:
time: 36.5 us; the launch traced here: 35.9 us
  blocking collectives  13.8 us (38%)
  starting transfers between devices  12.2 us (33%)
  waiting for transfers between devices  4.31 us (12%)
  Pallas kernels  4.18 us (11%)
  local copies, waits for them, and re-layouts  0.72 us (2%)
  between operations  0.71 us (2%)
    all_to_all x1, blocking collectives, body(): lax.all_to_all(scores, 'index', split_axis=0, concat_axis=0, tiled=True)  13.8 us
    ppermute x7, starting transfers between devices, body(): lax.ppermute(x, 'index', [(i, i ^ t) for i in range(peers)])  12.1 us
    pallas_call x1, Pallas kernels, body(): pl.pallas_call(functools.partial(score_kernel, slots, q_dev, per_query, q...  3.21 us
    ppermute x7, waiting for transfers between devices, body(): lax.ppermute(x, 'index', [(i, i ^ t) for i in range(peers)])  2.85 us
    ppermute x1, waiting for transfers between devices, body(): other = lax.ppermute(mine, 'query', [(0, 1), (1, 0)])  1.46 us
    pallas_call x1, Pallas kernels, body(): pl.pallas_call(pack_kernel, out_shape=[jax.ShapeDtypeStruct((copies, rows...  0.97 us
  transfers between devices with their start and end apart: 8, of which 5 were waited for; matrix products, arithmetic and copies ran while one was open for 0% of the time, Pallas kernels for 0%

profile of v8, /device:TPU:0, one launch (start us, length us, event | category | flops | bytes accessed | tf_op | source)
XLA Modules:
  0.0 35.9 jit_solution(10317628259391100680)
XLA Ops:
  0.6 1.0 %shard_map.86 = (bf16[1,272,128]{2,1,0:T(8,128)(2,1)S(1)}, s32[8192]{0:T(1024)S(1)}, s32[128]{0:T(128)S(1)}) custom-call(s32[4,8]{1,0:T(4,128)} %owner_hbm.1, s32[4,8]{1,0:T(4,128)} %local_hbm.1, bf16[4,32,128]{2,1,0:T(8,128)(2,1)} %queries_hbm.1, bf16[256,128]{1,0:T(8,128)(2,1)} %cent_hbm.1, s32[8192]{0:T(1024)} %bitcast.68, s32[128]{0:T(128)} %length_hbm.1), custom_call_target="tpu_custom_call" | custom-call | tf_op jit(solution)/shard_map/pallas_call | solution.py:245
  1.6 4.1 %collective-permute-start = (bf16[272,128]{1,0:T(8,128)(2,1)S(1)}, bf16[272,128]{1,0:T(8,128)(2,1)S(1)}, u32[]{:S(2)}, u32[]{:S(2)}) collective-permute-start(bf16[272,128]{1,0:T(8,128)(2,1)S(1)} %bitcast.61), channel_id=1, source_target_pairs={{0,8},{2,10},{4,12},{6,14},{8,0},{10,2},{12,4},{14,6},{1,9},{3,11}... | collective-permute-start | bytes 208904 | tf_op jit(solution)/shard_map/ppermute | solution.py:265
  5.7 1.3 %collective-permute-start.1 = (bf16[272,128]{1,0:T(8,128)(2,1)S(1)}, bf16[272,128]{1,0:T(8,128)(2,1)S(1)}, u32[]{:S(2)}, u32[]{:S(2)}) collective-permute-start(bf16[272,128]{1,0:T(8,128)(2,1)S(1)} %bitcast.62), channel_id=1, source_target_pairs={{0,12},{2,14},{4,8},{6,10},{8,4},{10,6},{12,0},{14,2},{1,13},{3,15... | collective-permute-start | bytes 208904 | tf_op jit(solution)/shard_map/ppermute | solution.py:265
  7.1 1.5 %collective-permute-start.2 = (bf16[272,128]{1,0:T(8,128)(2,1)S(1)}, bf16[272,128]{1,0:T(8,128)(2,1)S(1)}, u32[]{:S(2)}, u32[]{:S(2)}) collective-permute-start(bf16[272,128]{1,0:T(8,128)(2,1)S(1)} %bitcast.63), channel_id=1, source_target_pairs={{0,2},{2,0},{4,6},{6,4},{8,10},{10,8},{12,14},{14,12},{1,3},{3,1},... | collective-permute-start | bytes 208904 | tf_op jit(solution)/shard_map/ppermute | solution.py:265
  8.6 0.2 collective-permute-start.3
  8.8 1.8 %collective-permute-start.4 = (bf16[272,128]{1,0:T(8,128)(2,1)S(1)}, bf16[272,128]{1,0:T(8,128)(2,1)S(1)}, u32[]{:S(2)}, u32[]{:S(2)}) collective-permute-start(bf16[272,128]{1,0:T(8,128)(2,1)S(1)} %bitcast.65), channel_id=1, source_target_pairs={{0,4},{2,6},{4,0},{6,2},{8,12},{10,14},{12,8},{14,10},{1,5},{3,7},... | collective-permute-start | bytes 208904 | tf_op jit(solution)/shard_map/ppermute | solution.py:265
  10.6 0.0 collective-permute-done.refs_0_
  10.6 1.7 %collective-permute-start.5 = (bf16[272,128]{1,0:T(8,128)(2,1)S(1)}, bf16[272,128]{1,0:T(8,128)(2,1)S(1)}, u32[]{:S(2)}, u32[]{:S(2)}) collective-permute-start(bf16[272,128]{1,0:T(8,128)(2,1)S(1)} %collective-permute-done.refs_0_), channel_id=1, source_target_pairs={{0,2},{2,0},{4,6},{6,4},{8,10},{10,8},{12,14},{14,12},{1,3},{3,1},... | collective-permute-start | bytes 208904 | tf_op jit(solution)/shard_map/ppermute | solution.py:265
  12.3 0.1 collective-permute-done.1.refs_1_
  12.4 1.5 %collective-permute-start.6 = (bf16[272,128]{1,0:T(8,128)(2,1)S(1)}, bf16[272,128]{1,0:T(8,128)(2,1)S(1)}, u32[]{:S(2)}, u32[]{:S(2)}) collective-permute-start(bf16[272,128]{1,0:T(8,128)(2,1)S(1)} %collective-permute-done.1.refs_1_), channel_id=1, source_target_pairs={{0,2},{2,0},{4,6},{6,4},{8,10},{10,8},{12,14},{14,12},{1,3},{3,1},... | collective-permute-start | bytes 208904 | tf_op jit(solution)/shard_map/ppermute | solution.py:265
  13.9 0.0 collective-permute-done.2.refs_2_
  13.9 0.7 %collective-permute-done.3.refs_3_ = bf16[272,128]{1,0:T(8,128)(2,1)S(1)} collective-permute-done((bf16[272,128]{1,0:T(8,128)(2,1)S(1)}, bf16[272,128]{1,0:T(8,128)(2,1)S(1)}, u32[]{:S(2)}, u32[]{:S(2)}) %collective-permute-start.3) | collective-permute-done | bytes 69664 | tf_op jit(solution)/shard_map/ppermute | solution.py:265
  14.6 0.0 collective-permute-done.4.refs_4_
  14.7 0.5 %collective-permute-done.5.refs_5_ = bf16[272,128]{1,0:T(8,128)(2,1)S(1)} collective-permute-done((bf16[272,128]{1,0:T(8,128)(2,1)S(1)}, bf16[272,128]{1,0:T(8,128)(2,1)S(1)}, u32[]{:S(2)}, u32[]{:S(2)}) %collective-permute-start.5) | collective-permute-done | bytes 69664 | tf_op jit(solution)/shard_map/ppermute | solution.py:265
  15.2 1.5 %collective-permute-done.6.refs_6_ = bf16[272,128]{1,0:T(8,128)(2,1)S(1)} collective-permute-done((bf16[272,128]{1,0:T(8,128)(2,1)S(1)}, bf16[272,128]{1,0:T(8,128)(2,1)S(1)}, u32[]{:S(2)}, u32[]{:S(2)}) %collective-permute-start.6) | collective-permute-done | bytes 69664 | tf_op jit(solution)/shard_map/ppermute | solution.py:265
  16.7 0.1 collective-permute-start.7
  16.9 1.5 %collective-permute-done.7.refs_8_ = bf16[8,128,128]{2,1,0:T(8,128)(2,1)S(1)} collective-permute-done((bf16[8,128,128]{2,1,0:T(8,128)(2,1)S(1)}, bf16[8,128,128]{2,1,0:T(8,128)(2,1)S(1)}, u32[]{:S(2)}, u32[]{:S(2)}) %collective-permute-start.7) | collective-permute-done | bytes 262176 | tf_op jit(solution)/shard_map/ppermute | solution.py:280
  18.3 3.2 %shard_map.87 = f32[8,8,128]{2,1,0:T(8,128)S(1)} custom-call(s32[8,128]{1,0:T(8,128)S(1)} %bitcast.67, s32[128]{0:T(128)S(1)} %get-tuple-element.6.length_ref, s32[8192]{0:T(1024)S(1)} %get-tuple-element.7.codes_any, bf16[272,128]{1,0:T(8,128)(2,1)S(1)} %collective-permute-done.refs_0_, bf16[272,128]{1,0:T(8,128)(2,1)S(1)} %collective-permute-done.1.refs_1_, ...), custom_call_target="tpu_custom_call" | custom-call | tf_op jit(solution)/shard_map/pallas_call | solution.py:283
  21.5 13.8 %all_to_all.5 = f32[8,8,128]{2,1,0:T(8,128)S(1)} all-to-all(f32[8,8,128]{2,1,0:T(8,128)S(1)} %shard_map.87), channel_id=1, replica_groups=mesh['group'=2,'index'=8,'query'=2] {'index'}, dimensions={0} | all-to-all | bytes 65536 | tf_op jit(solution)/shard_map/all_to_all | solution.py:302
  35.3 0.6 %fusion = (f32[4,8]{1,0:T(4,128)}, f32[4,8]{1,0:T(4,128)}) fusion(f32[8,8]{1,0:T(8,128)S(1)} %slice_reduce_fusion), kind=kLoop, calls=%fused_computation.32 | loop fusion | bytes 512 | tf_op jit(solution)/shard_map/slice | solution.py:304
  (18 shorter events, 0.2 us)
Async XLA Ops:
  1.6 8.9 %collective-permute-start = (bf16[272,128]{1,0:T(8,128)(2,1)S(1)}, bf16[272,128]{1,0:T(8,128)(2,1)S(1)}, u32[]{:S(2)}, u32[]{:S(2)}) collective-permute-start(bf16[272,128]{1,0:T(8,128)(2,1)S(1)} %bitcast.61), channel_id=1, source_target_pairs={{0,8},{2,10},{4,12},{6,14},{8,0},{10,2},{12,4},{14,6},{1,9},{3,11}... | collective-permute-start | bytes 208904 | tf_op jit(solution)/shard_map/ppermute | solution.py:265
  5.7 6.7 %collective-permute-start.1 = (bf16[272,128]{1,0:T(8,128)(2,1)S(1)}, bf16[272,128]{1,0:T(8,128)(2,1)S(1)}, u32[]{:S(2)}, u32[]{:S(2)}) collective-permute-start(bf16[272,128]{1,0:T(8,128)(2,1)S(1)} %bitcast.62), channel_id=1, source_target_pairs={{0,12},{2,14},{4,8},{6,10},{8,4},{10,6},{12,0},{14,2},{1,13},{3,15... | collective-permute-start | bytes 208904 | tf_op jit(solution)/shard_map/ppermute | solution.py:265
  7.1 6.9 %collective-permute-start.2 = (bf16[272,128]{1,0:T(8,128)(2,1)S(1)}, bf16[272,128]{1,0:T(8,128)(2,1)S(1)}, u32[]{:S(2)}, u32[]{:S(2)}) collective-permute-start(bf16[272,128]{1,0:T(8,128)(2,1)S(1)} %bitcast.63), channel_id=1, source_target_pairs={{0,2},{2,0},{4,6},{6,4},{8,10},{10,8},{12,14},{14,12},{1,3},{3,1},... | collective-permute-start | bytes 208904 | tf_op jit(solution)/shard_map/ppermute | solution.py:265
  8.6 6.1 %collective-permute-start.3 = (bf16[272,128]{1,0:T(8,128)(2,1)S(1)}, bf16[272,128]{1,0:T(8,128)(2,1)S(1)}, u32[]{:S(2)}, u32[]{:S(2)}) collective-permute-start(bf16[272,128]{1,0:T(8,128)(2,1)S(1)} %bitcast.64), channel_id=1, source_target_pairs={{0,6},{2,4},{4,2},{6,0},{8,14},{10,12},{12,10},{14,8},{1,7},{3,5},... | collective-permute-start | bytes 208904 | tf_op jit(solution)/shard_map/ppermute | solution.py:265
  8.8 5.9 %collective-permute-start.4 = (bf16[272,128]{1,0:T(8,128)(2,1)S(1)}, bf16[272,128]{1,0:T(8,128)(2,1)S(1)}, u32[]{:S(2)}, u32[]{:S(2)}) collective-permute-start(bf16[272,128]{1,0:T(8,128)(2,1)S(1)} %bitcast.65), channel_id=1, source_target_pairs={{0,4},{2,6},{4,0},{6,2},{8,12},{10,14},{12,8},{14,10},{1,5},{3,7},... | collective-permute-start | bytes 208904 | tf_op jit(solution)/shard_map/ppermute | solution.py:265
  10.6 4.6 %collective-permute-start.5 = (bf16[272,128]{1,0:T(8,128)(2,1)S(1)}, bf16[272,128]{1,0:T(8,128)(2,1)S(1)}, u32[]{:S(2)}, u32[]{:S(2)}) collective-permute-start(bf16[272,128]{1,0:T(8,128)(2,1)S(1)} %collective-permute-done.refs_0_), channel_id=1, source_target_pairs={{0,2},{2,0},{4,6},{6,4},{8,10},{10,8},{12,14},{14,12},{1,3},{3,1},... | collective-permute-start | bytes 208904 | tf_op jit(solution)/shard_map/ppermute | solution.py:265
  12.4 4.3 %collective-permute-start.6 = (bf16[272,128]{1,0:T(8,128)(2,1)S(1)}, bf16[272,128]{1,0:T(8,128)(2,1)S(1)}, u32[]{:S(2)}, u32[]{:S(2)}) collective-permute-start(bf16[272,128]{1,0:T(8,128)(2,1)S(1)} %collective-permute-done.1.refs_1_), channel_id=1, source_target_pairs={{0,2},{2,0},{4,6},{6,4},{8,10},{10,8},{12,14},{14,12},{1,3},{3,1},... | collective-permute-start | bytes 208904 | tf_op jit(solution)/shard_map/ppermute | solution.py:265
  16.7 1.6 %collective-permute-start.7 = (bf16[8,128,128]{2,1,0:T(8,128)(2,1)S(1)}, bf16[8,128,128]{2,1,0:T(8,128)(2,1)S(1)}, u32[]{:S(2)}, u32[]{:S(2)}) collective-permute-start(bf16[8,128,128]{2,1,0:T(8,128)(2,1)S(1)} %constant_dynamic-update-slice_fusion.8), channel_id=1, source_target_pairs={{0,1},{1,0},{2,3},{3,2},{4,5},{5,4},{6,7},{7,6},{8,9},{9,8},{10,11... | collective-permute-start | bytes 786440 | tf_op jit(solution)/shard_map/ppermute | solution.py:280

commit v9 on v8

--- a/solution.py
+++ b/solution.py
@@ -31,6 +31,7 @@
     out_ref,
     codes_out,
     length_out,
+    codes_ref,
     count_ref,
     req_ref,
     owner_ref,
@@ -54,7 +55,7 @@
                 (local_hbm, local_ref),
                 (queries_hbm, queries_ref),
                 (cent_half, cent_ref),
-                (codes_hbm, codes_out),
+                (codes_hbm, codes_ref),
                 (length_hbm, length_out),
             )
         )
@@ -93,6 +94,15 @@
     lax.fori_loop(0, copies, send, 0)
     for move in moves[4:]:
         move.wait()
+    pair = UNIT // 2
+    for u in range(codes_ref.shape[0] // UNIT):
+        low = codes_ref[u * UNIT : u * UNIT + pair, :]
+        high = codes_ref[u * UNIT + pair : (u + 1) * UNIT, :]
+        codes_out[u * pair : (u + 1) * pair, :] = low | (high << 16)
+
+
+def field_bits(peers, slots, passages, seq):
+    return (seq // UNIT - 1).bit_length(), (passages - 1).bit_length(), (peers * slots).bit_length()
 
 
 def score_kernel(slots, q_dev, per_query, qtok, order, req_ref, length_ref, codes_any, *refs):
@@ -114,9 +124,7 @@
     best_ref[...] = jnp.full(best_ref.shape, -1000000000.0, jnp.float32)
     near_ref[...] = jnp.full(near_ref.shape, -1000000000.0, jnp.float32)
 
-    piece_bits = (pieces - 1).bit_length()
-    pass_bits = (passages - 1).bit_length()
-    slot_bits = total.bit_length()
+    piece_bits, pass_bits, slot_bits = field_bits(peers, slots, passages, seq)
     cand_bits = (per_query - 1).bit_length()
     slot_at = piece_bits + pass_bits
     head_at = slot_at + slot_bits
@@ -125,14 +133,10 @@
         return lax.shift_right_logical(word, at) & ((1 << bits) - 1)
 
     def listing(b, n):
-        asked = [req_ref[b, s] for s in range(slots)]
-        cands = [req_ref[b, s + dim // 2] for s in range(slots)]
-        lengths = [jnp.where(p >= 0, length_ref[jnp.maximum(p, 0)], 0) for p in asked]
-        for s, (p, c, length) in enumerate(zip(asked, cands, lengths)):
-            slot = b * slots + s
-            cand_ref[pl.ds(slot, 1), :] = jnp.full((1, dim), c, jnp.int32)
-            head = b * q_dev + lax.shift_right_logical(c, cand_bits)
-            word = (head << head_at) + (slot << slot_at) + (p << piece_bits)
+        words = [req_ref[b, s] for s in range(slots)]
+        lengths = [jnp.where(w >= 0, length_ref[field(w, piece_bits, pass_bits)], 0) for w in words]
+        for s, (word, length) in enumerate(zip(words, lengths)):
+            cand_ref[pl.ds(b * slots + s, 1), :] = jnp.full((1, dim), req_ref[b, s + dim // 2], jnp.int32)
             for u in range(pieces):
                 units_ref[n] = word + u
                 n = n + jnp.where(length > u * UNIT, 1, 0)
@@ -163,14 +167,18 @@
     token = lax.broadcasted_iota(jnp.int32, (UNIT, qtok), 0)
     nt = (((1,), (1,)), ((), ()))
 
+    pair = UNIT // 2
+
     def fetch(g, carry):
         for j in range(FETCH):
             unit = g * FETCH + j
             word = units_ref[unit]
-            base = field(word, 0, piece_bits) * (UNIT * passages) + field(word, piece_bits, pass_bits)
+            base = field(word, 0, piece_bits) * (pair * passages) + field(word, piece_bits, pass_bits)
             rows = rows_ref.at[pl.ds(pl.multiple_of(unit * UNIT, UNIT), UNIT)]
-            for t in range(UNIT):
-                rows[t : t + 1, :] = table_ref[pl.ds(codes_ref[base + t * passages], 1), :]
+            for t in range(pair):
+                codes = codes_ref[base + t * passages]
+                rows[t : t + 1, :] = table_ref[pl.ds(codes & 0xFFFF, 1), :]
+                rows[t + pair : t + pair + 1, :] = table_ref[pl.ds(lax.shift_right_logical(codes, 16), 1), :]
         return carry
 
     def compare(g, carry):
@@ -240,15 +248,17 @@
     hbm = pl.BlockSpec(memory_space=pltpu.HBM)
     copies = 1 if order else peers
     pack_mib = 2 * copies * rows * dim * 2 // MIB
-    held = [passage_codes.T.reshape(-1), passage_lengths]
+    held = [passage_codes.T, passage_lengths]
+    kept = [((seq // 2, residuals.shape[0]), jnp.int32), (passage_lengths.shape, jnp.int32)]
     inputs = [cand_owner, cand_local, queries, centroids] + held
     packed, *held = pl.pallas_call(
         pack_kernel,
         out_shape=[jax.ShapeDtypeStruct((copies, rows, dim), jnp.bfloat16)]
-        + [jax.ShapeDtypeStruct(x.shape, x.dtype) for x in held],
+        + [jax.ShapeDtypeStruct(*x) for x in kept],
         in_specs=[hbm] * 6,
         out_specs=[vmem] * 3,
         scratch_shapes=[
+            pltpu.VMEM(passage_codes.T.shape, jnp.int32),
             pltpu.SMEM((peers,), jnp.int32),
             pltpu.VMEM((peers + PAD, dim), jnp.float32),
             pltpu.SMEM(cand_owner.shape, jnp.int32),
@@ -259,7 +269,7 @@
         ],
         compiler_params=pltpu.CompilerParams(vmem_limit_bytes=(8 + pack_mib) * MIB),
     )(*(pltpu.with_memory_space_constraint(x, pltpu.HBM) for x in inputs))
-    codes, lengths = held
+    codes, lengths = held[0].reshape(-1), held[1]
     resid = pltpu.with_memory_space_constraint(residuals, pltpu.HBM)
     if order:
         swap = lambda x, t: lax.ppermute(x, "index", [(i, i ^ t) for i in range(peers)])
@@ -277,6 +287,13 @@
         parts = [lax.all_to_all(packed, "index", split_axis=0, concat_axis=0, tiled=True)]
         mine = parts[0][:, qrows : qrows + half]
         asked = parts[0][:, qrows + half]
+    asked = asked.astype(jnp.int32)
+    piece_bits, pass_bits, slot_bits = field_bits(peers, slots, residuals.shape[0], seq)
+    place = jnp.arange(peers, dtype=jnp.int32)[:, None] * slots + jnp.arange(dim // 2, dtype=jnp.int32)[None]
+    head = jnp.arange(peers, dtype=jnp.int32)[:, None] * q_dev + asked[:, dim // 2 :] // per_query
+    word = ((((head << slot_bits) + place) << pass_bits) + asked[:, : dim // 2]) << piece_bits
+    word = jnp.where(asked[:, : dim // 2] >= 0, word, -1)
+    asked = jnp.concatenate([word, asked[:, dim // 2 :]], axis=1)
     other = lax.ppermute(mine, "query", [(0, 1), (1, 0)])
     table_mib = 2 * peers * half * dim * 2 // MIB
     bests = (seq // UNIT) * (peers * slots + 8)
@@ -298,7 +315,7 @@
             pltpu.SemaphoreType.DMA((2,)),
         ],
         compiler_params=pltpu.CompilerParams(vmem_limit_bytes=(12 + 4 * table_mib + peers * slots * seq * dim * 4 // MIB) * MIB),
-    )(asked.astype(jnp.int32), lengths, codes, *parts, other, resid)
+    )(asked, lengths, codes, *parts, other, resid)
     back = lax.all_to_all(scores, "index", split_axis=0, concat_axis=0, tiled=True)
     result = jnp.sum(back[:, :, :per_query], axis=0)
     return result[:q_dev], result[q_dev:]

time: 36.5 us -> 36.1 us (0.989); the launches traced: 35.9 us -> 36.1 us
  blocking collectives: 13.8 us -> 14.2 us
    all_to_all x1, blocking collectives: 13.8 us -> 14.2 us  [body(): lax.all_to_all(scores, 'index', split_axis=0, concat_axis=0, tiled=True)]
  transfers between devices with their start and end apart: 8 -> 8, of which waited for: 5 -> 5; matrix products, arithmetic and copies ran while one was open for 0% -> 1% of each run, Pallas kernels for 0% -> 0%
where the time goes in v9:
time: 36.1 us
  blocking collectives  14.2 us (39%)
  starting transfers between devices  12.2 us (34%)
  waiting for transfers between devices  4.15 us (11%)
  Pallas kernels  3.92 us (11%)
  local copies, waits for them, and re-layouts  0.72 us (2%)
  between operations  0.71 us (2%)
    all_to_all x1, blocking collectives, body(): lax.all_to_all(scores, 'index', split_axis=0, concat_axis=0, tiled=True)  14.2 us
    ppermute x7, starting transfers between devices, body(): lax.ppermute(x, 'index', [(i, i ^ t) for i in range(peers)])  12.1 us
    pallas_call x1, Pallas kernels, body(): pl.pallas_call(functools.partial(score_kernel, slots, q_dev, per_query, q...  2.95 us
    ppermute x7, waiting for transfers between devices, body(): lax.ppermute(x, 'index', [(i, i ^ t) for i in range(peers)])  2.85 us
    ppermute x1, waiting for transfers between devices, body(): other = lax.ppermute(mine, 'query', [(0, 1), (1, 0)])  1.3 us
    pallas_call x1, Pallas kernels, body(): pl.pallas_call(pack_kernel, out_shape=[jax.ShapeDtypeStruct((copies, rows...  0.98 us
  transfers between devices with their start and end apart: 8, of which 5 were waited for; matrix products, arithmetic and copies ran while one was open for 1% of the time, Pallas kernels for 0%

profile of v9, /device:TPU:0, one launch (start us, length us, event | category | flops | bytes accessed | tf_op | source)
XLA Modules:
  0.0 36.1 jit_solution(12058442131807791699)
XLA Ops:
  0.6 1.0 %shard_map.86 = (bf16[1,272,128]{2,1,0:T(8,128)(2,1)S(1)}, s32[32,128]{1,0:T(8,128)S(1)}, s32[128]{0:T(128)S(1)}) custom-call(s32[4,8]{1,0:T(4,128)} %owner_hbm.1, s32[4,8]{1,0:T(4,128)} %local_hbm.1, bf16[4,32,128]{2,1,0:T(8,128)(2,1)} %queries_hbm.1, bf16[256,128]{1,0:T(8,128)(2,1)} %cent_hbm.1, s32[64,128]{1,0:T(8,128)} %bitcast.68, s32[128]{0:T(128)} %length_hbm.1), custom_call_target="tpu_custom_call" | custom-call | tf_op jit(solution)/shard_map/pallas_call | solution.py:254
  1.6 4.1 %collective-permute-start = (bf16[272,128]{1,0:T(8,128)(2,1)S(1)}, bf16[272,128]{1,0:T(8,128)(2,1)S(1)}, u32[]{:S(2)}, u32[]{:S(2)}) collective-permute-start(bf16[272,128]{1,0:T(8,128)(2,1)S(1)} %bitcast.60), channel_id=1, source_target_pairs={{0,8},{2,10},{4,12},{6,14},{8,0},{10,2},{12,4},{14,6},{1,9},{3,11}... | collective-permute-start | bytes 208904 | tf_op jit(solution)/shard_map/ppermute | solution.py:275
  5.7 1.3 %collective-permute-start.1 = (bf16[272,128]{1,0:T(8,128)(2,1)S(1)}, bf16[272,128]{1,0:T(8,128)(2,1)S(1)}, u32[]{:S(2)}, u32[]{:S(2)}) collective-permute-start(bf16[272,128]{1,0:T(8,128)(2,1)S(1)} %bitcast.61), channel_id=1, source_target_pairs={{0,12},{2,14},{4,8},{6,10},{8,4},{10,6},{12,0},{14,2},{1,13},{3,15... | collective-permute-start | bytes 208904 | tf_op jit(solution)/shard_map/ppermute | solution.py:275
  7.1 1.5 %collective-permute-start.2 = (bf16[272,128]{1,0:T(8,128)(2,1)S(1)}, bf16[272,128]{1,0:T(8,128)(2,1)S(1)}, u32[]{:S(2)}, u32[]{:S(2)}) collective-permute-start(bf16[272,128]{1,0:T(8,128)(2,1)S(1)} %bitcast.62), channel_id=1, source_target_pairs={{0,2},{2,0},{4,6},{6,4},{8,10},{10,8},{12,14},{14,12},{1,3},{3,1},... | collective-permute-start | bytes 208904 | tf_op jit(solution)/shard_map/ppermute | solution.py:275
  8.6 0.2 collective-permute-start.3
  8.8 1.8 %collective-permute-start.4 = (bf16[272,128]{1,0:T(8,128)(2,1)S(1)}, bf16[272,128]{1,0:T(8,128)(2,1)S(1)}, u32[]{:S(2)}, u32[]{:S(2)}) collective-permute-start(bf16[272,128]{1,0:T(8,128)(2,1)S(1)} %bitcast.64), channel_id=1, source_target_pairs={{0,4},{2,6},{4,0},{6,2},{8,12},{10,14},{12,8},{14,10},{1,5},{3,7},... | collective-permute-start | bytes 208904 | tf_op jit(solution)/shard_map/ppermute | solution.py:275
  10.6 0.0 collective-permute-done.refs_0_
  10.6 1.7 %collective-permute-start.5 = (bf16[272,128]{1,0:T(8,128)(2,1)S(1)}, bf16[272,128]{1,0:T(8,128)(2,1)S(1)}, u32[]{:S(2)}, u32[]{:S(2)}) collective-permute-start(bf16[272,128]{1,0:T(8,128)(2,1)S(1)} %collective-permute-done.refs_0_), channel_id=1, source_target_pairs={{0,2},{2,0},{4,6},{6,4},{8,10},{10,8},{12,14},{14,12},{1,3},{3,1},... | collective-permute-start | bytes 208904 | tf_op jit(solution)/shard_map/ppermute | solution.py:275
  12.3 0.1 collective-permute-done.1.refs_1_
  12.4 1.5 %collective-permute-start.6 = (bf16[272,128]{1,0:T(8,128)(2,1)S(1)}, bf16[272,128]{1,0:T(8,128)(2,1)S(1)}, u32[]{:S(2)}, u32[]{:S(2)}) collective-permute-start(bf16[272,128]{1,0:T(8,128)(2,1)S(1)} %collective-permute-done.1.refs_1_), channel_id=1, source_target_pairs={{0,2},{2,0},{4,6},{6,4},{8,10},{10,8},{12,14},{14,12},{1,3},{3,1},... | collective-permute-start | bytes 208904 | tf_op jit(solution)/shard_map/ppermute | solution.py:275
  13.9 0.0 collective-permute-done.2.refs_2_
  13.9 0.7 %collective-permute-done.3.refs_3_ = bf16[272,128]{1,0:T(8,128)(2,1)S(1)} collective-permute-done((bf16[272,128]{1,0:T(8,128)(2,1)S(1)}, bf16[272,128]{1,0:T(8,128)(2,1)S(1)}, u32[]{:S(2)}, u32[]{:S(2)}) %collective-permute-start.3) | collective-permute-done | bytes 69664 | tf_op jit(solution)/shard_map/ppermute | solution.py:275
  14.6 0.0 collective-permute-done.4.refs_4_
  14.7 0.6 %collective-permute-done.5.refs_5_ = bf16[272,128]{1,0:T(8,128)(2,1)S(1)} collective-permute-done((bf16[272,128]{1,0:T(8,128)(2,1)S(1)}, bf16[272,128]{1,0:T(8,128)(2,1)S(1)}, u32[]{:S(2)}, u32[]{:S(2)}) %collective-permute-start.5) | collective-permute-done | bytes 69664 | tf_op jit(solution)/shard_map/ppermute | solution.py:275
  15.3 1.5 %collective-permute-done.6.refs_6_ = bf16[272,128]{1,0:T(8,128)(2,1)S(1)} collective-permute-done((bf16[272,128]{1,0:T(8,128)(2,1)S(1)}, bf16[272,128]{1,0:T(8,128)(2,1)S(1)}, u32[]{:S(2)}, u32[]{:S(2)}) %collective-permute-start.6) | collective-permute-done | bytes 69664 | tf_op jit(solution)/shard_map/ppermute | solution.py:275
  16.7 0.1 collective-permute-start.7
  16.9 0.1 fusion.7
  17.0 0.1 pad_add_fusion.req_ref
  17.0 1.3 %collective-permute-done.7.refs_8_ = bf16[8,128,128]{2,1,0:T(8,128)(2,1)S(1)} collective-permute-done((bf16[8,128,128]{2,1,0:T(8,128)(2,1)S(1)}, bf16[8,128,128]{2,1,0:T(8,128)(2,1)S(1)}, u32[]{:S(2)}, u32[]{:S(2)}) %collective-permute-start.7) | collective-permute-done | bytes 262176 | tf_op jit(solution)/shard_map/ppermute | solution.py:297
  18.3 2.9 %shard_map.87 = f32[8,8,128]{2,1,0:T(8,128)S(1)} custom-call(s32[8,128]{1,0:T(8,128)S(1)} %pad_add_fusion.req_ref, s32[128]{0:T(128)S(1)} %get-tuple-element.6.length_ref, s32[4096]{0:T(1024)S(1)} %bitcast.66, bf16[272,128]{1,0:T(8,128)(2,1)S(1)} %collective-permute-done.refs_0_, bf16[272,128]{1,0:T(8,128)(2,1)S(1)} %collective-permute-done.1.refs_1_, ...), custom_call_target="tpu_custom_call" | custom-call | tf_op jit(solution)/shard_map/pallas_call | solution.py:300
  21.3 14.2 %all_to_all.5 = f32[8,8,128]{2,1,0:T(8,128)S(1)} all-to-all(f32[8,8,128]{2,1,0:T(8,128)S(1)} %shard_map.87), channel_id=1, replica_groups=mesh['group'=2,'index'=8,'query'=2] {'index'}, dimensions={0} | all-to-all | bytes 65536 | tf_op jit(solution)/shard_map/all_to_all | solution.py:319
  35.5 0.6 %fusion.9 = (f32[4,8]{1,0:T(4,128)}, f32[4,8]{1,0:T(4,128)}) fusion(f32[8,8]{1,0:T(8,128)S(1)} %slice_reduce_fusion), kind=kLoop, calls=%fused_computation.49 | loop fusion | bytes 512 | tf_op jit(solution)/shard_map/slice | solution.py:321
  (19 shorter events, 0.2 us)
Async XLA Ops:
  1.6 8.9 %collective-permute-start = (bf16[272,128]{1,0:T(8,128)(2,1)S(1)}, bf16[272,128]{1,0:T(8,128)(2,1)S(1)}, u32[]{:S(2)}, u32[]{:S(2)}) collective-permute-start(bf16[272,128]{1,0:T(8,128)(2,1)S(1)} %bitcast.60), channel_id=1, source_target_pairs={{0,8},{2,10},{4,12},{6,14},{8,0},{10,2},{12,4},{14,6},{1,9},{3,11}... | collective-permute-start | bytes 208904 | tf_op jit(solution)/shard_map/ppermute | solution.py:275
  5.7 6.7 %collective-permute-start.1 = (bf16[272,128]{1,0:T(8,128)(2,1)S(1)}, bf16[272,128]{1,0:T(8,128)(2,1)S(1)}, u32[]{:S(2)}, u32[]{:S(2)}) collective-permute-start(bf16[272,128]{1,0:T(8,128)(2,1)S(1)} %bitcast.61), channel_id=1, source_target_pairs={{0,12},{2,14},{4,8},{6,10},{8,4},{10,6},{12,0},{14,2},{1,13},{3,15... | collective-permute-start | bytes 208904 | tf_op jit(solution)/shard_map/ppermute | solution.py:275
  7.1 6.9 %collective-permute-start.2 = (bf16[272,128]{1,0:T(8,128)(2,1)S(1)}, bf16[272,128]{1,0:T(8,128)(2,1)S(1)}, u32[]{:S(2)}, u32[]{:S(2)}) collective-permute-start(bf16[272,128]{1,0:T(8,128)(2,1)S(1)} %bitcast.62), channel_id=1, source_target_pairs={{0,2},{2,0},{4,6},{6,4},{8,10},{10,8},{12,14},{14,12},{1,3},{3,1},... | collective-permute-start | bytes 208904 | tf_op jit(solution)/shard_map/ppermute | solution.py:275
  8.6 6.1 %collective-permute-start.3 = (bf16[272,128]{1,0:T(8,128)(2,1)S(1)}, bf16[272,128]{1,0:T(8,128)(2,1)S(1)}, u32[]{:S(2)}, u32[]{:S(2)}) collective-permute-start(bf16[272,128]{1,0:T(8,128)(2,1)S(1)} %bitcast.63), channel_id=1, source_target_pairs={{0,6},{2,4},{4,2},{6,0},{8,14},{10,12},{12,10},{14,8},{1,7},{3,5},... | collective-permute-start | bytes 208904 | tf_op jit(solution)/shard_map/ppermute | solution.py:275
  8.8 5.9 %collective-permute-start.4 = (bf16[272,128]{1,0:T(8,128)(2,1)S(1)}, bf16[272,128]{1,0:T(8,128)(2,1)S(1)}, u32[]{:S(2)}, u32[]{:S(2)}) collective-permute-start(bf16[272,128]{1,0:T(8,128)(2,1)S(1)} %bitcast.64), channel_id=1, source_target_pairs={{0,4},{2,6},{4,0},{6,2},{8,12},{10,14},{12,8},{14,10},{1,5},{3,7},... | collective-permute-start | bytes 208904 | tf_op jit(solution)/shard_map/ppermute | solution.py:275
  10.6 4.7 %collective-permute-start.5 = (bf16[272,128]{1,0:T(8,128)(2,1)S(1)}, bf16[272,128]{1,0:T(8,128)(2,1)S(1)}, u32[]{:S(2)}, u32[]{:S(2)}) collective-permute-start(bf16[272,128]{1,0:T(8,128)(2,1)S(1)} %collective-permute-done.refs_0_), channel_id=1, source_target_pairs={{0,2},{2,0},{4,6},{6,4},{8,10},{10,8},{12,14},{14,12},{1,3},{3,1},... | collective-permute-start | bytes 208904 | tf_op jit(solution)/shard_map/ppermute | solution.py:275
  12.4 4.3 %collective-permute-start.6 = (bf16[272,128]{1,0:T(8,128)(2,1)S(1)}, bf16[272,128]{1,0:T(8,128)(2,1)S(1)}, u32[]{:S(2)}, u32[]{:S(2)}) collective-permute-start(bf16[272,128]{1,0:T(8,128)(2,1)S(1)} %collective-permute-done.1.refs_1_), channel_id=1, source_target_pairs={{0,2},{2,0},{4,6},{6,4},{8,10},{10,8},{12,14},{14,12},{1,3},{3,1},... | collective-permute-start | bytes 208904 | tf_op jit(solution)/shard_map/ppermute | solution.py:275
  16.7 1.6 %collective-permute-start.7 = (bf16[8,128,128]{2,1,0:T(8,128)(2,1)S(1)}, bf16[8,128,128]{2,1,0:T(8,128)(2,1)S(1)}, u32[]{:S(2)}, u32[]{:S(2)}) collective-permute-start(bf16[8,128,128]{2,1,0:T(8,128)(2,1)S(1)} %constant_dynamic-update-slice_fusion.8), channel_id=1, source_target_pairs={{0,1},{1,0},{2,3},{3,2},{4,5},{5,4},{6,7},{7,6},{8,9},{9,8},{10,11... | collective-permute-start | bytes 786440 | tf_op jit(solution)/shard_map/ppermute | solution.py:297

commit v10 on v9

--- a/solution.py
+++ b/solution.py
@@ -105,9 +105,10 @@
     return (seq // UNIT - 1).bit_length(), (passages - 1).bit_length(), (peers * slots).bit_length()
 
 
-def score_kernel(slots, q_dev, per_query, qtok, order, req_ref, length_ref, codes_any, *refs):
-    (*parts, other_ref, resid_hbm, out_ref) = refs[:-10]
-    query_ref, table_ref, rows_ref, best_ref, near_ref, cand_ref, units_ref, codes_ref, resid_ref, sems = refs[-10:]
+def score_kernel(slots, q_dev, per_query, qtok, order, req_any, length_any, codes_any, *refs):
+    (*parts, other_ref, resid_hbm, out_ref) = refs[:-12]
+    query_ref, table_ref, rows_ref, best_ref, near_ref, cand_ref, units_ref = refs[-12:-5]
+    req_ref, length_ref, codes_ref, resid_ref, sems = refs[-5:]
     peers, half, dim = other_ref.shape
     qrows = q_dev * qtok
     passages, seq = resid_hbm.shape[:2]
@@ -117,10 +118,12 @@
     me = lax.axis_index("index")
     core = lax.axis_index("query")
 
-    bring_codes = pltpu.make_async_copy(codes_any, codes_ref, sems.at[0])
-    bring_codes.start()
-    bring_resid = pltpu.make_async_copy(resid_hbm, resid_ref, sems.at[1])
-    bring_resid.start()
+    bring_req = pltpu.make_async_copy(req_any, req_ref, sems.at[0])
+    bring_length = pltpu.make_async_copy(length_any, length_ref, sems.at[1])
+    bring_codes = pltpu.make_async_copy(codes_any, codes_ref, sems.at[2])
+    bring_resid = pltpu.make_async_copy(resid_hbm, resid_ref, sems.at[3])
+    for bring in (bring_req, bring_length, bring_codes, bring_resid):
+        bring.start()
     best_ref[...] = jnp.full(best_ref.shape, -1000000000.0, jnp.float32)
     near_ref[...] = jnp.full(near_ref.shape, -1000000000.0, jnp.float32)
 
@@ -142,10 +145,6 @@
                 n = n + jnp.where(length > u * UNIT, 1, 0)
         return n
 
-    count = lax.fori_loop(0, peers, listing, 0)
-    for u in range(GROUP):
-        units_ref[count + u] = total << slot_at
-
     def place(t, part, swapped):
         peer = me ^ order[t] if order else t
         first = pl.multiple_of(peer * shard + core * half, 8)
@@ -163,6 +162,12 @@
             place(t, parts[t], other_ref.at[t])
     else:
         lax.fori_loop(0, peers, place_loop, 0)
+
+    bring_req.wait()
+    bring_length.wait()
+    count = lax.fori_loop(0, peers, listing, 0)
+    for u in range(GROUP):
+        units_ref[count + u] = total << slot_at
 
     token = lax.broadcasted_iota(jnp.int32, (UNIT, qtok), 0)
     nt = (((1,), (1,)), ((), ()))
@@ -300,7 +305,7 @@
     scores = pl.pallas_call(
         functools.partial(score_kernel, slots, q_dev, per_query, qtok, order),
         out_shape=jax.ShapeDtypeStruct((peers, 2 * q_dev, dim), jnp.float32),
-        in_specs=[smem, smem, pl.BlockSpec(memory_space=pl.ANY)] + [vmem] * (len(parts) + 1) + [hbm],
+        in_specs=[pl.BlockSpec(memory_space=pl.ANY)] * 3 + [vmem] * (len(parts) + 1) + [hbm],
         out_specs=vmem,
         scratch_shapes=[
             pltpu.VMEM((peers * qrows, dim), jnp.bfloat16),
@@ -310,9 +315,11 @@
             pltpu.VMEM((bests, qtok), jnp.float32),
             pltpu.VMEM((peers * slots, dim), jnp.int32),
             pltpu.SMEM((peers * slots * (seq // UNIT) + GROUP,), jnp.int32),
+            pltpu.SMEM(asked.shape, jnp.int32),
+            pltpu.SMEM(lengths.shape, jnp.int32),
             pltpu.SMEM(codes.shape, jnp.int32),
             pltpu.VMEM(residuals.shape, residuals.dtype),
-            pltpu.SemaphoreType.DMA((2,)),
+            pltpu.SemaphoreType.DMA((4,)),
         ],
         compiler_params=pltpu.CompilerParams(vmem_limit_bytes=(12 + 4 * table_mib + peers * slots * seq * dim * 4 // MIB) * MIB),
     )(asked, lengths, codes, *parts, other, resid)

time: 36.1 us -> 35.2 us (0.975); the launches traced: 36.1 us -> 34.7 us
  blocking collectives: 14.2 us -> 11.2 us
  Pallas kernels: 3.92 us -> 5.56 us
    all_to_all x1, blocking collectives: 14.2 us -> 11.2 us  [body(): lax.all_to_all(scores, 'index', split_axis=0, concat_axis=0, tiled=True)]
    pallas_call x1, Pallas kernels: 2.95 us -> 4.58 us  [body(): pl.pallas_call(functools.partial(score_kernel, slots, q_dev, per_query, q...]
where the time goes in v10:
time: 35.2 us; the launch traced here: 34.7 us
  starting transfers between devices  12.2 us (35%)
  blocking collectives  11.2 us (32%)
  Pallas kernels  5.56 us (16%)
  waiting for transfers between devices  4.15 us (12%)
  local copies, waits for them, and re-layouts  0.72 us (2%)
  between operations  0.71 us (2%)
    ppermute x7, starting transfers between devices, body(): lax.ppermute(x, 'index', [(i, i ^ t) for i in range(peers)])  12.1 us
    all_to_all x1, blocking collectives, body(): lax.all_to_all(scores, 'index', split_axis=0, concat_axis=0, tiled=True)  11.2 us
    pallas_call x1, Pallas kernels, body(): pl.pallas_call(functools.partial(score_kernel, slots, q_dev, per_query, q...  4.58 us
    ppermute x7, waiting for transfers between devices, body(): lax.ppermute(x, 'index', [(i, i ^ t) for i in range(peers)])  2.85 us
    ppermute x1, waiting for transfers between devices, body(): other = lax.ppermute(mine, 'query', [(0, 1), (1, 0)])  1.3 us
    pallas_call x1, Pallas kernels, body(): pl.pallas_call(pack_kernel, out_shape=[jax.ShapeDtypeStruct((copies, rows...  0.98 us
  transfers between devices with their start and end apart: 8, of which 5 were waited for; matrix products, arithmetic and copies ran while one was open for 1% of the time, Pallas kernels for 0%

profile of v10, /device:TPU:0, one launch (start us, length us, event | category | flops | bytes accessed | tf_op | source)
XLA Modules:
  0.0 34.7 jit_solution(16247171435381690989)
XLA Ops:
  0.6 1.0 %shard_map.86 = (bf16[1,272,128]{2,1,0:T(8,128)(2,1)S(1)}, s32[32,128]{1,0:T(8,128)S(1)}, s32[128]{0:T(128)S(1)}) custom-call(s32[4,8]{1,0:T(4,128)} %owner_hbm.1, s32[4,8]{1,0:T(4,128)} %local_hbm.1, bf16[4,32,128]{2,1,0:T(8,128)(2,1)} %queries_hbm.1, bf16[256,128]{1,0:T(8,128)(2,1)} %cent_hbm.1, s32[64,128]{1,0:T(8,128)} %bitcast.68, s32[128]{0:T(128)} %length_hbm.1), custom_call_target="tpu_custom_call" | custom-call | tf_op jit(solution)/shard_map/pallas_call | solution.py:259
  1.6 4.1 %collective-permute-start = (bf16[272,128]{1,0:T(8,128)(2,1)S(1)}, bf16[272,128]{1,0:T(8,128)(2,1)S(1)}, u32[]{:S(2)}, u32[]{:S(2)}) collective-permute-start(bf16[272,128]{1,0:T(8,128)(2,1)S(1)} %bitcast.60), channel_id=1, source_target_pairs={{0,8},{2,10},{4,12},{6,14},{8,0},{10,2},{12,4},{14,6},{1,9},{3,11}... | collective-permute-start | bytes 208904 | tf_op jit(solution)/shard_map/ppermute | solution.py:280
  5.7 1.3 %collective-permute-start.1 = (bf16[272,128]{1,0:T(8,128)(2,1)S(1)}, bf16[272,128]{1,0:T(8,128)(2,1)S(1)}, u32[]{:S(2)}, u32[]{:S(2)}) collective-permute-start(bf16[272,128]{1,0:T(8,128)(2,1)S(1)} %bitcast.61), channel_id=1, source_target_pairs={{0,12},{2,14},{4,8},{6,10},{8,4},{10,6},{12,0},{14,2},{1,13},{3,15... | collective-permute-start | bytes 208904 | tf_op jit(solution)/shard_map/ppermute | solution.py:280
  7.1 1.5 %collective-permute-start.2 = (bf16[272,128]{1,0:T(8,128)(2,1)S(1)}, bf16[272,128]{1,0:T(8,128)(2,1)S(1)}, u32[]{:S(2)}, u32[]{:S(2)}) collective-permute-start(bf16[272,128]{1,0:T(8,128)(2,1)S(1)} %bitcast.62), channel_id=1, source_target_pairs={{0,2},{2,0},{4,6},{6,4},{8,10},{10,8},{12,14},{14,12},{1,3},{3,1},... | collective-permute-start | bytes 208904 | tf_op jit(solution)/shard_map/ppermute | solution.py:280
  8.6 0.2 collective-permute-start.3
  8.8 1.8 %collective-permute-start.4 = (bf16[272,128]{1,0:T(8,128)(2,1)S(1)}, bf16[272,128]{1,0:T(8,128)(2,1)S(1)}, u32[]{:S(2)}, u32[]{:S(2)}) collective-permute-start(bf16[272,128]{1,0:T(8,128)(2,1)S(1)} %bitcast.64), channel_id=1, source_target_pairs={{0,4},{2,6},{4,0},{6,2},{8,12},{10,14},{12,8},{14,10},{1,5},{3,7},... | collective-permute-start | bytes 208904 | tf_op jit(solution)/shard_map/ppermute | solution.py:280
  10.6 0.0 collective-permute-done.refs_0_
  10.6 1.7 %collective-permute-start.5 = (bf16[272,128]{1,0:T(8,128)(2,1)S(1)}, bf16[272,128]{1,0:T(8,128)(2,1)S(1)}, u32[]{:S(2)}, u32[]{:S(2)}) collective-permute-start(bf16[272,128]{1,0:T(8,128)(2,1)S(1)} %collective-permute-done.refs_0_), channel_id=1, source_target_pairs={{0,2},{2,0},{4,6},{6,4},{8,10},{10,8},{12,14},{14,12},{1,3},{3,1},... | collective-permute-start | bytes 208904 | tf_op jit(solution)/shard_map/ppermute | solution.py:280
  12.3 0.1 collective-permute-done.1.refs_1_
  12.4 1.5 %collective-permute-start.6 = (bf16[272,128]{1,0:T(8,128)(2,1)S(1)}, bf16[272,128]{1,0:T(8,128)(2,1)S(1)}, u32[]{:S(2)}, u32[]{:S(2)}) collective-permute-start(bf16[272,128]{1,0:T(8,128)(2,1)S(1)} %collective-permute-done.1.refs_1_), channel_id=1, source_target_pairs={{0,2},{2,0},{4,6},{6,4},{8,10},{10,8},{12,14},{14,12},{1,3},{3,1},... | collective-permute-start | bytes 208904 | tf_op jit(solution)/shard_map/ppermute | solution.py:280
  13.9 0.0 collective-permute-done.2.refs_2_
  13.9 0.7 %collective-permute-done.3.refs_3_ = bf16[272,128]{1,0:T(8,128)(2,1)S(1)} collective-permute-done((bf16[272,128]{1,0:T(8,128)(2,1)S(1)}, bf16[272,128]{1,0:T(8,128)(2,1)S(1)}, u32[]{:S(2)}, u32[]{:S(2)}) %collective-permute-start.3) | collective-permute-done | bytes 69664 | tf_op jit(solution)/shard_map/ppermute | solution.py:280
  14.6 0.0 collective-permute-done.4.refs_4_
  14.7 0.6 %collective-permute-done.5.refs_5_ = bf16[272,128]{1,0:T(8,128)(2,1)S(1)} collective-permute-done((bf16[272,128]{1,0:T(8,128)(2,1)S(1)}, bf16[272,128]{1,0:T(8,128)(2,1)S(1)}, u32[]{:S(2)}, u32[]{:S(2)}) %collective-permute-start.5) | collective-permute-done | bytes 69664 | tf_op jit(solution)/shard_map/ppermute | solution.py:280
  15.3 1.5 %collective-permute-done.6.refs_6_ = bf16[272,128]{1,0:T(8,128)(2,1)S(1)} collective-permute-done((bf16[272,128]{1,0:T(8,128)(2,1)S(1)}, bf16[272,128]{1,0:T(8,128)(2,1)S(1)}, u32[]{:S(2)}, u32[]{:S(2)}) %collective-permute-start.6) | collective-permute-done | bytes 69664 | tf_op jit(solution)/shard_map/ppermute | solution.py:280
  16.7 0.1 collective-permute-start.7
  16.9 0.1 fusion.7
  17.0 0.1 pad_add_fusion.req_any
  17.0 1.3 %collective-permute-done.7.refs_8_ = bf16[8,128,128]{2,1,0:T(8,128)(2,1)S(1)} collective-permute-done((bf16[8,128,128]{2,1,0:T(8,128)(2,1)S(1)}, bf16[8,128,128]{2,1,0:T(8,128)(2,1)S(1)}, u32[]{:S(2)}, u32[]{:S(2)}) %collective-permute-start.7) | collective-permute-done | bytes 262176 | tf_op jit(solution)/shard_map/ppermute | solution.py:302
  18.3 4.6 %shard_map.87 = f32[8,8,128]{2,1,0:T(8,128)S(1)} custom-call(s32[8,128]{1,0:T(8,128)S(1)} %pad_add_fusion.req_any, s32[128]{0:T(128)S(1)} %get-tuple-element.6.length_any, s32[4096]{0:T(1024)S(1)} %bitcast.66, bf16[272,128]{1,0:T(8,128)(2,1)S(1)} %collective-permute-done.refs_0_, bf16[272,128]{1,0:T(8,128)(2,1)S(1)} %collective-permute-done.1.refs_1_, ...), custom_call_target="tpu_custom_call" | custom-call | tf_op jit(solution)/shard_map/pallas_call | solution.py:305
  22.9 11.2 %all_to_all.5 = f32[8,8,128]{2,1,0:T(8,128)S(1)} all-to-all(f32[8,8,128]{2,1,0:T(8,128)S(1)} %shard_map.87), channel_id=1, replica_groups=mesh['group'=2,'index'=8,'query'=2] {'index'}, dimensions={0} | all-to-all | bytes 65536 | tf_op jit(solution)/shard_map/all_to_all | solution.py:326
  34.1 0.6 %fusion.9 = (f32[4,8]{1,0:T(4,128)}, f32[4,8]{1,0:T(4,128)}) fusion(f32[8,8]{1,0:T(8,128)S(1)} %slice_reduce_fusion), kind=kLoop, calls=%fused_computation.49 | loop fusion | bytes 512 | tf_op jit(solution)/shard_map/slice | solution.py:328
  (19 shorter events, 0.2 us)
Async XLA Ops:
  1.6 8.9 %collective-permute-start = (bf16[272,128]{1,0:T(8,128)(2,1)S(1)}, bf16[272,128]{1,0:T(8,128)(2,1)S(1)}, u32[]{:S(2)}, u32[]{:S(2)}) collective-permute-start(bf16[272,128]{1,0:T(8,128)(2,1)S(1)} %bitcast.60), channel_id=1, source_target_pairs={{0,8},{2,10},{4,12},{6,14},{8,0},{10,2},{12,4},{14,6},{1,9},{3,11}... | collective-permute-start | bytes 208904 | tf_op jit(solution)/shard_map/ppermute | solution.py:280
  5.7 6.7 %collective-permute-start.1 = (bf16[272,128]{1,0:T(8,128)(2,1)S(1)}, bf16[272,128]{1,0:T(8,128)(2,1)S(1)}, u32[]{:S(2)}, u32[]{:S(2)}) collective-permute-start(bf16[272,128]{1,0:T(8,128)(2,1)S(1)} %bitcast.61), channel_id=1, source_target_pairs={{0,12},{2,14},{4,8},{6,10},{8,4},{10,6},{12,0},{14,2},{1,13},{3,15... | collective-permute-start | bytes 208904 | tf_op jit(solution)/shard_map/ppermute | solution.py:280
  7.1 6.9 %collective-permute-start.2 = (bf16[272,128]{1,0:T(8,128)(2,1)S(1)}, bf16[272,128]{1,0:T(8,128)(2,1)S(1)}, u32[]{:S(2)}, u32[]{:S(2)}) collective-permute-start(bf16[272,128]{1,0:T(8,128)(2,1)S(1)} %bitcast.62), channel_id=1, source_target_pairs={{0,2},{2,0},{4,6},{6,4},{8,10},{10,8},{12,14},{14,12},{1,3},{3,1},... | collective-permute-start | bytes 208904 | tf_op jit(solution)/shard_map/ppermute | solution.py:280
  8.6 6.1 %collective-permute-start.3 = (bf16[272,128]{1,0:T(8,128)(2,1)S(1)}, bf16[272,128]{1,0:T(8,128)(2,1)S(1)}, u32[]{:S(2)}, u32[]{:S(2)}) collective-permute-start(bf16[272,128]{1,0:T(8,128)(2,1)S(1)} %bitcast.63), channel_id=1, source_target_pairs={{0,6},{2,4},{4,2},{6,0},{8,14},{10,12},{12,10},{14,8},{1,7},{3,5},... | collective-permute-start | bytes 208904 | tf_op jit(solution)/shard_map/ppermute | solution.py:280
  8.8 5.9 %collective-permute-start.4 = (bf16[272,128]{1,0:T(8,128)(2,1)S(1)}, bf16[272,128]{1,0:T(8,128)(2,1)S(1)}, u32[]{:S(2)}, u32[]{:S(2)}) collective-permute-start(bf16[272,128]{1,0:T(8,128)(2,1)S(1)} %bitcast.64), channel_id=1, source_target_pairs={{0,4},{2,6},{4,0},{6,2},{8,12},{10,14},{12,8},{14,10},{1,5},{3,7},... | collective-permute-start | bytes 208904 | tf_op jit(solution)/shard_map/ppermute | solution.py:280
  10.6 4.7 %collective-permute-start.5 = (bf16[272,128]{1,0:T(8,128)(2,1)S(1)}, bf16[272,128]{1,0:T(8,128)(2,1)S(1)}, u32[]{:S(2)}, u32[]{:S(2)}) collective-permute-start(bf16[272,128]{1,0:T(8,128)(2,1)S(1)} %collective-permute-done.refs_0_), channel_id=1, source_target_pairs={{0,2},{2,0},{4,6},{6,4},{8,10},{10,8},{12,14},{14,12},{1,3},{3,1},... | collective-permute-start | bytes 208904 | tf_op jit(solution)/shard_map/ppermute | solution.py:280
  12.4 4.3 %collective-permute-start.6 = (bf16[272,128]{1,0:T(8,128)(2,1)S(1)}, bf16[272,128]{1,0:T(8,128)(2,1)S(1)}, u32[]{:S(2)}, u32[]{:S(2)}) collective-permute-start(bf16[272,128]{1,0:T(8,128)(2,1)S(1)} %collective-permute-done.1.refs_1_), channel_id=1, source_target_pairs={{0,2},{2,0},{4,6},{6,4},{8,10},{10,8},{12,14},{14,12},{1,3},{3,1},... | collective-permute-start | bytes 208904 | tf_op jit(solution)/shard_map/ppermute | solution.py:280
  16.7 1.6 %collective-permute-start.7 = (bf16[8,128,128]{2,1,0:T(8,128)(2,1)S(1)}, bf16[8,128,128]{2,1,0:T(8,128)(2,1)S(1)}, u32[]{:S(2)}, u32[]{:S(2)}) collective-permute-start(bf16[8,128,128]{2,1,0:T(8,128)(2,1)S(1)} %constant_dynamic-update-slice_fusion.8), channel_id=1, source_target_pairs={{0,1},{1,0},{2,3},{3,2},{4,5},{5,4},{6,7},{7,6},{8,9},{9,8},{10,11... | collective-permute-start | bytes 786440 | tf_op jit(solution)/shard_map/ppermute | solution.py:302

commit v11 on v10

--- a/solution.py
+++ b/solution.py
@@ -165,7 +165,7 @@
 
     bring_req.wait()
     bring_length.wait()
-    count = lax.fori_loop(0, peers, listing, 0)
+    count = lax.fori_loop(0, peers, listing, 0, unroll=peers <= PAD)
     for u in range(GROUP):
         units_ref[count + u] = total << slot_at
 

time: 35.2 us -> 35.6 us (1.011); the launches traced: 34.7 us -> 35.4 us
  blocking collectives: 11.2 us -> 11.8 us
    all_to_all x1, blocking collectives: 11.2 us -> 11.8 us  [body(): lax.all_to_all(scores, 'index', split_axis=0, concat_axis=0, tiled=True)]
where the time goes in v11:
time: 35.6 us; the launch traced here: 35.4 us
  starting transfers between devices  12.2 us (34%)
  blocking collectives  11.8 us (33%)
  Pallas kernels  5.69 us (16%)
  waiting for transfers between devices  4.15 us (12%)
  local copies, waits for them, and re-layouts  0.72 us (2%)
  between operations  0.71 us (2%)
    ppermute x7, starting transfers between devices, body(): lax.ppermute(x, 'index', [(i, i ^ t) for i in range(peers)])  12.1 us
    all_to_all x1, blocking collectives, body(): lax.all_to_all(scores, 'index', split_axis=0, concat_axis=0, tiled=True)  11.8 us
    pallas_call x1, Pallas kernels, body(): pl.pallas_call(functools.partial(score_kernel, slots, q_dev, per_query, q...  4.72 us
    ppermute x7, waiting for transfers between devices, body(): lax.ppermute(x, 'index', [(i, i ^ t) for i in range(peers)])  2.85 us
    ppermute x1, waiting for transfers between devices, body(): other = lax.ppermute(mine, 'query', [(0, 1), (1, 0)])  1.3 us
    pallas_call x1, Pallas kernels, body(): pl.pallas_call(pack_kernel, out_shape=[jax.ShapeDtypeStruct((copies, rows...  0.98 us
  transfers between devices with their start and end apart: 8, of which 5 were waited for; matrix products, arithmetic and copies ran while one was open for 1% of the time, Pallas kernels for 0%

profile of v11, /device:TPU:0, one launch (start us, length us, event | category | flops | bytes accessed | tf_op | source)
XLA Modules:
  0.0 35.4 jit_solution(11004519466200209113)
XLA Ops:
  0.6 1.0 %shard_map.86 = (bf16[1,272,128]{2,1,0:T(8,128)(2,1)S(1)}, s32[32,128]{1,0:T(8,128)S(1)}, s32[128]{0:T(128)S(1)}) custom-call(s32[4,8]{1,0:T(4,128)} %owner_hbm.1, s32[4,8]{1,0:T(4,128)} %local_hbm.1, bf16[4,32,128]{2,1,0:T(8,128)(2,1)} %queries_hbm.1, bf16[256,128]{1,0:T(8,128)(2,1)} %cent_hbm.1, s32[64,128]{1,0:T(8,128)} %bitcast.68, s32[128]{0:T(128)} %length_hbm.1), custom_call_target="tpu_custom_call" | custom-call | tf_op jit(solution)/shard_map/pallas_call | solution.py:259
  1.6 4.1 %collective-permute-start = (bf16[272,128]{1,0:T(8,128)(2,1)S(1)}, bf16[272,128]{1,0:T(8,128)(2,1)S(1)}, u32[]{:S(2)}, u32[]{:S(2)}) collective-permute-start(bf16[272,128]{1,0:T(8,128)(2,1)S(1)} %bitcast.60), channel_id=1, source_target_pairs={{0,8},{2,10},{4,12},{6,14},{8,0},{10,2},{12,4},{14,6},{1,9},{3,11}... | collective-permute-start | bytes 208904 | tf_op jit(solution)/shard_map/ppermute | solution.py:280
  5.7 1.3 %collective-permute-start.1 = (bf16[272,128]{1,0:T(8,128)(2,1)S(1)}, bf16[272,128]{1,0:T(8,128)(2,1)S(1)}, u32[]{:S(2)}, u32[]{:S(2)}) collective-permute-start(bf16[272,128]{1,0:T(8,128)(2,1)S(1)} %bitcast.61), channel_id=1, source_target_pairs={{0,12},{2,14},{4,8},{6,10},{8,4},{10,6},{12,0},{14,2},{1,13},{3,15... | collective-permute-start | bytes 208904 | tf_op jit(solution)/shard_map/ppermute | solution.py:280
  7.1 1.5 %collective-permute-start.2 = (bf16[272,128]{1,0:T(8,128)(2,1)S(1)}, bf16[272,128]{1,0:T(8,128)(2,1)S(1)}, u32[]{:S(2)}, u32[]{:S(2)}) collective-permute-start(bf16[272,128]{1,0:T(8,128)(2,1)S(1)} %bitcast.62), channel_id=1, source_target_pairs={{0,2},{2,0},{4,6},{6,4},{8,10},{10,8},{12,14},{14,12},{1,3},{3,1},... | collective-permute-start | bytes 208904 | tf_op jit(solution)/shard_map/ppermute | solution.py:280
  8.6 0.2 collective-permute-start.3
  8.8 1.8 %collective-permute-start.4 = (bf16[272,128]{1,0:T(8,128)(2,1)S(1)}, bf16[272,128]{1,0:T(8,128)(2,1)S(1)}, u32[]{:S(2)}, u32[]{:S(2)}) collective-permute-start(bf16[272,128]{1,0:T(8,128)(2,1)S(1)} %bitcast.64), channel_id=1, source_target_pairs={{0,4},{2,6},{4,0},{6,2},{8,12},{10,14},{12,8},{14,10},{1,5},{3,7},... | collective-permute-start | bytes 208904 | tf_op jit(solution)/shard_map/ppermute | solution.py:280
  10.6 0.0 collective-permute-done.refs_0_
  10.6 1.7 %collective-permute-start.5 = (bf16[272,128]{1,0:T(8,128)(2,1)S(1)}, bf16[272,128]{1,0:T(8,128)(2,1)S(1)}, u32[]{:S(2)}, u32[]{:S(2)}) collective-permute-start(bf16[272,128]{1,0:T(8,128)(2,1)S(1)} %collective-permute-done.refs_0_), channel_id=1, source_target_pairs={{0,2},{2,0},{4,6},{6,4},{8,10},{10,8},{12,14},{14,12},{1,3},{3,1},... | collective-permute-start | bytes 208904 | tf_op jit(solution)/shard_map/ppermute | solution.py:280
  12.3 0.1 collective-permute-done.1.refs_1_
  12.4 1.5 %collective-permute-start.6 = (bf16[272,128]{1,0:T(8,128)(2,1)S(1)}, bf16[272,128]{1,0:T(8,128)(2,1)S(1)}, u32[]{:S(2)}, u32[]{:S(2)}) collective-permute-start(bf16[272,128]{1,0:T(8,128)(2,1)S(1)} %collective-permute-done.1.refs_1_), channel_id=1, source_target_pairs={{0,2},{2,0},{4,6},{6,4},{8,10},{10,8},{12,14},{14,12},{1,3},{3,1},... | collective-permute-start | bytes 208904 | tf_op jit(solution)/shard_map/ppermute | solution.py:280
  13.9 0.0 collective-permute-done.2.refs_2_
  13.9 0.7 %collective-permute-done.3.refs_3_ = bf16[272,128]{1,0:T(8,128)(2,1)S(1)} collective-permute-done((bf16[272,128]{1,0:T(8,128)(2,1)S(1)}, bf16[272,128]{1,0:T(8,128)(2,1)S(1)}, u32[]{:S(2)}, u32[]{:S(2)}) %collective-permute-start.3) | collective-permute-done | bytes 69664 | tf_op jit(solution)/shard_map/ppermute | solution.py:280
  14.6 0.0 collective-permute-done.4.refs_4_
  14.7 0.6 %collective-permute-done.5.refs_5_ = bf16[272,128]{1,0:T(8,128)(2,1)S(1)} collective-permute-done((bf16[272,128]{1,0:T(8,128)(2,1)S(1)}, bf16[272,128]{1,0:T(8,128)(2,1)S(1)}, u32[]{:S(2)}, u32[]{:S(2)}) %collective-permute-start.5) | collective-permute-done | bytes 69664 | tf_op jit(solution)/shard_map/ppermute | solution.py:280
  15.3 1.5 %collective-permute-done.6.refs_6_ = bf16[272,128]{1,0:T(8,128)(2,1)S(1)} collective-permute-done((bf16[272,128]{1,0:T(8,128)(2,1)S(1)}, bf16[272,128]{1,0:T(8,128)(2,1)S(1)}, u32[]{:S(2)}, u32[]{:S(2)}) %collective-permute-start.6) | collective-permute-done | bytes 69664 | tf_op jit(solution)/shard_map/ppermute | solution.py:280
  16.7 0.1 collective-permute-start.7
  16.9 0.1 fusion.7
  17.0 0.1 pad_add_fusion.req_any
  17.0 1.3 %collective-permute-done.7.refs_8_ = bf16[8,128,128]{2,1,0:T(8,128)(2,1)S(1)} collective-permute-done((bf16[8,128,128]{2,1,0:T(8,128)(2,1)S(1)}, bf16[8,128,128]{2,1,0:T(8,128)(2,1)S(1)}, u32[]{:S(2)}, u32[]{:S(2)}) %collective-permute-start.7) | collective-permute-done | bytes 262176 | tf_op jit(solution)/shard_map/ppermute | solution.py:302
  18.3 4.7 %shard_map.87 = f32[8,8,128]{2,1,0:T(8,128)S(1)} custom-call(s32[8,128]{1,0:T(8,128)S(1)} %pad_add_fusion.req_any, s32[128]{0:T(128)S(1)} %get-tuple-element.6.length_any, s32[4096]{0:T(1024)S(1)} %bitcast.66, bf16[272,128]{1,0:T(8,128)(2,1)S(1)} %collective-permute-done.refs_0_, bf16[272,128]{1,0:T(8,128)(2,1)S(1)} %collective-permute-done.1.refs_1_, ...), custom_call_target="tpu_custom_call" | custom-call | tf_op jit(solution)/shard_map/pallas_call | solution.py:305
  23.1 11.8 %all_to_all.5 = f32[8,8,128]{2,1,0:T(8,128)S(1)} all-to-all(f32[8,8,128]{2,1,0:T(8,128)S(1)} %shard_map.87), channel_id=1, replica_groups=mesh['group'=2,'index'=8,'query'=2] {'index'}, dimensions={0} | all-to-all | bytes 65536 | tf_op jit(solution)/shard_map/all_to_all | solution.py:326
  34.9 0.6 %fusion.9 = (f32[4,8]{1,0:T(4,128)}, f32[4,8]{1,0:T(4,128)}) fusion(f32[8,8]{1,0:T(8,128)S(1)} %slice_reduce_fusion), kind=kLoop, calls=%fused_computation.49 | loop fusion | bytes 512 | tf_op jit(solution)/shard_map/slice | solution.py:328
  (19 shorter events, 0.2 us)
Async XLA Ops:
  1.6 8.9 %collective-permute-start = (bf16[272,128]{1,0:T(8,128)(2,1)S(1)}, bf16[272,128]{1,0:T(8,128)(2,1)S(1)}, u32[]{:S(2)}, u32[]{:S(2)}) collective-permute-start(bf16[272,128]{1,0:T(8,128)(2,1)S(1)} %bitcast.60), channel_id=1, source_target_pairs={{0,8},{2,10},{4,12},{6,14},{8,0},{10,2},{12,4},{14,6},{1,9},{3,11}... | collective-permute-start | bytes 208904 | tf_op jit(solution)/shard_map/ppermute | solution.py:280
  5.7 6.7 %collective-permute-start.1 = (bf16[272,128]{1,0:T(8,128)(2,1)S(1)}, bf16[272,128]{1,0:T(8,128)(2,1)S(1)}, u32[]{:S(2)}, u32[]{:S(2)}) collective-permute-start(bf16[272,128]{1,0:T(8,128)(2,1)S(1)} %bitcast.61), channel_id=1, source_target_pairs={{0,12},{2,14},{4,8},{6,10},{8,4},{10,6},{12,0},{14,2},{1,13},{3,15... | collective-permute-start | bytes 208904 | tf_op jit(solution)/shard_map/ppermute | solution.py:280
  7.1 6.9 %collective-permute-start.2 = (bf16[272,128]{1,0:T(8,128)(2,1)S(1)}, bf16[272,128]{1,0:T(8,128)(2,1)S(1)}, u32[]{:S(2)}, u32[]{:S(2)}) collective-permute-start(bf16[272,128]{1,0:T(8,128)(2,1)S(1)} %bitcast.62), channel_id=1, source_target_pairs={{0,2},{2,0},{4,6},{6,4},{8,10},{10,8},{12,14},{14,12},{1,3},{3,1},... | collective-permute-start | bytes 208904 | tf_op jit(solution)/shard_map/ppermute | solution.py:280
  8.6 6.1 %collective-permute-start.3 = (bf16[272,128]{1,0:T(8,128)(2,1)S(1)}, bf16[272,128]{1,0:T(8,128)(2,1)S(1)}, u32[]{:S(2)}, u32[]{:S(2)}) collective-permute-start(bf16[272,128]{1,0:T(8,128)(2,1)S(1)} %bitcast.63), channel_id=1, source_target_pairs={{0,6},{2,4},{4,2},{6,0},{8,14},{10,12},{12,10},{14,8},{1,7},{3,5},... | collective-permute-start | bytes 208904 | tf_op jit(solution)/shard_map/ppermute | solution.py:280
  8.8 5.9 %collective-permute-start.4 = (bf16[272,128]{1,0:T(8,128)(2,1)S(1)}, bf16[272,128]{1,0:T(8,128)(2,1)S(1)}, u32[]{:S(2)}, u32[]{:S(2)}) collective-permute-start(bf16[272,128]{1,0:T(8,128)(2,1)S(1)} %bitcast.64), channel_id=1, source_target_pairs={{0,4},{2,6},{4,0},{6,2},{8,12},{10,14},{12,8},{14,10},{1,5},{3,7},... | collective-permute-start | bytes 208904 | tf_op jit(solution)/shard_map/ppermute | solution.py:280
  10.6 4.7 %collective-permute-start.5 = (bf16[272,128]{1,0:T(8,128)(2,1)S(1)}, bf16[272,128]{1,0:T(8,128)(2,1)S(1)}, u32[]{:S(2)}, u32[]{:S(2)}) collective-permute-start(bf16[272,128]{1,0:T(8,128)(2,1)S(1)} %collective-permute-done.refs_0_), channel_id=1, source_target_pairs={{0,2},{2,0},{4,6},{6,4},{8,10},{10,8},{12,14},{14,12},{1,3},{3,1},... | collective-permute-start | bytes 208904 | tf_op jit(solution)/shard_map/ppermute | solution.py:280
  12.4 4.3 %collective-permute-start.6 = (bf16[272,128]{1,0:T(8,128)(2,1)S(1)}, bf16[272,128]{1,0:T(8,128)(2,1)S(1)}, u32[]{:S(2)}, u32[]{:S(2)}) collective-permute-start(bf16[272,128]{1,0:T(8,128)(2,1)S(1)} %collective-permute-done.1.refs_1_), channel_id=1, source_target_pairs={{0,2},{2,0},{4,6},{6,4},{8,10},{10,8},{12,14},{14,12},{1,3},{3,1},... | collective-permute-start | bytes 208904 | tf_op jit(solution)/shard_map/ppermute | solution.py:280
  16.7 1.6 %collective-permute-start.7 = (bf16[8,128,128]{2,1,0:T(8,128)(2,1)S(1)}, bf16[8,128,128]{2,1,0:T(8,128)(2,1)S(1)}, u32[]{:S(2)}, u32[]{:S(2)}) collective-permute-start(bf16[8,128,128]{2,1,0:T(8,128)(2,1)S(1)} %constant_dynamic-update-slice_fusion.8), channel_id=1, source_target_pairs={{0,1},{1,0},{2,3},{3,2},{4,5},{5,4},{6,7},{7,6},{8,9},{9,8},{10,11... | collective-permute-start | bytes 786440 | tf_op jit(solution)/shard_map/ppermute | solution.py:302

commit v12 on v10

--- a/solution.py
+++ b/solution.py
@@ -11,7 +11,7 @@
 PAD = 16
 UNIT = 32
 GROUP = 32
-ORDER = (4, 6, 1, 3, 2, 5, 7, 0)
+ORDER = (4, 6, 1, 2, 3, 5, 7, 0)
 RELAYED = (5, 7)
 FETCH = 8
 MIB = 1024 * 1024

time: 35.2 us -> 35.8 us (1.017); the launches traced: 34.7 us -> 35.9 us
  blocking collectives: 11.2 us -> 12.4 us
  starting transfers between devices: 12.2 us -> 11.8 us
    all_to_all x1, blocking collectives: 11.2 us -> 12.4 us  [body(): lax.all_to_all(scores, 'index', split_axis=0, concat_axis=0, tiled=True)]
    ppermute x7, starting transfers between devices: 12.1 us -> 11.8 us  [body(): lax.ppermute(x, 'index', [(i, i ^ t) for i in range(peers)])]
where the time goes in v12:
time: 35.8 us; the launch traced here: 35.9 us
  blocking collectives  12.4 us (35%)
  starting transfers between devices  11.8 us (33%)
  Pallas kernels  5.55 us (16%)
  waiting for transfers between devices  4.49 us (13%)
  local copies, waits for them, and re-layouts  0.72 us (2%)
  between operations  0.71 us (2%)
    all_to_all x1, blocking collectives, body(): lax.all_to_all(scores, 'index', split_axis=0, concat_axis=0, tiled=True)  12.4 us
    ppermute x7, starting transfers between devices, body(): lax.ppermute(x, 'index', [(i, i ^ t) for i in range(peers)])  11.8 us
    pallas_call x1, Pallas kernels, body(): pl.pallas_call(functools.partial(score_kernel, slots, q_dev, per_query, q...  4.58 us
    ppermute x7, waiting for transfers between devices, body(): lax.ppermute(x, 'index', [(i, i ^ t) for i in range(peers)])  3.19 us
    ppermute x1, waiting for transfers between devices, body(): other = lax.ppermute(mine, 'query', [(0, 1), (1, 0)])  1.3 us
    pallas_call x1, Pallas kernels, body(): pl.pallas_call(pack_kernel, out_shape=[jax.ShapeDtypeStruct((copies, rows...  0.98 us
  transfers between devices with their start and end apart: 8, of which 5 were waited for; matrix products, arithmetic and copies ran while one was open for 1% of the time, Pallas kernels for 0%

profile of v12, /device:TPU:0, one launch (start us, length us, event | category | flops | bytes accessed | tf_op | source)
XLA Modules:
  0.0 35.9 jit_solution(1399803071244734398)
XLA Ops:
  0.6 1.0 %shard_map.86 = (bf16[1,272,128]{2,1,0:T(8,128)(2,1)S(1)}, s32[32,128]{1,0:T(8,128)S(1)}, s32[128]{0:T(128)S(1)}) custom-call(s32[4,8]{1,0:T(4,128)} %owner_hbm.1, s32[4,8]{1,0:T(4,128)} %local_hbm.1, bf16[4,32,128]{2,1,0:T(8,128)(2,1)} %queries_hbm.1, bf16[256,128]{1,0:T(8,128)(2,1)} %cent_hbm.1, s32[64,128]{1,0:T(8,128)} %bitcast.68, s32[128]{0:T(128)} %length_hbm.1), custom_call_target="tpu_custom_call" | custom-call | tf_op jit(solution)/shard_map/pallas_call | solution.py:259
  1.6 4.1 %collective-permute-start = (bf16[272,128]{1,0:T(8,128)(2,1)S(1)}, bf16[272,128]{1,0:T(8,128)(2,1)S(1)}, u32[]{:S(2)}, u32[]{:S(2)}) collective-permute-start(bf16[272,128]{1,0:T(8,128)(2,1)S(1)} %bitcast.60), channel_id=1, source_target_pairs={{0,8},{2,10},{4,12},{6,14},{8,0},{10,2},{12,4},{14,6},{1,9},{3,11}... | collective-permute-start | bytes 208904 | tf_op jit(solution)/shard_map/ppermute | solution.py:280
  5.7 1.3 %collective-permute-start.1 = (bf16[272,128]{1,0:T(8,128)(2,1)S(1)}, bf16[272,128]{1,0:T(8,128)(2,1)S(1)}, u32[]{:S(2)}, u32[]{:S(2)}) collective-permute-start(bf16[272,128]{1,0:T(8,128)(2,1)S(1)} %bitcast.61), channel_id=1, source_target_pairs={{0,12},{2,14},{4,8},{6,10},{8,4},{10,6},{12,0},{14,2},{1,13},{3,15... | collective-permute-start | bytes 208904 | tf_op jit(solution)/shard_map/ppermute | solution.py:280
  7.1 1.5 %collective-permute-start.2 = (bf16[272,128]{1,0:T(8,128)(2,1)S(1)}, bf16[272,128]{1,0:T(8,128)(2,1)S(1)}, u32[]{:S(2)}, u32[]{:S(2)}) collective-permute-start(bf16[272,128]{1,0:T(8,128)(2,1)S(1)} %bitcast.62), channel_id=1, source_target_pairs={{0,2},{2,0},{4,6},{6,4},{8,10},{10,8},{12,14},{14,12},{1,3},{3,1},... | collective-permute-start | bytes 208904 | tf_op jit(solution)/shard_map/ppermute | solution.py:280
  8.6 0.2 collective-permute-start.3
  8.8 1.8 %collective-permute-start.4 = (bf16[272,128]{1,0:T(8,128)(2,1)S(1)}, bf16[272,128]{1,0:T(8,128)(2,1)S(1)}, u32[]{:S(2)}, u32[]{:S(2)}) collective-permute-start(bf16[272,128]{1,0:T(8,128)(2,1)S(1)} %bitcast.64), channel_id=1, source_target_pairs={{0,6},{2,4},{4,2},{6,0},{8,14},{10,12},{12,10},{14,8},{1,7},{3,5},... | collective-permute-start | bytes 208904 | tf_op jit(solution)/shard_map/ppermute | solution.py:280
  10.6 0.0 collective-permute-done.refs_0_
  10.6 1.7 %collective-permute-start.5 = (bf16[272,128]{1,0:T(8,128)(2,1)S(1)}, bf16[272,128]{1,0:T(8,128)(2,1)S(1)}, u32[]{:S(2)}, u32[]{:S(2)}) collective-permute-start(bf16[272,128]{1,0:T(8,128)(2,1)S(1)} %collective-permute-done.refs_0_), channel_id=1, source_target_pairs={{0,2},{2,0},{4,6},{6,4},{8,10},{10,8},{12,14},{14,12},{1,3},{3,1},... | collective-permute-start | bytes 208904 | tf_op jit(solution)/shard_map/ppermute | solution.py:280
  12.3 0.1 collective-permute-done.1.refs_1_
  12.4 1.1 %collective-permute-start.6 = (bf16[272,128]{1,0:T(8,128)(2,1)S(1)}, bf16[272,128]{1,0:T(8,128)(2,1)S(1)}, u32[]{:S(2)}, u32[]{:S(2)}) collective-permute-start(bf16[272,128]{1,0:T(8,128)(2,1)S(1)} %collective-permute-done.1.refs_1_), channel_id=1, source_target_pairs={{0,2},{2,0},{4,6},{6,4},{8,10},{10,8},{12,14},{14,12},{1,3},{3,1},... | collective-permute-start | bytes 208904 | tf_op jit(solution)/shard_map/ppermute | solution.py:280
  13.5 0.0 collective-permute-done.2.refs_2_
  13.6 0.0 collective-permute-done.3.refs_3_
  13.6 1.5 %collective-permute-done.4.refs_4_ = bf16[272,128]{1,0:T(8,128)(2,1)S(1)} collective-permute-done((bf16[272,128]{1,0:T(8,128)(2,1)S(1)}, bf16[272,128]{1,0:T(8,128)(2,1)S(1)}, u32[]{:S(2)}, u32[]{:S(2)}) %collective-permute-start.4) | collective-permute-done | bytes 69664 | tf_op jit(solution)/shard_map/ppermute | solution.py:280
  15.1 0.6 %collective-permute-done.5.refs_5_ = bf16[272,128]{1,0:T(8,128)(2,1)S(1)} collective-permute-done((bf16[272,128]{1,0:T(8,128)(2,1)S(1)}, bf16[272,128]{1,0:T(8,128)(2,1)S(1)}, u32[]{:S(2)}, u32[]{:S(2)}) %collective-permute-start.5) | collective-permute-done | bytes 69664 | tf_op jit(solution)/shard_map/ppermute | solution.py:280
  15.7 1.0 %collective-permute-done.6.refs_6_ = bf16[272,128]{1,0:T(8,128)(2,1)S(1)} collective-permute-done((bf16[272,128]{1,0:T(8,128)(2,1)S(1)}, bf16[272,128]{1,0:T(8,128)(2,1)S(1)}, u32[]{:S(2)}, u32[]{:S(2)}) %collective-permute-start.6) | collective-permute-done | bytes 69664 | tf_op jit(solution)/shard_map/ppermute | solution.py:280
  16.7 0.1 collective-permute-start.7
  16.8 0.1 fusion.7
  16.9 0.1 pad_add_fusion.req_any
  17.0 1.3 %collective-permute-done.7.refs_8_ = bf16[8,128,128]{2,1,0:T(8,128)(2,1)S(1)} collective-permute-done((bf16[8,128,128]{2,1,0:T(8,128)(2,1)S(1)}, bf16[8,128,128]{2,1,0:T(8,128)(2,1)S(1)}, u32[]{:S(2)}, u32[]{:S(2)}) %collective-permute-start.7) | collective-permute-done | bytes 262176 | tf_op jit(solution)/shard_map/ppermute | solution.py:302
  18.3 4.6 %shard_map.87 = f32[8,8,128]{2,1,0:T(8,128)S(1)} custom-call(s32[8,128]{1,0:T(8,128)S(1)} %pad_add_fusion.req_any, s32[128]{0:T(128)S(1)} %get-tuple-element.6.length_any, s32[4096]{0:T(1024)S(1)} %bitcast.66, bf16[272,128]{1,0:T(8,128)(2,1)S(1)} %collective-permute-done.refs_0_, bf16[272,128]{1,0:T(8,128)(2,1)S(1)} %collective-permute-done.1.refs_1_, ...), custom_call_target="tpu_custom_call" | custom-call | tf_op jit(solution)/shard_map/pallas_call | solution.py:305
  22.9 12.4 %all_to_all.5 = f32[8,8,128]{2,1,0:T(8,128)S(1)} all-to-all(f32[8,8,128]{2,1,0:T(8,128)S(1)} %shard_map.87), channel_id=1, replica_groups=mesh['group'=2,'index'=8,'query'=2] {'index'}, dimensions={0} | all-to-all | bytes 65536 | tf_op jit(solution)/shard_map/all_to_all | solution.py:326
  35.3 0.6 %fusion.9 = (f32[4,8]{1,0:T(4,128)}, f32[4,8]{1,0:T(4,128)}) fusion(f32[8,8]{1,0:T(8,128)S(1)} %slice_reduce_fusion), kind=kLoop, calls=%fused_computation.49 | loop fusion | bytes 512 | tf_op jit(solution)/shard_map/slice | solution.py:328
  (19 shorter events, 0.2 us)
Async XLA Ops:
  1.6 8.9 %collective-permute-start = (bf16[272,128]{1,0:T(8,128)(2,1)S(1)}, bf16[272,128]{1,0:T(8,128)(2,1)S(1)}, u32[]{:S(2)}, u32[]{:S(2)}) collective-permute-start(bf16[272,128]{1,0:T(8,128)(2,1)S(1)} %bitcast.60), channel_id=1, source_target_pairs={{0,8},{2,10},{4,12},{6,14},{8,0},{10,2},{12,4},{14,6},{1,9},{3,11}... | collective-permute-start | bytes 208904 | tf_op jit(solution)/shard_map/ppermute | solution.py:280
  5.7 6.7 %collective-permute-start.1 = (bf16[272,128]{1,0:T(8,128)(2,1)S(1)}, bf16[272,128]{1,0:T(8,128)(2,1)S(1)}, u32[]{:S(2)}, u32[]{:S(2)}) collective-permute-start(bf16[272,128]{1,0:T(8,128)(2,1)S(1)} %bitcast.61), channel_id=1, source_target_pairs={{0,12},{2,14},{4,8},{6,10},{8,4},{10,6},{12,0},{14,2},{1,13},{3,15... | collective-permute-start | bytes 208904 | tf_op jit(solution)/shard_map/ppermute | solution.py:280
  7.1 6.5 %collective-permute-start.2 = (bf16[272,128]{1,0:T(8,128)(2,1)S(1)}, bf16[272,128]{1,0:T(8,128)(2,1)S(1)}, u32[]{:S(2)}, u32[]{:S(2)}) collective-permute-start(bf16[272,128]{1,0:T(8,128)(2,1)S(1)} %bitcast.62), channel_id=1, source_target_pairs={{0,2},{2,0},{4,6},{6,4},{8,10},{10,8},{12,14},{14,12},{1,3},{3,1},... | collective-permute-start | bytes 208904 | tf_op jit(solution)/shard_map/ppermute | solution.py:280
  8.6 5.0 %collective-permute-start.3 = (bf16[272,128]{1,0:T(8,128)(2,1)S(1)}, bf16[272,128]{1,0:T(8,128)(2,1)S(1)}, u32[]{:S(2)}, u32[]{:S(2)}) collective-permute-start(bf16[272,128]{1,0:T(8,128)(2,1)S(1)} %bitcast.63), channel_id=1, source_target_pairs={{0,4},{2,6},{4,0},{6,2},{8,12},{10,14},{12,8},{14,10},{1,5},{3,7},... | collective-permute-start | bytes 208904 | tf_op jit(solution)/shard_map/ppermute | solution.py:280
  8.8 6.3 %collective-permute-start.4 = (bf16[272,128]{1,0:T(8,128)(2,1)S(1)}, bf16[272,128]{1,0:T(8,128)(2,1)S(1)}, u32[]{:S(2)}, u32[]{:S(2)}) collective-permute-start(bf16[272,128]{1,0:T(8,128)(2,1)S(1)} %bitcast.64), channel_id=1, source_target_pairs={{0,6},{2,4},{4,2},{6,0},{8,14},{10,12},{12,10},{14,8},{1,7},{3,5},... | collective-permute-start | bytes 208904 | tf_op jit(solution)/shard_map/ppermute | solution.py:280
  10.6 5.1 %collective-permute-start.5 = (bf16[272,128]{1,0:T(8,128)(2,1)S(1)}, bf16[272,128]{1,0:T(8,128)(2,1)S(1)}, u32[]{:S(2)}, u32[]{:S(2)}) collective-permute-start(bf16[272,128]{1,0:T(8,128)(2,1)S(1)} %collective-permute-done.refs_0_), channel_id=1, source_target_pairs={{0,2},{2,0},{4,6},{6,4},{8,10},{10,8},{12,14},{14,12},{1,3},{3,1},... | collective-permute-start | bytes 208904 | tf_op jit(solution)/shard_map/ppermute | solution.py:280
  12.4 4.3 %collective-permute-start.6 = (bf16[272,128]{1,0:T(8,128)(2,1)S(1)}, bf16[272,128]{1,0:T(8,128)(2,1)S(1)}, u32[]{:S(2)}, u32[]{:S(2)}) collective-permute-start(bf16[272,128]{1,0:T(8,128)(2,1)S(1)} %collective-permute-done.1.refs_1_), channel_id=1, source_target_pairs={{0,2},{2,0},{4,6},{6,4},{8,10},{10,8},{12,14},{14,12},{1,3},{3,1},... | collective-permute-start | bytes 208904 | tf_op jit(solution)/shard_map/ppermute | solution.py:280
  16.7 1.6 %collective-permute-start.7 = (bf16[8,128,128]{2,1,0:T(8,128)(2,1)S(1)}, bf16[8,128,128]{2,1,0:T(8,128)(2,1)S(1)}, u32[]{:S(2)}, u32[]{:S(2)}) collective-permute-start(bf16[8,128,128]{2,1,0:T(8,128)(2,1)S(1)} %constant_dynamic-update-slice_fusion.8), channel_id=1, source_target_pairs={{0,1},{1,0},{2,3},{3,2},{4,5},{5,4},{6,7},{7,6},{8,9},{9,8},{10,11... | collective-permute-start | bytes 786440 | tf_op jit(solution)/shard_map/ppermute | solution.py:302

commit v13 on v10

--- a/solution.py
+++ b/solution.py
@@ -10,7 +10,7 @@
 EPS = 1e-06
 PAD = 16
 UNIT = 32
-GROUP = 32
+GROUP = 48
 ORDER = (4, 6, 1, 3, 2, 5, 7, 0)
 RELAYED = (5, 7)
 FETCH = 8

time: 35.2 us -> 35.6 us (1.011); the launches traced: 34.7 us -> 35.7 us
  blocking collectives: 11.2 us -> 14.2 us
  Pallas kernels: 5.56 us -> 3.56 us
    all_to_all x1, blocking collectives: 11.2 us -> 14.2 us  [body(): lax.all_to_all(scores, 'index', split_axis=0, concat_axis=0, tiled=True)]
    pallas_call x1, Pallas kernels: 4.58 us -> 2.58 us  [body(): pl.pallas_call(functools.partial(score_kernel, slots, q_dev, per_query, q...]
where the time goes in v13:
time: 35.6 us; the launch traced here: 35.7 us
  blocking collectives  14.2 us (40%)
  starting transfers between devices  12.2 us (34%)
  waiting for transfers between devices  4.15 us (12%)
  Pallas kernels  3.56 us (10%)
  local copies, waits for them, and re-layouts  0.72 us (2%)
  between operations  0.71 us (2%)
    all_to_all x1, blocking collectives, body(): lax.all_to_all(scores, 'index', split_axis=0, concat_axis=0, tiled=True)  14.2 us
    ppermute x7, starting transfers between devices, body(): lax.ppermute(x, 'index', [(i, i ^ t) for i in range(peers)])  12.1 us
    ppermute x7, waiting for transfers between devices, body(): lax.ppermute(x, 'index', [(i, i ^ t) for i in range(peers)])  2.85 us
    pallas_call x1, Pallas kernels, body(): pl.pallas_call(functools.partial(score_kernel, slots, q_dev, per_query, q...  2.58 us
    ppermute x1, waiting for transfers between devices, body(): other = lax.ppermute(mine, 'query', [(0, 1), (1, 0)])  1.3 us
    pallas_call x1, Pallas kernels, body(): pl.pallas_call(pack_kernel, out_shape=[jax.ShapeDtypeStruct((copies, rows...  0.98 us
  transfers between devices with their start and end apart: 8, of which 5 were waited for; matrix products, arithmetic and copies ran while one was open for 1% of the time, Pallas kernels for 0%

profile of v13, /device:TPU:0, one launch (start us, length us, event | category | flops | bytes accessed | tf_op | source)
XLA Modules:
  0.0 35.7 jit_solution(7966915702970459434)
XLA Ops:
  0.6 1.0 %shard_map.86 = (bf16[1,272,128]{2,1,0:T(8,128)(2,1)S(1)}, s32[32,128]{1,0:T(8,128)S(1)}, s32[128]{0:T(128)S(1)}) custom-call(s32[4,8]{1,0:T(4,128)} %owner_hbm.1, s32[4,8]{1,0:T(4,128)} %local_hbm.1, bf16[4,32,128]{2,1,0:T(8,128)(2,1)} %queries_hbm.1, bf16[256,128]{1,0:T(8,128)(2,1)} %cent_hbm.1, s32[64,128]{1,0:T(8,128)} %bitcast.68, s32[128]{0:T(128)} %length_hbm.1), custom_call_target="tpu_custom_call" | custom-call | tf_op jit(solution)/shard_map/pallas_call | solution.py:259
  1.6 4.1 %collective-permute-start = (bf16[272,128]{1,0:T(8,128)(2,1)S(1)}, bf16[272,128]{1,0:T(8,128)(2,1)S(1)}, u32[]{:S(2)}, u32[]{:S(2)}) collective-permute-start(bf16[272,128]{1,0:T(8,128)(2,1)S(1)} %bitcast.60), channel_id=1, source_target_pairs={{0,8},{2,10},{4,12},{6,14},{8,0},{10,2},{12,4},{14,6},{1,9},{3,11}... | collective-permute-start | bytes 208904 | tf_op jit(solution)/shard_map/ppermute | solution.py:280
  5.7 1.3 %collective-permute-start.1 = (bf16[272,128]{1,0:T(8,128)(2,1)S(1)}, bf16[272,128]{1,0:T(8,128)(2,1)S(1)}, u32[]{:S(2)}, u32[]{:S(2)}) collective-permute-start(bf16[272,128]{1,0:T(8,128)(2,1)S(1)} %bitcast.61), channel_id=1, source_target_pairs={{0,12},{2,14},{4,8},{6,10},{8,4},{10,6},{12,0},{14,2},{1,13},{3,15... | collective-permute-start | bytes 208904 | tf_op jit(solution)/shard_map/ppermute | solution.py:280
  7.1 1.5 %collective-permute-start.2 = (bf16[272,128]{1,0:T(8,128)(2,1)S(1)}, bf16[272,128]{1,0:T(8,128)(2,1)S(1)}, u32[]{:S(2)}, u32[]{:S(2)}) collective-permute-start(bf16[272,128]{1,0:T(8,128)(2,1)S(1)} %bitcast.62), channel_id=1, source_target_pairs={{0,2},{2,0},{4,6},{6,4},{8,10},{10,8},{12,14},{14,12},{1,3},{3,1},... | collective-permute-start | bytes 208904 | tf_op jit(solution)/shard_map/ppermute | solution.py:280
  8.6 0.2 collective-permute-start.3
  8.8 1.8 %collective-permute-start.4 = (bf16[272,128]{1,0:T(8,128)(2,1)S(1)}, bf16[272,128]{1,0:T(8,128)(2,1)S(1)}, u32[]{:S(2)}, u32[]{:S(2)}) collective-permute-start(bf16[272,128]{1,0:T(8,128)(2,1)S(1)} %bitcast.64), channel_id=1, source_target_pairs={{0,4},{2,6},{4,0},{6,2},{8,12},{10,14},{12,8},{14,10},{1,5},{3,7},... | collective-permute-start | bytes 208904 | tf_op jit(solution)/shard_map/ppermute | solution.py:280
  10.6 0.0 collective-permute-done.refs_0_
  10.6 1.7 %collective-permute-start.5 = (bf16[272,128]{1,0:T(8,128)(2,1)S(1)}, bf16[272,128]{1,0:T(8,128)(2,1)S(1)}, u32[]{:S(2)}, u32[]{:S(2)}) collective-permute-start(bf16[272,128]{1,0:T(8,128)(2,1)S(1)} %collective-permute-done.refs_0_), channel_id=1, source_target_pairs={{0,2},{2,0},{4,6},{6,4},{8,10},{10,8},{12,14},{14,12},{1,3},{3,1},... | collective-permute-start | bytes 208904 | tf_op jit(solution)/shard_map/ppermute | solution.py:280
  12.3 0.1 collective-permute-done.1.refs_1_
  12.4 1.5 %collective-permute-start.6 = (bf16[272,128]{1,0:T(8,128)(2,1)S(1)}, bf16[272,128]{1,0:T(8,128)(2,1)S(1)}, u32[]{:S(2)}, u32[]{:S(2)}) collective-permute-start(bf16[272,128]{1,0:T(8,128)(2,1)S(1)} %collective-permute-done.1.refs_1_), channel_id=1, source_target_pairs={{0,2},{2,0},{4,6},{6,4},{8,10},{10,8},{12,14},{14,12},{1,3},{3,1},... | collective-permute-start | bytes 208904 | tf_op jit(solution)/shard_map/ppermute | solution.py:280
  13.9 0.0 collective-permute-done.2.refs_2_
  13.9 0.7 %collective-permute-done.3.refs_3_ = bf16[272,128]{1,0:T(8,128)(2,1)S(1)} collective-permute-done((bf16[272,128]{1,0:T(8,128)(2,1)S(1)}, bf16[272,128]{1,0:T(8,128)(2,1)S(1)}, u32[]{:S(2)}, u32[]{:S(2)}) %collective-permute-start.3) | collective-permute-done | bytes 69664 | tf_op jit(solution)/shard_map/ppermute | solution.py:280
  14.6 0.0 collective-permute-done.4.refs_4_
  14.7 0.6 %collective-permute-done.5.refs_5_ = bf16[272,128]{1,0:T(8,128)(2,1)S(1)} collective-permute-done((bf16[272,128]{1,0:T(8,128)(2,1)S(1)}, bf16[272,128]{1,0:T(8,128)(2,1)S(1)}, u32[]{:S(2)}, u32[]{:S(2)}) %collective-permute-start.5) | collective-permute-done | bytes 69664 | tf_op jit(solution)/shard_map/ppermute | solution.py:280
  15.3 1.5 %collective-permute-done.6.refs_6_ = bf16[272,128]{1,0:T(8,128)(2,1)S(1)} collective-permute-done((bf16[272,128]{1,0:T(8,128)(2,1)S(1)}, bf16[272,128]{1,0:T(8,128)(2,1)S(1)}, u32[]{:S(2)}, u32[]{:S(2)}) %collective-permute-start.6) | collective-permute-done | bytes 69664 | tf_op jit(solution)/shard_map/ppermute | solution.py:280
  16.7 0.1 collective-permute-start.7
  16.9 0.1 fusion.7
  17.0 0.1 pad_add_fusion.req_any
  17.0 1.3 %collective-permute-done.7.refs_8_ = bf16[8,128,128]{2,1,0:T(8,128)(2,1)S(1)} collective-permute-done((bf16[8,128,128]{2,1,0:T(8,128)(2,1)S(1)}, bf16[8,128,128]{2,1,0:T(8,128)(2,1)S(1)}, u32[]{:S(2)}, u32[]{:S(2)}) %collective-permute-start.7) | collective-permute-done | bytes 262176 | tf_op jit(solution)/shard_map/ppermute | solution.py:302
  18.3 2.6 %shard_map.87 = f32[8,8,128]{2,1,0:T(8,128)S(1)} custom-call(s32[8,128]{1,0:T(8,128)S(1)} %pad_add_fusion.req_any, s32[128]{0:T(128)S(1)} %get-tuple-element.6.length_any, s32[4096]{0:T(1024)S(1)} %bitcast.66, bf16[272,128]{1,0:T(8,128)(2,1)S(1)} %collective-permute-done.refs_0_, bf16[272,128]{1,0:T(8,128)(2,1)S(1)} %collective-permute-done.1.refs_1_, ...), custom_call_target="tpu_custom_call" | custom-call | tf_op jit(solution)/shard_map/pallas_call | solution.py:305
  20.9 14.2 %all_to_all.5 = f32[8,8,128]{2,1,0:T(8,128)S(1)} all-to-all(f32[8,8,128]{2,1,0:T(8,128)S(1)} %shard_map.87), channel_id=1, replica_groups=mesh['group'=2,'index'=8,'query'=2] {'index'}, dimensions={0} | all-to-all | bytes 65536 | tf_op jit(solution)/shard_map/all_to_all | solution.py:326
  35.1 0.6 %fusion.9 = (f32[4,8]{1,0:T(4,128)}, f32[4,8]{1,0:T(4,128)}) fusion(f32[8,8]{1,0:T(8,128)S(1)} %slice_reduce_fusion), kind=kLoop, calls=%fused_computation.49 | loop fusion | bytes 512 | tf_op jit(solution)/shard_map/slice | solution.py:328
  (19 shorter events, 0.2 us)
Async XLA Ops:
  1.6 8.9 %collective-permute-start = (bf16[272,128]{1,0:T(8,128)(2,1)S(1)}, bf16[272,128]{1,0:T(8,128)(2,1)S(1)}, u32[]{:S(2)}, u32[]{:S(2)}) collective-permute-start(bf16[272,128]{1,0:T(8,128)(2,1)S(1)} %bitcast.60), channel_id=1, source_target_pairs={{0,8},{2,10},{4,12},{6,14},{8,0},{10,2},{12,4},{14,6},{1,9},{3,11}... | collective-permute-start | bytes 208904 | tf_op jit(solution)/shard_map/ppermute | solution.py:280
  5.7 6.7 %collective-permute-start.1 = (bf16[272,128]{1,0:T(8,128)(2,1)S(1)}, bf16[272,128]{1,0:T(8,128)(2,1)S(1)}, u32[]{:S(2)}, u32[]{:S(2)}) collective-permute-start(bf16[272,128]{1,0:T(8,128)(2,1)S(1)} %bitcast.61), channel_id=1, source_target_pairs={{0,12},{2,14},{4,8},{6,10},{8,4},{10,6},{12,0},{14,2},{1,13},{3,15... | collective-permute-start | bytes 208904 | tf_op jit(solution)/shard_map/ppermute | solution.py:280
  7.1 6.9 %collective-permute-start.2 = (bf16[272,128]{1,0:T(8,128)(2,1)S(1)}, bf16[272,128]{1,0:T(8,128)(2,1)S(1)}, u32[]{:S(2)}, u32[]{:S(2)}) collective-permute-start(bf16[272,128]{1,0:T(8,128)(2,1)S(1)} %bitcast.62), channel_id=1, source_target_pairs={{0,2},{2,0},{4,6},{6,4},{8,10},{10,8},{12,14},{14,12},{1,3},{3,1},... | collective-permute-start | bytes 208904 | tf_op jit(solution)/shard_map/ppermute | solution.py:280
  8.6 6.1 %collective-permute-start.3 = (bf16[272,128]{1,0:T(8,128)(2,1)S(1)}, bf16[272,128]{1,0:T(8,128)(2,1)S(1)}, u32[]{:S(2)}, u32[]{:S(2)}) collective-permute-start(bf16[272,128]{1,0:T(8,128)(2,1)S(1)} %bitcast.63), channel_id=1, source_target_pairs={{0,6},{2,4},{4,2},{6,0},{8,14},{10,12},{12,10},{14,8},{1,7},{3,5},... | collective-permute-start | bytes 208904 | tf_op jit(solution)/shard_map/ppermute | solution.py:280
  8.8 5.9 %collective-permute-start.4 = (bf16[272,128]{1,0:T(8,128)(2,1)S(1)}, bf16[272,128]{1,0:T(8,128)(2,1)S(1)}, u32[]{:S(2)}, u32[]{:S(2)}) collective-permute-start(bf16[272,128]{1,0:T(8,128)(2,1)S(1)} %bitcast.64), channel_id=1, source_target_pairs={{0,4},{2,6},{4,0},{6,2},{8,12},{10,14},{12,8},{14,10},{1,5},{3,7},... | collective-permute-start | bytes 208904 | tf_op jit(solution)/shard_map/ppermute | solution.py:280
  10.6 4.7 %collective-permute-start.5 = (bf16[272,128]{1,0:T(8,128)(2,1)S(1)}, bf16[272,128]{1,0:T(8,128)(2,1)S(1)}, u32[]{:S(2)}, u32[]{:S(2)}) collective-permute-start(bf16[272,128]{1,0:T(8,128)(2,1)S(1)} %collective-permute-done.refs_0_), channel_id=1, source_target_pairs={{0,2},{2,0},{4,6},{6,4},{8,10},{10,8},{12,14},{14,12},{1,3},{3,1},... | collective-permute-start | bytes 208904 | tf_op jit(solution)/shard_map/ppermute | solution.py:280
  12.4 4.3 %collective-permute-start.6 = (bf16[272,128]{1,0:T(8,128)(2,1)S(1)}, bf16[272,128]{1,0:T(8,128)(2,1)S(1)}, u32[]{:S(2)}, u32[]{:S(2)}) collective-permute-start(bf16[272,128]{1,0:T(8,128)(2,1)S(1)} %collective-permute-done.1.refs_1_), channel_id=1, source_target_pairs={{0,2},{2,0},{4,6},{6,4},{8,10},{10,8},{12,14},{14,12},{1,3},{3,1},... | collective-permute-start | bytes 208904 | tf_op jit(solution)/shard_map/ppermute | solution.py:280
  16.7 1.6 %collective-permute-start.7 = (bf16[8,128,128]{2,1,0:T(8,128)(2,1)S(1)}, bf16[8,128,128]{2,1,0:T(8,128)(2,1)S(1)}, u32[]{:S(2)}, u32[]{:S(2)}) collective-permute-start(bf16[8,128,128]{2,1,0:T(8,128)(2,1)S(1)} %constant_dynamic-update-slice_fusion.8), channel_id=1, source_target_pairs={{0,1},{1,0},{2,3},{3,2},{4,5},{5,4},{6,7},{7,6},{8,9},{9,8},{10,11... | collective-permute-start | bytes 786440 | tf_op jit(solution)/shard_map/ppermute | solution.py:302
